TPU v7x, 32 devices: a whole 2x2x4 slice. The times are simulated.
32 devices in a mesh: wide: 16 (over z, x, core), blk: 2 (over y).
Axes of the slice: x: 2, y: 2, z: 4, core: 2. Of those that a mesh axis runs over, the one named last changes fastest.
Arguments:
- tokens: bfloat16 [32768, 768], P(('wide', 'blk')), may hold values from -6 to 6
- lengths: int32 [16, 6], P('wide'), may hold values from 1 to 1536, as said below
- ln1_gain: float32 [768], replicated, may hold values from 0.5 to 1.5
- ln1_bias: float32 [768], replicated, may hold values from -3 to 3
- w_qkv: bfloat16 [768, 2304], replicated, may hold values from -0.21875 to 0.21875
- q_gain: float32 [768], replicated, may hold values from 0.5 to 1.5
- k_gain: float32 [768], replicated, may hold values from 0.5 to 1.5
- w_out: bfloat16 [768, 768], replicated, may hold values from -6 to 6
- ln2_gain: float32 [768], replicated, may hold values from 0.5 to 1.5
- ln2_bias: float32 [768], replicated, may hold values from -3 to 3
- w_up: bfloat16 [768, 3072], replicated, may hold values from -0.21875 to 0.21875
- w_down: bfloat16 [3072, 768], replicated, may hold values from -0.109375 to 0.109375
- cotangent: bfloat16 [32768, 768], P(('wide', 'blk')), may hold values from -6 to 6
Outputs:
- output: bfloat16 [32768, 768], P(('wide', 'blk'))
- grad_tokens: bfloat16 [32768, 768], P(('wide', 'blk'))
- grad_ln1_gain: float32 [768], P(('wide', 'blk'))
- grad_ln1_bias: float32 [768], P(('wide', 'blk'))
- grad_w_qkv: float32 [768, 2304], P(('wide', 'blk'))
- grad_q_gain: float32 [768], P(('wide', 'blk'))
- grad_k_gain: float32 [768], P(('wide', 'blk'))
- grad_w_out: float32 [768, 768], P(('wide', 'blk'))
- grad_ln2_gain: float32 [768], P(('wide', 'blk'))
- grad_ln2_bias: float32 [768], P(('wide', 'blk'))
- grad_w_up: float32 [768, 3072], P(('wide', 'blk'))
- grad_w_down: float32 [3072, 768], P(('wide', 'blk'))
Inputs may be any that keep to these rules, and one draw needn't show every extreme that they name: Each row of lengths sums to 2048. The second image of every group begins within its first 1024 patches and ends within its last 1024.
All inputs are finite; a program needn't handle non-finite values.
Results may differ from a plain program's by a relative error of at most 0.02.
Values may be sent and summed in bfloat16 or wider, within the bound.
A program may use at most 320 MiB of HBM per device.

v0:
```python
import math

import jax
import jax.numpy as jnp
from jax import lax
from jax.sharding import PartitionSpec as P

H = 12
HD = 64


EPS = 1e-06
MASKED = -1e30
HIGH = lax.Precision.HIGHEST


def layer_norm(value, gain, shift):
    mean = jnp.mean(value, axis=-1, keepdims=True)
    centred = value - mean
    spread = jnp.mean(centred * centred, axis=-1, keepdims=True)
    return centred * lax.rsqrt(spread + EPS) * gain + shift


def head_norm(value, gain):
    mean = jnp.mean(value, axis=-1, keepdims=True)
    centred = value - mean
    spread = jnp.mean(centred * centred, axis=-1, keepdims=True)
    return centred * lax.rsqrt(spread + EPS) * gain.reshape(value.shape[1], value.shape[2])


def segment_ids(lengths_row, count):
    ends = jnp.cumsum(lengths_row)
    places = jnp.arange(count, dtype=jnp.int32)
    return jnp.sum((places[:, None] >= ends[None, :]).astype(jnp.int32), axis=1)


def transpose_times(left, right):
    return lax.dot_general(
        left, right, (((0,), (0,)), ((), ())), preferred_element_type=jnp.float32
    )


def times_transpose(left, right):
    return lax.dot_general(
        left, right, (((1,), (1,)), ((), ())), preferred_element_type=jnp.float32
    )


def split_blocks(piece):
    count = piece.shape[0]
    size = math.gcd(count, 512)
    return piece.reshape((count // size, size) + piece.shape[1:])


def block_grads(q_blk, do_blk, top_blk, total_blk, delta_blk, seg_q, k_blk, v_blk, seg_k):
    scale = 1.0 / math.sqrt(HD)
    raw = jnp.einsum("qhd,khd->hqk", q_blk, k_blk, preferred_element_type=jnp.float32) * scale
    same = seg_q[:, None] == seg_k[None, :]
    masked = jnp.where(same[None], raw, MASKED)
    weights = jnp.exp(masked - top_blk[..., None])
    prob = weights / total_blk[..., None]
    d_prob = jnp.einsum("qhd,khd->hqk", do_blk, v_blk, preferred_element_type=jnp.float32)
    d_score = (prob * (d_prob - delta_blk[..., None])).astype(jnp.bfloat16)
    d_q = None
    d_key = None
    d_value = None
    d_q = jnp.einsum("hqk,khd->hqd", d_score, k_blk, preferred_element_type=jnp.float32) * scale
    d_key = jnp.einsum("hqk,qhd->khd", d_score, q_blk, preferred_element_type=jnp.float32) * scale
    scaled_do = do_blk.astype(jnp.float32) / jnp.transpose(total_blk)[..., None]
    d_value = jnp.einsum(
        "hqk,qhd->khd",
        weights.astype(jnp.bfloat16).astype(jnp.float32),
        scaled_do,
        precision=HIGH,
        preferred_element_type=jnp.float32,
    )
    return (d_q, d_key, d_value)


def shards(
    tokens,
    lengths,
    ln1_gain,
    ln1_bias,
    w_qkv,
    q_gain,
    k_gain,
    w_out,
    ln2_gain,
    ln2_bias,
    w_up,
    w_down,
    cotangent,
):
    rows, width = tokens.shape
    group = rows * lax.axis_size("blk")
    first = lax.axis_index("blk") * rows
    scale = 1.0 / math.sqrt(HD)
    seg_all = segment_ids(lengths[0], group)
    seg_own = lax.dynamic_slice_in_dim(seg_all, first, rows)
    x = tokens.astype(jnp.float32)
    normed, ln1_back = jax.vjp(layer_norm, x, ln1_gain, ln1_bias)
    h_low = normed.astype(jnp.bfloat16)
    qkv = jnp.dot(h_low, w_qkv, preferred_element_type=jnp.float32)
    q_norm, q_back = jax.vjp(head_norm, qkv[:, :width].reshape(rows, H, HD), q_gain)
    k_norm, k_back = jax.vjp(head_norm, qkv[:, width : 2 * width].reshape(rows, H, HD), k_gain)
    q_low = q_norm.astype(jnp.bfloat16)
    k_send = k_norm.astype(jnp.bfloat16).reshape(rows, width)
    v_send = qkv[:, 2 * width :].astype(jnp.bfloat16)

    def scores(k_blk, seg_k):
        raw = jnp.einsum("qhd,khd->hqk", q_low, k_blk, preferred_element_type=jnp.float32) * scale
        same = seg_own[:, None] == seg_k[None, :]
        return jnp.where(same[None], raw, MASKED)

    def piece_blocks(pieces):
        count = pieces[0].shape[0]
        k_blocks = split_blocks(pieces[0].reshape(count, H, HD))
        v_blocks = split_blocks(pieces[1].reshape(count, H, HD))
        return (k_blocks, v_blocks, seg_all.reshape(k_blocks.shape[0], k_blocks.shape[1]))

    init_forward = (
        jnp.full((H, rows), MASKED, jnp.float32),
        jnp.zeros((H, rows), jnp.float32),
        jnp.zeros((H, rows, HD), jnp.float32),
    )

    def step(state, block):
        top, total, acc = state
        s = scores(block[0], block[2])
        new_top = jnp.maximum(top, jnp.max(s, axis=-1))
        fade = jnp.exp(top - new_top)
        weights = jnp.exp(s - new_top[..., None])
        total = total * fade + jnp.sum(weights, axis=-1)
        acc = acc * fade[..., None] + jnp.einsum(
            "hqk,khd->hqd",
            weights.astype(jnp.bfloat16),
            block[1],
            preferred_element_type=jnp.float32,
        )
        return ((new_top, total, acc), None)

    state, _ = lax.scan(
        step,
        init_forward,
        piece_blocks(
            (
                lax.all_gather(k_send, "blk", axis=0, tiled=True),
                lax.all_gather(v_send, "blk", axis=0, tiled=True),
            )
        ),
    )
    top, total, acc = state
    attn = jnp.transpose(acc / total[..., None], (1, 0, 2))
    attn_low = attn.reshape(rows, width).astype(jnp.bfloat16)
    x1 = x + jnp.dot(attn_low, w_out, preferred_element_type=jnp.float32)
    normed_two, ln2_back = jax.vjp(layer_norm, x1, ln2_gain, ln2_bias)
    h2_low = normed_two.astype(jnp.bfloat16)
    up = jnp.dot(h2_low, w_up, preferred_element_type=jnp.float32)
    act, gelu_back = jax.vjp(jax.nn.gelu, up)
    act_low = act.astype(jnp.bfloat16)
    output = (x1 + jnp.dot(act_low, w_down, preferred_element_type=jnp.float32)).astype(
        jnp.bfloat16
    )
    grad_w_down = transpose_times(act_low, cotangent)
    d_act = times_transpose(cotangent, w_down)
    d_up = gelu_back(d_act)[0].astype(jnp.bfloat16)
    grad_w_up = transpose_times(h2_low, d_up)
    d_h2 = times_transpose(d_up, w_up)
    d_x1_norm, grad_ln2_gain, grad_ln2_bias = ln2_back(d_h2)
    d_x1 = cotangent.astype(jnp.float32) + d_x1_norm
    d_branch = d_x1.astype(jnp.bfloat16)
    grad_w_out = transpose_times(attn_low, d_branch)
    d_attn = times_transpose(d_branch, w_out).astype(jnp.bfloat16).reshape(rows, H, HD)
    delta = jnp.transpose(jnp.sum(d_attn.astype(jnp.float32) * attn, axis=-1))
    pieces = (
        lax.all_gather(k_send, "blk", axis=0, tiled=True),
        lax.all_gather(v_send, "blk", axis=0, tiled=True),
    )
    d_query = jnp.zeros((H, rows, HD), jnp.float32)
    count = pieces[0].shape[0]

    def step(d_q, block):
        part_q, d_key, d_value = block_grads(
            q_low, d_attn, top, total, delta, seg_own, block[0], block[1], block[2]
        )
        size = d_key.shape[0]
        return (
            d_q + part_q,
            jnp.concatenate([d_key.reshape(size, width), d_value.reshape(size, width)], axis=1),
        )

    d_query, d_blocks = lax.scan(step, d_query, piece_blocks(pieces))
    d_pairs = d_blocks.reshape(count, 2 * width)
    d_query, d_pairs = (d_query, d_pairs)
    d_own = lax.psum_scatter(
        d_pairs.astype(jnp.bfloat16), "blk", scatter_dimension=0, tiled=True
    ).astype(jnp.float32)
    d_q_raw, grad_q_gain = q_back(jnp.transpose(d_query, (1, 0, 2)))
    d_k_raw, grad_k_gain = k_back(d_own[:, :width].reshape(rows, H, HD))
    d_qkv = jnp.concatenate(
        [d_q_raw.reshape(rows, width), d_k_raw.reshape(rows, width), d_own[:, width:]], axis=1
    ).astype(jnp.bfloat16)
    grad_w_qkv = transpose_times(h_low, d_qkv)
    d_h = times_transpose(d_qkv, w_qkv)
    d_x_norm, grad_ln1_gain, grad_ln1_bias = ln1_back(d_h)
    grad_tokens = (d_x1 + d_x_norm).astype(jnp.bfloat16)
    (
        sum_w_out,
        sum_w_up,
        sum_w_down,
        sum_ln2_gain,
        sum_ln2_bias,
        sum_w_qkv,
        sum_ln1_gain,
        sum_ln1_bias,
        sum_q_gain,
        sum_k_gain,
    ) = (
        lax.psum_scatter(grad_w_out, ("wide", "blk"), scatter_dimension=0, tiled=True),
        lax.psum_scatter(grad_w_up, ("wide", "blk"), scatter_dimension=0, tiled=True),
        lax.psum_scatter(grad_w_down, ("wide", "blk"), scatter_dimension=0, tiled=True),
        lax.psum_scatter(grad_ln2_gain, ("wide", "blk"), scatter_dimension=0, tiled=True),
        lax.psum_scatter(grad_ln2_bias, ("wide", "blk"), scatter_dimension=0, tiled=True),
        lax.psum_scatter(grad_w_qkv, ("wide", "blk"), scatter_dimension=0, tiled=True),
        lax.psum_scatter(grad_ln1_gain, ("wide", "blk"), scatter_dimension=0, tiled=True),
        lax.psum_scatter(grad_ln1_bias, ("wide", "blk"), scatter_dimension=0, tiled=True),
        lax.psum_scatter(grad_q_gain, ("wide", "blk"), scatter_dimension=0, tiled=True),
        lax.psum_scatter(grad_k_gain, ("wide", "blk"), scatter_dimension=0, tiled=True),
    )
    return (
        output,
        grad_tokens,
        sum_ln1_gain,
        sum_ln1_bias,
        sum_w_qkv,
        sum_q_gain,
        sum_k_gain,
        sum_w_out,
        sum_ln2_gain,
        sum_ln2_bias,
        sum_w_up,
        sum_w_down,
    )


def solution(mesh):
    in_specs = (
        P(("wide", "blk"), None),
        P("wide", None),
        P(),
        P(),
        P(),
        P(),
        P(),
        P(),
        P(),
        P(),
        P(),
        P(),
        P(("wide", "blk"), None),
    )
    out_specs = (
        P(("wide", "blk"), None),
        P(("wide", "blk"), None),
        P(("wide", "blk")),
        P(("wide", "blk")),
        P(("wide", "blk"), None),
        P(("wide", "blk")),
        P(("wide", "blk")),
        P(("wide", "blk"), None),
        P(("wide", "blk")),
        P(("wide", "blk")),
        P(("wide", "blk"), None),
        P(("wide", "blk"), None),
    )
    return jax.shard_map(shards, mesh=mesh, in_specs=in_specs, out_specs=out_specs, check_vma=False)
```

profile of v0, /device:TPU:0, one launch (start us, length us, event | category | flops | bytes accessed | tf_op | source)
XLA Modules:
  0.0 1232.1 jit_solution(16951241228476677009)
XLA Ops:
  90.6 27.7 %all-gather.3.cloned.1.call-done = bf16[2048,768]{1,0:T(8,128)(2,1)} async-done(((bf16[1024,768]{1,0:T(8,128)(2,1)}), bf16[2048,768]{1,0:T(8,128)(2,1)}) %all-gather.3.cloned.1.call-update) | async-done | bytes 3145744 | tf_op jit(solution)/shard_map/all_gather | solution.py:148
  133.6 159.9 %while.28 = (s32[]{:T(128)}, f32[12,1024]{1,0:T(8,128)}, f32[12,1024]{1,0:T(8,128)}, f32[12,1024,64]{1,2,0:T(8,128)}, s32[1024]{0:T(1024)S(1)}, /*index=5*/s32[4...) while((s32[]{:T(128)}, f32[12,1024]{1,0:T(8,128)}, ...), condition=%wide.region_11.12_spmd.clone, body=%wide.region_8.11_spmd.clone.sunk | while | flops 1682763776 | bytes 113584392 | solution.py:143
  134.7 13.9 %fusion.135 = (f32[12,1024]{1,0:T(8,128)S(1)}, f32[12,512,1024]{2,1,0:T(8,128)}) fusion(pred[1024,512]{0,1:T(8,128)(4,1)S(1)} %broadcast_compare_fusion.4, bf16[1024,12,64]{0,2,1:T(8,128)(2,1)} %get-tuple-element.567, bf16[4,512,12,64]{1,3,2,0:T(8,128)(2,1)} %get-tuple-element.566, s32[]{:T(128)S(6)} %copy.146), kind=kOutput, calls=%fused_computation.4.clone.1 | convolution fusion | flops 824168448 | bytes 28098564 | tf_op jit(solution)/shard_map/while/body/eval_jaxpr/qhd,khd->hqk/dot_general | solution.py:112
  148.6 11.3 fusion.136
  160.0 11.8 fusion.138
  174.6 13.9 %fusion.135 = (f32[12,1024]{1,0:T(8,128)S(1)}, f32[12,512,1024]{2,1,0:T(8,128)}) fusion(pred[1024,512]{0,1:T(8,128)(4,1)S(1)} %broadcast_compare_fusion.4, bf16[1024,12,64]{0,2,1:T(8,128)(2,1)} %get-tuple-element.567, bf16[4,512,12,64]{1,3,2,0:T(8,128)(2,1)} %get-tuple-element.566, s32[]{:T(128)S(6)} %copy.146), kind=kOutput, calls=%fused_computation.4.clone.1 | convolution fusion | flops 824168448 | bytes 28098564 | tf_op jit(solution)/shard_map/while/body/eval_jaxpr/qhd,khd->hqk/dot_general | solution.py:112
  188.5 11.3 fusion.136
  199.9 11.8 fusion.138
  214.5 13.9 %fusion.135 = (f32[12,1024]{1,0:T(8,128)S(1)}, f32[12,512,1024]{2,1,0:T(8,128)}) fusion(pred[1024,512]{0,1:T(8,128)(4,1)S(1)} %broadcast_compare_fusion.4, bf16[1024,12,64]{0,2,1:T(8,128)(2,1)} %get-tuple-element.567, bf16[4,512,12,64]{1,3,2,0:T(8,128)(2,1)} %get-tuple-element.566, s32[]{:T(128)S(6)} %copy.146), kind=kOutput, calls=%fused_computation.4.clone.1 | convolution fusion | flops 824168448 | bytes 28098564 | tf_op jit(solution)/shard_map/while/body/eval_jaxpr/qhd,khd->hqk/dot_general | solution.py:112
  228.4 11.3 fusion.136
  239.8 11.8 fusion.138
  254.3 13.9 %fusion.135 = (f32[12,1024]{1,0:T(8,128)S(1)}, f32[12,512,1024]{2,1,0:T(8,128)}) fusion(pred[1024,512]{0,1:T(8,128)(4,1)S(1)} %broadcast_compare_fusion.4, bf16[1024,12,64]{0,2,1:T(8,128)(2,1)} %get-tuple-element.567, bf16[4,512,12,64]{1,3,2,0:T(8,128)(2,1)} %get-tuple-element.566, s32[]{:T(128)S(6)} %copy.146), kind=kOutput, calls=%fused_computation.4.clone.1 | convolution fusion | flops 824168448 | bytes 28098564 | tf_op jit(solution)/shard_map/while/body/eval_jaxpr/qhd,khd->hqk/dot_general | solution.py:112
  268.3 11.3 fusion.136
  279.6 11.8 fusion.138
  305.1 16.9 %fusion.48 = bf16[1024,3072]{1,0:T(8,128)(2,1)} fusion(f32[1024,3072]{1,0:T(8,128)S(1)} %fusion.81, bf16[1024,768]{1,0:T(8,128)(2,1)S(1)} %copy-done.35, bf16[3072,768]{1,0:T(8,128)(2,1)} %param.28), kind=kOutput, calls=%fused_computation.61 | convolution fusion | flops 4894752768 | bytes 25165824 | tf_op jit(solution)/shard_map/dot_general | solution.py:44
  322.0 10.4 fusion.87
  347.7 278.3 %while.29 = (s32[]{:T(128)}, f32[12,1024,64]{1,2,0:T(8,128)}, bf16[4,512,1536]{1,2,0:T(8,128)(2,1)}, s32[1024]{0:T(1024)S(1)}, s32[4,512]{1,0:T(4,128)}, /*index...) while((s32[]{:T(128)}, f32[12,1024,64]{1,2,0:T(8,128)}, ...), condition=%wide.region_18.19_spmd.clone, body=%wide.region_17.18_spmd.clone.sunk | while | flops 8130658304 | bytes 149858656 | solution.py:193
  349.2 13.6 %fusion.149 = f32[12,512,1024]{2,1,0:T(8,128)} fusion(bf16[1024,12,64]{0,2,1:T(8,128)(2,1)} %get-tuple-element.605, bf16[4,512,12,64]{1,3,2,0:T(8,128)(2,1)} %get-tuple-element.604, s32[]{:T(128)S(6)} %copy.157), kind=kOutput, calls=%fused_computation.42.clone.1 | convolution fusion | flops 805306368 | bytes 27525124 | tf_op jit(solution)/shard_map/while/body/eval_jaxpr/qhd,khd->hqk/dot_general | solution.py:57
  362.9 17.9 %fusion.151 = bf16[12,64,512]{2,1,0:T(8,128)(2,1)} fusion(f32[12,512,1024]{2,1,0:T(8,128)} %fusion.149, f32[12,1024]{1,0:T(8,128)S(1)} %copy-done.25, pred[1024,512]{0,1:T(8,128)(4,1)S(1)} %broadcast_compare_fusion.5, bf16[1024,12,64]{0,2,1:T(8,128)(2,1)S(1)} %copy-done.40, f32[1024,12]{0,1:T(8,128)S(1)} %bitcast.181), kind=kOutput, calls=%fused_computation.30.clone.1 | convolution fusion | flops 4858576896 | bytes 28147712 | tf_op jit(solution)/shard_map/while/body/eval_jaxpr/hqk,qhd->khd/dot_general | solution.py:70
  380.8 16.1 %fusion.150 = bf16[12,1024,512]{1,2,0:T(8,128)(2,1)} fusion(f32[12,512,1024]{2,1,0:T(8,128)} %fusion.149, f32[12,1024]{1,0:T(8,128)} %get-tuple-element.610, f32[12,1024]{1,0:T(8,128)} %get-tuple-element.607, f32[12,1024]{1,0:T(8,128)} %get-tuple-element.606, pred[1024,512]{0,1:T(8,128)(4,1)} %copy-done.19, ...), kind=kOutput, calls=%fused_computation.25.clone.1 | convolution fusion | flops 849346560 | bytes 40828932 | tf_op jit(solution)/shard_map/while/body/eval_jaxpr/qhd,khd->hqk/dot_general | solution.py:62
  396.9 9.8 convolution_multiply_fusion.2
  406.7 8.9 select_add_fusion.2
  418.0 13.6 %fusion.149 = f32[12,512,1024]{2,1,0:T(8,128)} fusion(bf16[1024,12,64]{0,2,1:T(8,128)(2,1)} %get-tuple-element.605, bf16[4,512,12,64]{1,3,2,0:T(8,128)(2,1)} %get-tuple-element.604, s32[]{:T(128)S(6)} %copy.157), kind=kOutput, calls=%fused_computation.42.clone.1 | convolution fusion | flops 805306368 | bytes 27525124 | tf_op jit(solution)/shard_map/while/body/eval_jaxpr/qhd,khd->hqk/dot_general | solution.py:57
  431.6 17.9 %fusion.151 = bf16[12,64,512]{2,1,0:T(8,128)(2,1)} fusion(f32[12,512,1024]{2,1,0:T(8,128)} %fusion.149, f32[12,1024]{1,0:T(8,128)S(1)} %copy-done.25, pred[1024,512]{0,1:T(8,128)(4,1)S(1)} %broadcast_compare_fusion.5, bf16[1024,12,64]{0,2,1:T(8,128)(2,1)S(1)} %copy-done.40, f32[1024,12]{0,1:T(8,128)S(1)} %bitcast.181), kind=kOutput, calls=%fused_computation.30.clone.1 | convolution fusion | flops 4858576896 | bytes 28147712 | tf_op jit(solution)/shard_map/while/body/eval_jaxpr/hqk,qhd->khd/dot_general | solution.py:70
  449.6 16.1 %fusion.150 = bf16[12,1024,512]{1,2,0:T(8,128)(2,1)} fusion(f32[12,512,1024]{2,1,0:T(8,128)} %fusion.149, f32[12,1024]{1,0:T(8,128)} %get-tuple-element.610, f32[12,1024]{1,0:T(8,128)} %get-tuple-element.607, f32[12,1024]{1,0:T(8,128)} %get-tuple-element.606, pred[1024,512]{0,1:T(8,128)(4,1)} %copy-done.19, ...), kind=kOutput, calls=%fused_computation.25.clone.1 | convolution fusion | flops 849346560 | bytes 40828932 | tf_op jit(solution)/shard_map/while/body/eval_jaxpr/qhd,khd->hqk/dot_general | solution.py:62
  465.7 9.8 convolution_multiply_fusion.2
  475.5 9.8 select_add_fusion.2
  487.7 13.6 %fusion.149 = f32[12,512,1024]{2,1,0:T(8,128)} fusion(bf16[1024,12,64]{0,2,1:T(8,128)(2,1)} %get-tuple-element.605, bf16[4,512,12,64]{1,3,2,0:T(8,128)(2,1)} %get-tuple-element.604, s32[]{:T(128)S(6)} %copy.157), kind=kOutput, calls=%fused_computation.42.clone.1 | convolution fusion | flops 805306368 | bytes 27525124 | tf_op jit(solution)/shard_map/while/body/eval_jaxpr/qhd,khd->hqk/dot_general | solution.py:57
  501.3 17.9 %fusion.151 = bf16[12,64,512]{2,1,0:T(8,128)(2,1)} fusion(f32[12,512,1024]{2,1,0:T(8,128)} %fusion.149, f32[12,1024]{1,0:T(8,128)S(1)} %copy-done.25, pred[1024,512]{0,1:T(8,128)(4,1)S(1)} %broadcast_compare_fusion.5, bf16[1024,12,64]{0,2,1:T(8,128)(2,1)S(1)} %copy-done.40, f32[1024,12]{0,1:T(8,128)S(1)} %bitcast.181), kind=kOutput, calls=%fused_computation.30.clone.1 | convolution fusion | flops 4858576896 | bytes 28147712 | tf_op jit(solution)/shard_map/while/body/eval_jaxpr/hqk,qhd->khd/dot_general | solution.py:70
  519.2 16.1 %fusion.150 = bf16[12,1024,512]{1,2,0:T(8,128)(2,1)} fusion(f32[12,512,1024]{2,1,0:T(8,128)} %fusion.149, f32[12,1024]{1,0:T(8,128)} %get-tuple-element.610, f32[12,1024]{1,0:T(8,128)} %get-tuple-element.607, f32[12,1024]{1,0:T(8,128)} %get-tuple-element.606, pred[1024,512]{0,1:T(8,128)(4,1)} %copy-done.19, ...), kind=kOutput, calls=%fused_computation.25.clone.1 | convolution fusion | flops 849346560 | bytes 40828932 | tf_op jit(solution)/shard_map/while/body/eval_jaxpr/qhd,khd->hqk/dot_general | solution.py:62
  535.4 9.8 convolution_multiply_fusion.2
  545.2 9.8 select_add_fusion.2
  557.3 13.6 %fusion.149 = f32[12,512,1024]{2,1,0:T(8,128)} fusion(bf16[1024,12,64]{0,2,1:T(8,128)(2,1)} %get-tuple-element.605, bf16[4,512,12,64]{1,3,2,0:T(8,128)(2,1)} %get-tuple-element.604, s32[]{:T(128)S(6)} %copy.157), kind=kOutput, calls=%fused_computation.42.clone.1 | convolution fusion | flops 805306368 | bytes 27525124 | tf_op jit(solution)/shard_map/while/body/eval_jaxpr/qhd,khd->hqk/dot_general | solution.py:57
  571.0 17.9 %fusion.151 = bf16[12,64,512]{2,1,0:T(8,128)(2,1)} fusion(f32[12,512,1024]{2,1,0:T(8,128)} %fusion.149, f32[12,1024]{1,0:T(8,128)S(1)} %copy-done.25, pred[1024,512]{0,1:T(8,128)(4,1)S(1)} %broadcast_compare_fusion.5, bf16[1024,12,64]{0,2,1:T(8,128)(2,1)S(1)} %copy-done.40, f32[1024,12]{0,1:T(8,128)S(1)} %bitcast.181), kind=kOutput, calls=%fused_computation.30.clone.1 | convolution fusion | flops 4858576896 | bytes 28147712 | tf_op jit(solution)/shard_map/while/body/eval_jaxpr/hqk,qhd->khd/dot_general | solution.py:70
  588.9 16.1 %fusion.150 = bf16[12,1024,512]{1,2,0:T(8,128)(2,1)} fusion(f32[12,512,1024]{2,1,0:T(8,128)} %fusion.149, f32[12,1024]{1,0:T(8,128)} %get-tuple-element.610, f32[12,1024]{1,0:T(8,128)} %get-tuple-element.607, f32[12,1024]{1,0:T(8,128)} %get-tuple-element.606, pred[1024,512]{0,1:T(8,128)(4,1)} %copy-done.19, ...), kind=kOutput, calls=%fused_computation.25.clone.1 | convolution fusion | flops 849346560 | bytes 40828932 | tf_op jit(solution)/shard_map/while/body/eval_jaxpr/qhd,khd->hqk/dot_general | solution.py:62
  605.0 9.8 convolution_multiply_fusion.2
  614.9 9.8 select_add_fusion.2
  626.0 8.7 copy.125
  639.7 13.9 %fusion.82 = f32[3072,768]{1,0:T(8,128)} fusion(bf16[1024,768]{1,0:T(8,128)(2,1)} %param.29, f32[1024,3072]{1,0:T(8,128)} %copy-done.20), kind=kOutput, calls=%fused_computation.145 | convolution fusion | flops 4860149760 | bytes 23592960 | tf_op jit(solution)/shard_map/dot_general | solution.py:38
  654.3 10.7 fusion.80
  677.5 34.5 %reduce-scatter.6.cloned.1.call-done = bf16[1024,1536]{1,0:T(8,128)(2,1)} async-done(((bf16[2048,1536]{1,0:T(8,128)(2,1)}), bf16[1024,1536]{1,0:T(8,128)(2,1)}) %reduce-scatter.6.cloned.1.call-update) | async-done | bytes 3145744 | tf_op jit(solution)/shard_map/reduce_scatter | solution.py:196
  738.0 7.6 multiply_reduce_fusion.1
  753.8 11.8 add_convert_fusion.2
  770.0 8.5 fusion.86
  787.8 40.1 %all-reduce.6 = (f32[768]{0:T(1024)}, f32[768]{0:T(1024)}, f32[768]{0:T(1024)}, f32[768]{0:T(1024)}, f32[768]{0:T(1024)}, /*index=5*/f32[768]{0:T(1024)}) all-reduce(f32[768]{0:T(1024)} %get-tuple-element.334, f32[768]{0:T(1024)} %get-tuple-element.398, f32[768]{0:T(1024)} %reshape.293, ...), channel_id=3, replica_groups=mesh['wide'=16,'blk'=2] {'wide','blk'}, use_global_device_ids=true, to_apply=%region_27.28.clone | all-reduce | flops 4608 | bytes 36864
  845.4 113.2 %reduce-scatter.14.cloned.1.call-done = f32[96,768]{1,0:T(8,128)} async-done(((f32[3072,768]{1,0:T(8,128)}), f32[96,768]{1,0:T(8,128)}) %reduce-scatter.14.cloned.1.call-update) | async-done | bytes 294928 | tf_op jit(solution)/shard_map/reduce_scatter | solution.py:222
  958.6 141.9 %reduce-scatter.12.cloned.1.call-done = f32[24,3072]{1,0:T(8,128)} async-done(((f32[768,3072]{1,0:T(8,128)}), f32[24,3072]{1,0:T(8,128)}) %reduce-scatter.12.cloned.1.call-update) | async-done | bytes 294928 | tf_op jit(solution)/shard_map/reduce_scatter | solution.py:221
  1100.5 124.4 %reduce-scatter.8.cloned.1.call-done = f32[24,2304]{1,0:T(8,128)} async-done(((f32[768,2304]{1,0:T(8,128)}), f32[24,2304]{1,0:T(8,128)}) %reduce-scatter.8.cloned.1.call-update) | async-done | bytes 221200 | tf_op jit(solution)/shard_map/reduce_scatter | solution.py:225
  (367 shorter events, 229.0 us)
Async XLA Ops:
  7.2 68.0 %all-gather.5.cloned.1.call-start = ((), (), s32[]{:S(2)}) async-start(), calls=%async_computation.6 | async-start | bytes 4718592 | tf_op jit(solution)/shard_map/all_gather | solution.py:149
  23.4 94.9 %all-gather.3.cloned.1.call-start = ((), (), s32[]{:S(2)}) async-start(), calls=%async_computation.5 | async-start | bytes 4718592 | tf_op jit(solution)/shard_map/all_gather | solution.py:148
  57.9 654.1 %reduce-scatter.6.cloned.1.call-start = ((), (), s32[]{:S(2)}) async-start(), calls=%async_computation.7 | async-start | bytes 9437184 | tf_op jit(solution)/shard_map/reduce_scatter | solution.py:196
  134.7 13.9 %copy-start.24 = (f32[12,1024]{1,0:T(8,128)S(1)}, f32[12,1024]{1,0:T(8,128)}, u32[]{:S(2)}) copy-start(f32[12,1024]{1,0:T(8,128)} %get-tuple-element.550) | copy-start | bytes 147460 | tf_op jit(solution)/shard_map/while
  148.6 11.3 copy-start.26
  148.6 11.4 copy-start.21
  160.0 11.8 copy-start.27
  174.6 13.9 %copy-start.24 = (f32[12,1024]{1,0:T(8,128)S(1)}, f32[12,1024]{1,0:T(8,128)}, u32[]{:S(2)}) copy-start(f32[12,1024]{1,0:T(8,128)} %get-tuple-element.550) | copy-start | bytes 147460 | tf_op jit(solution)/shard_map/while
  188.5 11.3 copy-start.26
  188.5 11.4 copy-start.21
  199.9 11.8 copy-start.27
  214.4 13.9 %copy-start.24 = (f32[12,1024]{1,0:T(8,128)S(1)}, f32[12,1024]{1,0:T(8,128)}, u32[]{:S(2)}) copy-start(f32[12,1024]{1,0:T(8,128)} %get-tuple-element.550) | copy-start | bytes 147460 | tf_op jit(solution)/shard_map/while
  228.4 11.3 copy-start.26
  228.4 11.4 copy-start.21
  239.7 11.8 copy-start.27
  254.3 13.9 %copy-start.24 = (f32[12,1024]{1,0:T(8,128)S(1)}, f32[12,1024]{1,0:T(8,128)}, u32[]{:S(2)}) copy-start(f32[12,1024]{1,0:T(8,128)} %get-tuple-element.550) | copy-start | bytes 147460 | tf_op jit(solution)/shard_map/while
  268.2 11.3 copy-start.26
  268.3 11.4 copy-start.21
  279.6 11.8 copy-start.27
  297.8 42.6 %copy-start.49 = (f32[1024]{0:T(1024)}, f32[1024]{0:T(1024)S(1)}, u32[]{:S(2)}) copy-start(f32[1024]{0:T(1024)S(1)} %broadcast_multiply_fusion.2) | copy-start | bytes 12292
  299.5 40.9 %copy-start.52 = (f32[1024]{0:T(1024)}, f32[1024]{0:T(1024)S(1)}, u32[]{:S(2)}) copy-start(f32[1024]{0:T(1024)S(1)} %fusion.73) | copy-start | bytes 12292
  305.1 16.9 %copy-start.20 = (f32[1024,3072]{1,0:T(8,128)}, f32[1024,3072]{1,0:T(8,128)S(1)}, u32[]{:S(2)}) copy-start(f32[1024,3072]{1,0:T(8,128)S(1)} %fusion.81) | copy-start | bytes 37748740
  349.2 13.7 %copy-start.19 = (pred[1024,512]{0,1:T(8,128)(4,1)}, pred[1024,512]{0,1:T(8,128)(4,1)S(1)}, u32[]{:S(2)}) copy-start(pred[1024,512]{0,1:T(8,128)(4,1)S(1)} %broadcast_compare_fusion.5) | copy-start | bytes 1572868 | tf_op jit(solution)/shard_map/while
  349.2 13.7 %copy-start.25 = (f32[12,1024]{1,0:T(8,128)S(1)}, f32[12,1024]{1,0:T(8,128)}, u32[]{:S(2)}) copy-start(f32[12,1024]{1,0:T(8,128)} %get-tuple-element.606) | copy-start | bytes 147460 | tf_op jit(solution)/shard_map/while
  349.2 13.7 %copy-start.29 = (f32[12,1024]{1,0:T(8,128)S(1)}, f32[12,1024]{1,0:T(8,128)}, u32[]{:S(2)}) copy-start(f32[12,1024]{1,0:T(8,128)} %get-tuple-element.607) | copy-start | bytes 147460 | tf_op jit(solution)/shard_map/while
  349.2 13.7 %copy-start.40 = (bf16[1024,12,64]{0,2,1:T(8,128)(2,1)S(1)}, bf16[1024,12,64]{0,2,1:T(8,128)(2,1)}, u32[]{:S(2)}) copy-start(bf16[1024,12,64]{0,2,1:T(8,128)(2,1)} %get-tuple-element.609) | copy-start | bytes 4718596 | tf_op jit(solution)/shard_map/while
  417.9 13.7 %copy-start.19 = (pred[1024,512]{0,1:T(8,128)(4,1)}, pred[1024,512]{0,1:T(8,128)(4,1)S(1)}, u32[]{:S(2)}) copy-start(pred[1024,512]{0,1:T(8,128)(4,1)S(1)} %broadcast_compare_fusion.5) | copy-start | bytes 1572868 | tf_op jit(solution)/shard_map/while
  418.0 13.7 %copy-start.25 = (f32[12,1024]{1,0:T(8,128)S(1)}, f32[12,1024]{1,0:T(8,128)}, u32[]{:S(2)}) copy-start(f32[12,1024]{1,0:T(8,128)} %get-tuple-element.606) | copy-start | bytes 147460 | tf_op jit(solution)/shard_map/while
  418.0 13.7 %copy-start.29 = (f32[12,1024]{1,0:T(8,128)S(1)}, f32[12,1024]{1,0:T(8,128)}, u32[]{:S(2)}) copy-start(f32[12,1024]{1,0:T(8,128)} %get-tuple-element.607) | copy-start | bytes 147460 | tf_op jit(solution)/shard_map/while
  418.0 13.7 %copy-start.40 = (bf16[1024,12,64]{0,2,1:T(8,128)(2,1)S(1)}, bf16[1024,12,64]{0,2,1:T(8,128)(2,1)}, u32[]{:S(2)}) copy-start(bf16[1024,12,64]{0,2,1:T(8,128)(2,1)} %get-tuple-element.609) | copy-start | bytes 4718596 | tf_op jit(solution)/shard_map/while
  475.5 9.8 copy-start.16
  475.5 9.8 copy-start.17
  487.6 13.7 %copy-start.19 = (pred[1024,512]{0,1:T(8,128)(4,1)}, pred[1024,512]{0,1:T(8,128)(4,1)S(1)}, u32[]{:S(2)}) copy-start(pred[1024,512]{0,1:T(8,128)(4,1)S(1)} %broadcast_compare_fusion.5) | copy-start | bytes 1572868 | tf_op jit(solution)/shard_map/while
  487.6 13.7 %copy-start.25 = (f32[12,1024]{1,0:T(8,128)S(1)}, f32[12,1024]{1,0:T(8,128)}, u32[]{:S(2)}) copy-start(f32[12,1024]{1,0:T(8,128)} %get-tuple-element.606) | copy-start | bytes 147460 | tf_op jit(solution)/shard_map/while
  487.6 13.7 %copy-start.29 = (f32[12,1024]{1,0:T(8,128)S(1)}, f32[12,1024]{1,0:T(8,128)}, u32[]{:S(2)}) copy-start(f32[12,1024]{1,0:T(8,128)} %get-tuple-element.607) | copy-start | bytes 147460 | tf_op jit(solution)/shard_map/while
  487.6 13.7 %copy-start.40 = (bf16[1024,12,64]{0,2,1:T(8,128)(2,1)S(1)}, bf16[1024,12,64]{0,2,1:T(8,128)(2,1)}, u32[]{:S(2)}) copy-start(bf16[1024,12,64]{0,2,1:T(8,128)(2,1)} %get-tuple-element.609) | copy-start | bytes 4718596 | tf_op jit(solution)/shard_map/while
  545.2 9.8 copy-start.16
  545.2 9.8 copy-start.17
  557.3 13.7 %copy-start.19 = (pred[1024,512]{0,1:T(8,128)(4,1)}, pred[1024,512]{0,1:T(8,128)(4,1)S(1)}, u32[]{:S(2)}) copy-start(pred[1024,512]{0,1:T(8,128)(4,1)S(1)} %broadcast_compare_fusion.5) | copy-start | bytes 1572868 | tf_op jit(solution)/shard_map/while
  557.3 13.7 %copy-start.25 = (f32[12,1024]{1,0:T(8,128)S(1)}, f32[12,1024]{1,0:T(8,128)}, u32[]{:S(2)}) copy-start(f32[12,1024]{1,0:T(8,128)} %get-tuple-element.606) | copy-start | bytes 147460 | tf_op jit(solution)/shard_map/while
  557.3 13.7 %copy-start.29 = (f32[12,1024]{1,0:T(8,128)S(1)}, f32[12,1024]{1,0:T(8,128)}, u32[]{:S(2)}) copy-start(f32[12,1024]{1,0:T(8,128)} %get-tuple-element.607) | copy-start | bytes 147460 | tf_op jit(solution)/shard_map/while
  557.3 13.7 %copy-start.40 = (bf16[1024,12,64]{0,2,1:T(8,128)(2,1)S(1)}, bf16[1024,12,64]{0,2,1:T(8,128)(2,1)}, u32[]{:S(2)}) copy-start(bf16[1024,12,64]{0,2,1:T(8,128)(2,1)} %get-tuple-element.609) | copy-start | bytes 4718596 | tf_op jit(solution)/shard_map/while
  614.9 9.8 copy-start.16
  614.9 9.8 copy-start.17
  634.8 210.6 %reduce-scatter.10.cloned.1.call-start = ((), (), s32[]{:S(2)}) async-start(), calls=%async_computation.9 | async-start | bytes 2433024 | tf_op jit(solution)/shard_map/reduce_scatter | solution.py:220
  639.6 319.0 %reduce-scatter.14.cloned.1.call-start = ((), (), s32[]{:S(2)}) async-start(), calls=%async_computation.11 | async-start | bytes 9732096 | tf_op jit(solution)/shard_map/reduce_scatter | solution.py:222
  653.6 446.9 %reduce-scatter.12.cloned.1.call-start = ((), (), s32[]{:S(2)}) async-start(), calls=%async_computation.10 | async-start | bytes 9732096 | tf_op jit(solution)/shard_map/reduce_scatter | solution.py:221
  665.0 559.9 %reduce-scatter.8.cloned.1.call-start = ((), (), s32[]{:S(2)}) async-start(), calls=%async_computation.8 | async-start | bytes 7299072 | tf_op jit(solution)/shard_map/reduce_scatter | solution.py:225
  (74 other events, 302.8 us)
Sparse Core Ops, SparseCore 0:
  23.5 47.6 all-gather.4
  73.3 44.9 all-gather.2
  634.9 77.0 reduce-scatter.5
  718.5 98.9 reduce-scatter.9
  823.9 134.6 reduce-scatter.13
  965.9 134.5 reduce-scatter.11
  1106.7 118.0 reduce-scatter.7
where the time goes:
time: 1240 us; the launch traced here: 1230 us
  matrix products  467 us (38%)
  waiting for transfers between devices  442 us (36%)
  local copies, waits for them, and re-layouts  137 us (11%)
  other arithmetic  129 us (10%)
  blocking collectives  40.1 us (3%)
  between operations  15.3 us (1%)
    reduce_scatter x1, waiting for transfers between devices, shards(): lax.psum_scatter(grad_w_up, ('wide', 'blk'), scatter_dimension=0, tiled=T...  142 us
    reduce_scatter x1, waiting for transfers between devices, shards(): lax.psum_scatter(grad_w_qkv, ('wide', 'blk'), scatter_dimension=0, tiled=...  124 us
    reduce_scatter x1, waiting for transfers between devices, shards(): lax.psum_scatter(grad_w_down, ('wide', 'blk'), scatter_dimension=0, tiled...  113 us
    dot_general x4, matrix products, block_grads(): jnp.einsum('hqk,qhd->khd', weights.astype(jnp.bfloat16).astype(jnp.float3...  71.7 us
    dot_general x4, matrix products, block_grads(): jnp.einsum('qhd,khd->hqk', do_blk, v_blk, preferred_element_type=jnp.floa...  64.5 us
    dot_general x4, matrix products, scores(): jnp.einsum('qhd,khd->hqk', q_low, k_blk, preferred_element_type=jnp.float32)  55.6 us
    dot_general x4, matrix products, block_grads(): jnp.einsum('qhd,khd->hqk', q_blk, k_blk, preferred_element_type=jnp.float32)  54.6 us
    dot_general x4, matrix products, step(): jnp.einsum('hqk,khd->hqd', weights.astype(jnp.bfloat16), block[1], prefer...  47.3 us
  transfers between devices with their start and end apart: 7, of which 5 were waited for; matrix products, arithmetic and copies ran while one was open for 16% of the time, Pallas kernels for 0%

commit v1 on v0

v1 whole, which is shorter than its diff:
```python
import functools
import math

import jax
import jax.numpy as jnp
from jax import lax
from jax.experimental import pallas as pl
from jax.experimental.pallas import tpu as pltpu
from jax.sharding import PartitionSpec as P

H = 12
HD = 64
EPS = 1e-06
AXES = ("wide", "blk")
AUG = 16
BLOCKED = -512.0
LOG2E = math.log2(math.e)
NN = (((1,), (0,)), ((), ()))
NT = (((1,), (1,)), ((), ()))
TN = (((0,), (0,)), ((), ()))
TT = (((0,), (1,)), ((), ()))
BF16 = jnp.bfloat16
F32 = jnp.float32
VMEM_LIMIT = 56 * 2**20


def mul(left, right, dims, kind=F32):
    return lax.dot_general(left, right, dims, preferred_element_type=F32).astype(kind)


def forward_kernel(bk, first, *refs):
    if first:
        q_ref, k_ref, v_ref, mq_ref, mk_ref, ones_ref, acc_ref, e_ref = refs
    else:
        q_ref, k_ref, v_ref, mq_ref, mk_ref, ones_ref, had_ref, e_ref, o_ref, linv_ref = refs
    keys = k_ref.shape[2]
    q = jnp.concatenate([q_ref[0], mq_ref[...]], axis=0)
    acc = None if first else had_ref[0]
    for i in range(keys // bk):
        cut = slice(i * bk, (i + 1) * bk)
        k = jnp.concatenate([k_ref[0, :, cut], mk_ref[:, cut]], axis=0)
        v = jnp.concatenate([v_ref[0, :, cut], ones_ref[:, cut]], axis=0)
        e = jnp.exp2(mul(k, q, TN)).astype(BF16)
        e_ref[0, cut, :] = e
        part = mul(v, e, NN)
        acc = part if acc is None else acc + part
    if first:
        acc_ref[0] = acc
    else:
        linv = 1.0 / acc[HD : HD + 1]
        o_ref[0] = (acc[:HD] * linv).astype(BF16)
        linv_ref[0] = jnp.broadcast_to(linv, linv_ref.shape[1:])


def head_block(*tail):
    return pl.BlockSpec((1,) + tail, lambda h: (h,) + (0,) * len(tail))


def whole_block(shape):
    return pl.BlockSpec(shape, lambda h: (0,) * len(shape))


def key_block(keys):
    return math.gcd(keys, 512)


def attend(q, k, v, mask_q, mask_k, ones, had=None):
    heads, _, rows = q.shape
    keys = k.shape[2]
    first = had is None
    ins = [q, k, v, mask_q, mask_k, ones]
    specs = [head_block(HD, rows), head_block(HD, keys), head_block(HD, keys)]
    specs += [whole_block(a.shape) for a in (mask_q, mask_k, ones)]
    e_shape = jax.ShapeDtypeStruct((heads, keys, rows), BF16)
    e_spec = head_block(keys, rows)
    if first:
        outs = [jax.ShapeDtypeStruct((heads, HD + AUG, rows), F32), e_shape]
        out_specs = [head_block(HD + AUG, rows), e_spec]
    else:
        ins.append(had)
        specs.append(head_block(HD + AUG, rows))
        outs = [
            e_shape,
            jax.ShapeDtypeStruct((heads, HD, rows), BF16),
            jax.ShapeDtypeStruct((heads, 8, rows), F32),
        ]
        out_specs = [e_spec, head_block(HD, rows), head_block(8, rows)]
    return pl.pallas_call(
        functools.partial(forward_kernel, key_block(keys), first),
        grid=(heads,),
        in_specs=specs,
        out_specs=out_specs,
        out_shape=outs,
        compiler_params=pltpu.CompilerParams(vmem_limit_bytes=VMEM_LIMIT),
        cost_estimate=pl.CostEstimate(
            flops=heads * rows * keys * 1024,
            bytes_accessed=heads * rows * keys * 2,
            transcendentals=heads * rows * keys,
        ),
        name="attend_first" if first else "attend_last",
    )(*ins)


def backward_kernel(bk, first, *refs):
    if first:
        e_ref, do_ref, o_ref, linv_ref, q_ref, k_ref, v_ref, ones_ref, dq_ref, dk_ref, dv_ref = refs
    else:
        e_ref, do_ref, o_ref, linv_ref, q_ref, k_ref, v_ref, ones_ref, had_ref, dq_ref, dk_ref, dv_ref = refs
    keys = k_ref.shape[2]
    low = (do_ref[0] * linv_ref[0, :1]).astype(BF16)
    delta = -jnp.sum(low.astype(F32) * o_ref[0].astype(F32), axis=0, keepdims=True)
    top = delta.astype(BF16).astype(F32)
    row = lax.broadcasted_iota(jnp.int32, (AUG, delta.shape[1]), 0)
    extra = jnp.where(row == 0, top, jnp.where(row == 1, delta - top, 0.0)).astype(BF16)
    do = jnp.concatenate([low, extra], axis=0)
    q = q_ref[0]
    acc = None if first else had_ref[0]
    for i in range(keys // bk):
        cut = slice(i * bk, (i + 1) * bk)
        k = k_ref[0, :, cut]
        v = jnp.concatenate([v_ref[0, :, cut], ones_ref[:, cut]], axis=0)
        e = e_ref[0, cut, :]
        ds = (e.astype(F32) * mul(v, do, TN)).astype(BF16)
        part = mul(k, ds, NN)
        acc = part if acc is None else acc + part
        dk_ref[0, :, cut] = mul(q, ds, NT).astype(dk_ref.dtype)
        dv_ref[0, :, cut] = mul(low, e, NT).astype(dv_ref.dtype)
    dq_ref[0] = acc


def attend_back(e, do, o, linv, q, k, v, ones, start, heads, kind, had=None):
    _, keys, rows = e.shape
    first = had is None

    def block(*tail):
        return pl.BlockSpec((1,) + tail, lambda h: (h + start,) + (0,) * len(tail))

    ins = [e, do, o, linv, q, k, v, ones]
    specs = [block(keys, rows), block(HD, rows), block(HD, rows), block(8, rows), block(HD, rows)]
    specs += [block(HD, keys), block(HD, keys), whole_block(ones.shape)]
    if not first:
        ins.append(had)
        specs.append(head_block(HD, rows))
    return pl.pallas_call(
        functools.partial(backward_kernel, key_block(keys), first),
        grid=(heads,),
        in_specs=specs,
        out_specs=[head_block(HD, rows), head_block(HD, keys), head_block(HD, keys)],
        out_shape=[
            jax.ShapeDtypeStruct((heads, HD, rows), F32),
            jax.ShapeDtypeStruct((heads, HD, keys), kind),
            jax.ShapeDtypeStruct((heads, HD, keys), kind),
        ],
        compiler_params=pltpu.CompilerParams(vmem_limit_bytes=VMEM_LIMIT),
        cost_estimate=pl.CostEstimate(
            flops=heads * rows * keys * 2300,
            bytes_accessed=heads * rows * keys * 2,
            transcendentals=0,
        ),
        name="attend_back_first" if first else "attend_back_last",
    )(*ins)


def norm(value, axis):
    mean = jnp.mean(value, axis=axis, keepdims=True)
    centred = value - mean
    scale = lax.rsqrt(jnp.mean(centred * centred, axis=axis, keepdims=True) + EPS)
    return centred * scale, scale


def norm_back(grad, unit, scale, axis):
    mean = jnp.mean(grad, axis=axis, keepdims=True)
    along = jnp.mean(grad * unit, axis=axis, keepdims=True)
    return scale * (grad - mean - unit * along)


def gelu_parts(u):
    root = math.sqrt(2.0 / math.pi)
    square = u * u
    t = jnp.tanh(root * (u + 0.044715 * u * square))
    value = 0.5 * u * (1.0 + t)
    slope = 0.5 * (1.0 + t) + 0.5 * u * (1.0 - t * t) * root * (1.0 + 3 * 0.044715 * square)
    return value, slope


def place(index):
    return index // 8, index // 4 % 2, index // 2 % 2, index % 2


def device(z, x, core, y):
    return ((z * 2 + x) * 2 + core) * 2 + y


def pairs(other):
    return [(i, device(*other(*place(i)))) for i in range(32)]


SWAP = pairs(lambda z, x, c, y: (z, x, y, c))
ACROSS = {
    "c": pairs(lambda z, x, c, y: (z, x, 1 - c, y)),
    "x": pairs(lambda z, x, c, y: (z, 1 - x, c, y)),
    "y": pairs(lambda z, x, c, y: (z, x, c, 1 - y)),
    "l": pairs(lambda z, x, c, y: (z // 2 * 2 + 1 - z % 2, x, c, y)),
    "h": pairs(lambda z, x, c, y: (3 - (z // 2 * 2 + 1 - z % 2), x, c, y)),
}
ACROSS["h"] = pairs(lambda z, x, c, y: ((z + 2) % 4, x, c, y))


def summed(piece, order, at):
    names = ["h", "l", "x", "c", "y"]
    shape = piece.shape
    part = piece.reshape((2,) * 5 + (shape[0] // 32,) + shape[1:])
    for step, name in enumerate(order):
        axis = names.index(name)
        names.pop(axis)
        give = lax.dynamic_index_in_dim(part, 1 - at[name], axis, keepdims=False)
        keep = lax.dynamic_index_in_dim(part, at[name], axis, keepdims=False)
        came = lax.ppermute(give, AXES, ACROSS[name])
        part = keep.astype(F32) + came.astype(F32)
        if step < 4:
            part = part.astype(BF16)
    return part


def shards(
    tokens,
    lengths,
    ln1_gain,
    ln1_bias,
    w_qkv,
    q_gain,
    k_gain,
    w_out,
    ln2_gain,
    ln2_bias,
    w_up,
    w_down,
    cotangent,
):
    rows, width = tokens.shape
    parts = lax.axis_size("blk")
    known = parts == 2 and lax.axis_size("wide") == 16
    group = rows * parts
    if known:
        wide = lax.axis_index("wide")
        at = {
            "h": wide // 8,
            "l": wide // 4 % 2,
            "x": wide // 2 % 2,
            "c": wide % 2,
            "y": lax.axis_index("blk"),
        }
        lengths = lax.ppermute(lengths, AXES, SWAP)
        tokens = lax.ppermute(tokens, AXES, SWAP)
        cotangent = lax.ppermute(cotangent, AXES, SWAP)
        mine = at["c"]
    else:
        mine = lax.axis_index("blk")

    count = lengths.shape[1]
    place_of = jnp.arange(count)
    ends = jnp.sum(jnp.where(place_of[:, None] <= place_of[None, :], lengths[0][:, None], 0), axis=0)
    spots = jnp.arange(group, dtype=jnp.int32)
    segment = jnp.sum((spots[None, :] >= ends[:, None]).astype(jnp.int32), axis=0)
    is_in = jnp.arange(AUG)[:, None] == segment[None, :]
    mask_k = is_in.astype(BF16)
    mask_q = jnp.where(is_in, 0.0, BLOCKED).astype(BF16)
    mask_q = lax.dynamic_slice_in_dim(mask_q, mine * rows, rows, axis=1)
    ones = jnp.broadcast_to((jnp.arange(AUG) < 2)[:, None], (AUG, group)).astype(BF16)

    x = tokens.astype(F32)
    unit1, scale1 = norm(x, -1)
    h = (unit1 * ln1_gain + ln1_bias).astype(BF16)
    qkv = mul(w_qkv, h, TT).reshape(3, H, HD, rows)
    gain_q = q_gain.reshape(H, HD, 1)
    gain_k = k_gain.reshape(H, HD, 1)
    unit_k, scale_k = norm(qkv[1], 1)
    k = (unit_k * gain_k).astype(BF16)
    v = qkv[2].astype(BF16)
    unit_q, scale_q = norm(qkv[0], 1)
    q = (unit_q * (gain_q * (LOG2E / math.sqrt(HD)))).astype(BF16)
    if known:
        theirs = lax.ppermute(jnp.stack([k, v]), AXES, ACROSS["c"])
        k_far, v_far = theirs[0], theirs[1]
        mask_near = lax.dynamic_slice_in_dim(mask_k, mine * rows, rows, axis=1)
        mask_far = lax.dynamic_slice_in_dim(mask_k, (1 - mine) * rows, rows, axis=1)
        ones_half = ones[:, :rows]
        had, e_near = attend(q, k, v, mask_q, mask_near, ones_half)
        e_far, o, linv = attend(q, k_far, v_far, mask_q, mask_far, ones_half, had)
    else:
        k_all = lax.all_gather(k, "blk", axis=2, tiled=True)
        v_all = lax.all_gather(v, "blk", axis=2, tiled=True)
        had, e_all = attend(q, k_all, v_all, mask_q, mask_k, ones)
        linv = jnp.broadcast_to(1.0 / had[:, HD : HD + 1], (H, 8, rows))
        o = (had[:, :HD] * linv[:, :1]).astype(BF16)
    o_flat = o.reshape(width, rows)
    x1 = x + mul(o_flat, w_out, TN)
    unit2, scale2 = norm(x1, -1)
    h2 = (unit2 * ln2_gain + ln2_bias).astype(BF16)
    up = mul(h2, w_up, NN)
    act, slope = gelu_parts(up)
    act = act.astype(BF16)
    output = (x1 + mul(act, w_down, NN)).astype(BF16)
    if known:
        output = lax.ppermute(output, AXES, SWAP)

    grad_w_down = mul(act, cotangent, TN, BF16 if known else F32)
    d_up = (mul(cotangent, w_down, NT) * slope).astype(BF16)
    grad_w_up = mul(h2, d_up, TN, BF16 if known else F32)
    d_h2 = mul(d_up, w_up, NT)
    grad_ln2_gain = jnp.sum(d_h2 * unit2, axis=0)
    grad_ln2_bias = jnp.sum(d_h2, axis=0)
    d_x1 = cotangent.astype(F32) + norm_back(d_h2 * ln2_gain, unit2, scale2, -1)
    d_branch = d_x1.astype(BF16)
    grad_w_out = mul(o_flat, d_branch, NN, BF16 if known else F32)
    d_o = mul(w_out, d_branch, NT).reshape(H, HD, rows)

    if known:
        sum_w_down = summed(grad_w_down, "cxlhy", at)
        sum_w_up = summed(grad_w_up, "cxlhy", at)
        sum_w_out = summed(grad_w_out, "cyxlh", at)

    def back(start, heads):
        if known:
            d_q, give_k, give_v = attend_back(
                e_far, d_o, o, linv, q, k_far, v_far, ones_half, start, heads, BF16
            )
            came = lax.ppermute(jnp.stack([give_k, give_v]), AXES, ACROSS["c"]).astype(F32)
            d_q, d_k, d_v = attend_back(
                e_near, d_o, o, linv, q, k, v, ones_half, start, heads, F32, d_q
            )
            d_k, d_v = d_k + came[0], d_v + came[1]
        else:
            d_q, d_k, d_v = attend_back(
                e_all, d_o, o, linv, q, k_all, v_all, ones, start, heads, F32
            )
            pair = jnp.stack([d_k, d_v]).reshape(2, heads, HD, parts, rows)
            pair = jnp.transpose(pair, (3, 0, 1, 2, 4)).astype(BF16)
            pair = lax.psum_scatter(pair, "blk", scatter_dimension=0, tiled=False)
            d_k, d_v = pair[0].astype(F32), pair[1].astype(F32)
        return d_q, d_k, d_v

    def back_norms(start, heads, d_q, d_k, d_v):
        cut = slice(start, start + heads)
        d_q = d_q * (1.0 / math.sqrt(HD))
        d_k = d_k * (1.0 / LOG2E)
        g_q = jnp.sum(d_q * unit_q[cut], axis=2)
        g_k = jnp.sum(d_k * unit_k[cut], axis=2)
        d_q = norm_back(d_q * gain_q[cut], unit_q[cut], scale_q[cut], 1)
        d_k = norm_back(d_k * gain_k[cut], unit_k[cut], scale_k[cut], 1)
        return jnp.stack([d_q, d_k, d_v]).astype(BF16), g_q, g_k

    if known:
        half = H // 2
        first = back_norms(0, half, *back(0, half))
        second = back_norms(half, half, *back(half, half))
        d_qkv = jnp.concatenate([first[0], second[0]], axis=1).reshape(3 * width, rows)
        grad_q_gain = jnp.concatenate([first[1], second[1]]).reshape(width)
        grad_k_gain = jnp.concatenate([first[2], second[2]]).reshape(width)
        half_a = mul(h, first[0].reshape(3 * width // 2, rows), TT, BF16)
        half_b = mul(h, second[0].reshape(3 * width // 2, rows), TT, BF16)
    else:
        d_qkv, grad_q_gain, grad_k_gain = back_norms(0, H, *back(0, H))
        d_qkv = d_qkv.reshape(3 * width, rows)
        grad_q_gain, grad_k_gain = grad_q_gain.reshape(width), grad_k_gain.reshape(width)
        grad_w_qkv = mul(h, d_qkv, TT)
    d_h = mul(d_qkv, w_qkv, TT)
    grad_ln1_gain = jnp.sum(d_h * unit1, axis=0)
    grad_ln1_bias = jnp.sum(d_h, axis=0)
    grad_tokens = (d_x1 + norm_back(d_h * ln1_gain, unit1, scale1, -1)).astype(BF16)
    vectors = [grad_ln1_gain, grad_ln1_bias, grad_q_gain, grad_k_gain, grad_ln2_gain, grad_ln2_bias]
    if known:
        grad_tokens = lax.ppermute(grad_tokens, AXES, SWAP)
        sum_a = summed(half_a, "cxylh", at)
        table = jnp.pad(jnp.stack(vectors, axis=1), ((0, 0), (0, 128 - len(vectors))))
        sum_b = summed(jnp.concatenate([half_b, table.astype(BF16)], axis=1), "cyxlh", at)
        sums = [sum_b[:, 3 * width // 2 + i] for i in range(len(vectors))]
        sum_a = sum_a.reshape(-1, 3, width // 2)
        sum_b = sum_b[:, : 3 * width // 2].reshape(-1, 3, width // 2)
        sum_w_qkv = jnp.concatenate([sum_a, sum_b], axis=2).reshape(-1, 3 * width)
    else:
        scatter = functools.partial(
            lax.psum_scatter, axis_name=AXES, scatter_dimension=0, tiled=True
        )
        sum_w_down, sum_w_up = scatter(grad_w_down), scatter(grad_w_up)
        sum_w_out, sum_w_qkv = scatter(grad_w_out), scatter(grad_w_qkv)
        sums = [scatter(g) for g in vectors]
    return (
        output,
        grad_tokens,
        sums[0],
        sums[1],
        sum_w_qkv,
        sums[2],
        sums[3],
        sum_w_out,
        sums[4],
        sums[5],
        sum_w_up,
        sum_w_down,
    )


def solution(mesh):
    split = P(AXES, None)
    in_specs = (split, P("wide", None)) + (P(),) * 10 + (split,)
    vector = P(AXES)
    out_specs = (
        split,
        split,
        vector,
        vector,
        split,
        vector,
        vector,
        split,
        vector,
        vector,
        split,
        split,
    )
    return jax.shard_map(shards, mesh=mesh, in_specs=in_specs, out_specs=out_specs, check_vma=False)
```

time: 1240 us -> 564 us (0.45)
  matrix products: 467 us -> 92.3 us
  waiting for transfers between devices: 442 us -> 105 us
  Pallas kernels: 0 us -> 103 us
  starting transfers between devices: 0.5 us -> 84.1 us
  local copies, waits for them, and re-layouts: 137 us -> 85 us
  other arithmetic: 129 us -> 81.7 us
  blocking collectives: 40.1 us -> 0 us
  between operations: 15.3 us -> 2.31 us
    reduce_scatter x5 -> x0, waiting for transfers between devices: 414 us -> none  [the longest x1 142 us: shards(): lax.psum_scatter(grad_w_up, ('wide', 'blk'), scatter_dimension=0, tiled=T...]
    dot_general x40 -> x13, matrix products: 467 us -> 92.3 us  [mul(): lax.dot_general(left, right, dims, preferred_element_type=F32).astype(kind)]
    ppermute x0 -> x33, waiting for transfers between devices: none -> 105 us  [the longest x25 105 us: summed(): came = lax.ppermute(give, AXES, ACROSS[name])]
    pallas_call x0 -> x6, Pallas kernels: none -> 103 us  [the longest x4 66.6 us: attend_back(): pl.pallas_call(functools.partial(backward_kernel, key_block(keys), first)...]
    ppermute x0 -> x33, starting transfers between devices: none -> 84.1 us  [the longest x25 28.7 us: summed(): came = lax.ppermute(give, AXES, ACROSS[name])]
    reduce_sum x22 -> x13, other arithmetic: 90.2 us -> 26.6 us  [the longest x3 7.47 us: norm(): mean = jnp.mean(value, axis=axis, keepdims=True)]
    unnamed x1 -> x0, blocking collectives: 40.1 us -> none
    all_gather x2 -> x0, waiting for transfers between devices: 27.7 us -> none  [the longest x1 27.7 us: shards(): lax.all_gather(k_send, 'blk', axis=0, tiled=True)]
  transfers between devices with their start and end apart: 7 -> 33, of which waited for: 5 -> 13; matrix products, arithmetic and copies ran while one was open for 16% -> 36% of each run, Pallas kernels for 0% -> 13%
where the time goes in v1:
time: 564 us; the launch traced here: 554 us
  waiting for transfers between devices  105 us (19%)
  Pallas kernels  103 us (18%)
  matrix products  92.3 us (16%)
  local copies, waits for them, and re-layouts  85 us (15%)
  starting transfers between devices  84.1 us (15%)
  other arithmetic  81.7 us (14%)
    ppermute x25, waiting for transfers between devices, summed(): came = lax.ppermute(give, AXES, ACROSS[name])  105 us
    dot_general x13, matrix products, mul(): lax.dot_general(left, right, dims, preferred_element_type=F32).astype(kind)  92.3 us
    pallas_call x4, Pallas kernels, attend_back(): pl.pallas_call(functools.partial(backward_kernel, key_block(keys), first)...  66.6 us
    pallas_call x2, Pallas kernels, attend(): pl.pallas_call(functools.partial(forward_kernel, key_block(keys), first),...  36.8 us
    ppermute x25, starting transfers between devices, summed(): came = lax.ppermute(give, AXES, ACROSS[name])  28.7 us
    unnamed x167, local copies, waits for them, and re-layouts  20.1 us
    convert_element_type x20, other arithmetic, summed(): part = part.astype(BF16)  16.9 us
    ppermute x1, starting transfers between devices, shards(): tokens = lax.ppermute(tokens, AXES, SWAP)  13.3 us
  transfers between devices with their start and end apart: 33, of which 13 were waited for; matrix products, arithmetic and copies ran while one was open for 36% of the time, Pallas kernels for 13%

profile of v1, /device:TPU:0, one launch (start us, length us, event | category | flops | bytes accessed | tf_op | source)
XLA Modules:
  0.0 554.0 jit_solution(17446768239390547428)
XLA Ops:
  0.7 2.7 copy.158
  3.4 13.3 %collective-permute-start = (bf16[1024,768]{0,1:T(8,128)(2,1)}, bf16[1024,768]{0,1:T(8,128)(2,1)}, u32[]{:S(2)}, u32[]{:S(2)}) collective-permute-start(bf16[1024,768]{0,1:T(8,128)(2,1)} %copy.158), channel_id=1, source_target_pairs={{0,0},{1,2},{2,1},{3,3},{4,4},{5,6},{6,5},{7,7},{8,8},{9,10},{10,9... | collective-permute-start | bytes 4718600 | tf_op jit(solution)/shard_map/ppermute | solution.py:254
  21.1 13.3 %collective-permute-start.4 = (bf16[1024,768]{0,1:T(8,128)(2,1)}, bf16[1024,768]{0,1:T(8,128)(2,1)}, u32[]{:S(2)}, u32[]{:S(2)}) collective-permute-start(bf16[1024,768]{0,1:T(8,128)(2,1)} %copy.165), channel_id=1, source_target_pairs={{0,0},{1,2},{2,1},{3,3},{4,4},{5,6},{6,5},{7,7},{8,8},{9,10},{10,9... | collective-permute-start | bytes 4718600 | tf_op jit(solution)/shard_map/ppermute | solution.py:255
  47.4 5.7 %convolution_bitcast_fusion = f32[2304,1024]{0,1:T(8,128)S(1)} fusion(bf16[768,2304]{1,0:T(8,128)(2,1)S(1)} %copy-done, bf16[1024,768]{0,1:T(8,128)(2,1)} %collective-permute-done, f32[768]{0:T(1024)S(1)} %copy-done.73, f32[768]{0:T(1024)S(1)} %copy-done.62, f32[1024]{0:T(1024)S(1)} %add_rsqrt_fusion.3, f32[1024]{0:T(1024)S(1)} %broadcast_multiply_fusion.16), kind=kOutput, calls=%fused_computation.3 | convolution fusion | flops 3628597248 | bytes 14563328 | tf_op jit(solution)/shard_map/dot_general | solution.py:28
  54.4 3.1 fusion.53
  57.6 2.7 copy.162
  60.3 3.5 copy.160
  63.8 2.9 reduce_sum.274
  74.8 3.6 copy.159
  78.4 2.9 reduce_sum.272
  86.8 5.5 multiply_convert_fusion.2
  93.0 17.4 %attend_first.1 = (f32[12,80,1024]{2,1,0:T(8,128)}, bf16[12,1024,1024]{2,1,0:T(8,128)(2,1)}) custom-call(bf16[12,64,1024]{2,1,0:T(8,128)(2,1)} %get-tuple-element.186.refs_0_.refs_4_, bf16[12,64,1024]{2,1,0:T(8,128)(2,1)} %get-tuple-element.148.refs_1_.refs_5_, bf16[12,64,1024]{2,1,0:T(8,128)(2,1)} %bitcast.231, ...), custom_call_target="tpu_custom_call" | custom-call | flops 12884901888 | bytes 25165824 | tf_op jit(solution)/shard_map/attend_first/pallas_call | solution.py:88
  110.4 4.0 slice_bitcast_fusion.4
  114.5 19.4 %attend_last.1 = (bf16[12,1024,1024]{2,1,0:T(8,128)(2,1)}, bf16[12,64,1024]{2,1,0:T(8,128)(2,1)}, f32[12,8,1024]{2,1,0:T(8,128)}) custom-call(bf16[12,64,1024]{2,1,0:T(8,128)(2,1)} %get-tuple-element.186.refs_0_.refs_4_, bf16[12,64,1024]{2,1,0:T(8,128)(2,1)} %get-tuple-element.163.refs_1_.refs_5_, bf16[12,64,1024]{2,1,0:T(8,128)(2,1)} %get-tuple-element.162.refs_2_.refs_6_, ...), custom_call_target="tpu_custom_call" | custom-call | flops 12884901888 | bytes 25165824 | tf_op jit(solution)/shard_map/attend_last/pallas_call | solution.py:88
  133.9 3.6 fusion.56
  138.3 8.6 %fusion.47 = f32[1024,3072]{1,0:T(8,128)} fusion(bf16[768,3072]{1,0:T(8,128)(2,1)S(1)} %bitcast.236, f32[1024,768]{0,1:T(8,128)S(1)} %get-tuple-element.181, f32[768]{0:T(1024)S(1)} %copy-done.46, f32[768]{0:T(1024)S(1)} %copy-done.44, f32[1024]{0:T(1024)S(1)} %add_rsqrt_fusion.2, f32[1024]{0:T(1024)S(1)} %broadcast_multiply_fusion.15), kind=kOutput, calls=%fused_computation.210 | convolution fusion | flops 4835770368 | bytes 20461568 | tf_op jit(solution)/shard_map/dot_general | solution.py:28
  146.9 10.0 %add_convert_fusion = bf16[1024,768]{0,1:T(8,128)(2,1)} fusion(f32[1024,768]{0,1:T(8,128)S(1)} %get-tuple-element.181, bf16[3072,768]{1,0:T(8,128)(2,1)S(1)} %bitcast.250, f32[1024,3072]{1,0:T(8,128)} %fusion.47), kind=kOutput, calls=%fused_computation.40 | convolution fusion | flops 4861722624 | bytes 22020096 | tf_op jit(solution)/shard_map/dot_general | solution.py:28
  156.8 15.7 %multiply_convert_fusion = bf16[1024,3072]{1,0:T(8,128)(2,1)} fusion(f32[1024,3072]{1,0:T(8,128)} %fusion.47, bf16[1024,768]{0,1:T(8,128)(2,1)} %collective-permute-done.4, bf16[3072,768]{1,0:T(8,128)(2,1)S(1)} %bitcast.250), kind=kOutput, calls=%fused_computation | convolution fusion | flops 4888461312 | bytes 25165824 | tf_op jit(solution)/shard_map/dot_general | solution.py:28
  172.5 8.8 %fusion.58 = (bf16[768]{0:T(1024)(128)(2,1)S(1)}, f32[1024,768]{1,0:T(8,128)}) fusion(bf16[1024,3072]{1,0:T(8,128)(2,1)} %multiply_convert_fusion, bf16[768,3072]{1,0:T(8,128)(2,1)S(1)} %bitcast.236), kind=kOutput, calls=%fused_computation.216 | convolution fusion | flops 4832623616 | bytes 14157312 | tf_op jit(solution)/shard_map/dot_general | solution.py:28
  181.4 7.1 %convolution_convert_fusion.1 = bf16[768,3072]{1,0:T(8,128)(2,1)} fusion(bf16[1024,3072]{1,0:T(8,128)(2,1)S(1)} %copy-done.76, f32[1024,768]{0,1:T(8,128)S(1)} %get-tuple-element.181, f32[768]{0:T(1024)S(1)} %copy-done.46, f32[768]{0:T(1024)S(1)} %copy-done.44, f32[1024]{0:T(1024)S(1)} %add_rsqrt_fusion.2, f32[1024]{0:T(1024)S(1)} %broadcast_multiply_fusion.15), kind=kOutput, calls=%fused_computation.5 | convolution fusion | flops 4838129664 | bytes 14170112 | tf_op jit(solution)/shard_map/dot_general | solution.py:28
  188.5 3.9 copy.166
  192.5 4.0 multiply_reduce_fusion
  201.9 3.2 fusion.35
  205.1 16.3 %attend_back_first.3 = (f32[6,64,1024]{2,1,0:T(8,128)}, bf16[6,64,1024]{2,1,0:T(8,128)(2,1)}, bf16[6,64,1024]{2,1,0:T(8,128)(2,1)}) custom-call(bf16[12,1024,1024]{2,1,0:T(8,128)(2,1)} %get-tuple-element.33.refs_0_, f32[12,64,1024]{2,1,0:T(8,128)} %bitcast.251, bf16[12,64,1024]{2,1,0:T(8,128)(2,1)} %get-tuple-element.30.refs_2_, ...), custom_call_target="tpu_custom_call" | custom-call | flops 14470348800 | bytes 12582912 | tf_op jit(solution)/shard_map/attend_back_first/pallas_call | solution.py:144
  221.4 16.3 %attend_back_first.2 = (f32[6,64,1024]{2,1,0:T(8,128)}, bf16[6,64,1024]{2,1,0:T(8,128)(2,1)}, bf16[6,64,1024]{2,1,0:T(8,128)(2,1)}) custom-call(bf16[12,1024,1024]{2,1,0:T(8,128)(2,1)} %get-tuple-element.33.refs_0_, f32[12,64,1024]{2,1,0:T(8,128)} %bitcast.252, bf16[12,64,1024]{2,1,0:T(8,128)(2,1)} %get-tuple-element.30.refs_2_, ...), custom_call_target="tpu_custom_call" | custom-call | flops 14470348800 | bytes 12582912 | tf_op jit(solution)/shard_map/attend_back_first/pallas_call | solution.py:144
  237.8 13.3 %collective-permute-start.3 = (bf16[1024,768]{0,1:T(8,128)(2,1)}, bf16[1024,768]{0,1:T(8,128)(2,1)}, u32[]{:S(2)}, u32[]{:S(2)}) collective-permute-start(bf16[1024,768]{0,1:T(8,128)(2,1)} %add_convert_fusion), channel_id=1, source_target_pairs={{0,0},{1,2},{2,1},{3,3},{4,4},{5,6},{6,5},{7,7},{8,8},{9,10},{10,9... | collective-permute-start | bytes 4718600 | tf_op jit(solution)/shard_map/ppermute | solution.py:305
  251.0 11.9 %convolution_convert_fusion = bf16[3072,768]{1,0:T(8,128)(2,1)S(1)} fusion(bf16[1024,768]{0,1:T(8,128)(2,1)} %collective-permute-done.4, f32[1024,3072]{1,0:T(8,128)} %fusion.47), kind=kOutput, calls=%fused_computation.4 | convolution fusion | flops 4862509056 | bytes 18874368 | tf_op jit(solution)/shard_map/dot_general | solution.py:28
  271.7 16.8 %attend_back_last.3 = (f32[6,64,1024]{2,1,0:T(8,128)}, f32[6,64,1024]{2,1,0:T(8,128)}, f32[6,64,1024]{2,1,0:T(8,128)}) custom-call(bf16[12,1024,1024]{2,1,0:T(8,128)(2,1)} %get-tuple-element.31.refs_0_, f32[12,64,1024]{2,1,0:T(8,128)} %bitcast.253, bf16[12,64,1024]{2,1,0:T(8,128)(2,1)} %get-tuple-element.30.refs_2_, ...), custom_call_target="tpu_custom_call" | custom-call | flops 14470348800 | bytes 12582912 | tf_op jit(solution)/shard_map/attend_back_last/pallas_call | solution.py:144
  288.5 17.1 %attend_back_last.2 = (f32[6,64,1024]{2,1,0:T(8,128)}, f32[6,64,1024]{2,1,0:T(8,128)}, f32[6,64,1024]{2,1,0:T(8,128)}) custom-call(bf16[12,1024,1024]{2,1,0:T(8,128)(2,1)} %get-tuple-element.31.refs_0_, f32[12,64,1024]{2,1,0:T(8,128)} %bitcast.254, bf16[12,64,1024]{2,1,0:T(8,128)(2,1)} %get-tuple-element.30.refs_2_, ...), custom_call_target="tpu_custom_call" | custom-call | flops 14470348800 | bytes 12582912 | tf_op jit(solution)/shard_map/attend_back_last/pallas_call | solution.py:144
  308.2 4.3 constant_dynamic-slice_fusion.3
  316.2 7.7 %collective-permute-done.19 = bf16[2,2,2,24,768]{4,3,0,1,2:T(8,128)(2,1)S(1)} collective-permute-done((bf16[2,2,2,24,768]{4,3,0,1,2:T(8,128)(2,1)S(1)}, bf16[2,2,2,24,768]{4,3,0,1,2:T(8,128)(2,1)S(1)}, u32[]{:S(2)}, u32[]{:S(2)}) %collective-permute-start.19) | collective-permute-done | bytes 294944 | tf_op jit(solution)/shard_map/ppermute | solution.py:218
  326.0 3.8 collective-permute-done.20
  352.0 3.8 convolution_convert_fusion.2
  360.0 6.4 %fusion.57 = (bf16[768]{0:T(1024)(128)(2,1)}, f32[1024,768]{1,0:T(8,128)}) fusion(bf16[2304,1024]{1,0:T(8,128)(2,1)S(1)} %bitcast.239, bf16[768,2304]{1,0:T(8,128)(2,1)S(1)} %copy-done), kind=kOutput, calls=%fused_computation.215 | convolution fusion | flops 3624664320 | bytes 11404800 | tf_op jit(solution)/shard_map/dot_general | solution.py:28
  366.4 3.5 copy.167
  369.9 5.9 %convolution_convert_fusion.3 = bf16[768,1152]{1,0:T(8,128)(2,1)} fusion(bf16[1152,1024]{1,0:T(8,128)(2,1)} %bitcast.228, bf16[1024,768]{0,1:T(8,128)(2,1)} %collective-permute-done, f32[768]{0:T(1024)S(1)} %copy-done.74, f32[768]{0:T(1024)S(1)} %copy-done.63, f32[1024]{0:T(1024)S(1)} %copy-done.58, f32[1024]{0:T(1024)S(1)} %copy-done.54), kind=kOutput, calls=%fused_computation.25 | convolution fusion | flops 1817542656 | bytes 5715968 | tf_op jit(solution)/shard_map/dot_general | solution.py:28
  375.9 3.1 fusion.16
  387.4 4.5 fusion.15
  392.0 13.3 %collective-permute-start.7 = (bf16[1024,768]{0,1:T(8,128)(2,1)}, bf16[1024,768]{0,1:T(8,128)(2,1)}, u32[]{:S(2)}, u32[]{:S(2)}) collective-permute-start(bf16[1024,768]{0,1:T(8,128)(2,1)} %fusion.15), channel_id=1, source_target_pairs={{0,0},{1,2},{2,1},{3,3},{4,4},{5,6},{6,5},{7,7},{8,8},{9,10},{10,9... | collective-permute-start | bytes 4718600 | tf_op jit(solution)/shard_map/ppermute | solution.py:373
  405.2 2.8 copy.180
  408.1 3.2 fusion
  414.0 2.6 fusion.1
  423.0 42.8 %collective-permute-done.14 = bf16[2,2,2,24,1152]{4,3,0,1,2:T(8,128)(2,1)S(1)} collective-permute-done((bf16[2,2,2,24,1152]{4,3,0,1,2:T(8,128)(2,1)S(1)}, bf16[2,2,2,24,1152]{4,3,0,1,2:T(8,128)(2,1)S(1)}, u32[]{:S(2)}, u32[]{:S(2)}) %collective-permute-start.14) | collective-permute-done | bytes 442400 | tf_op jit(solution)/shard_map/ppermute | solution.py:218
  466.3 6.4 %collective-permute-done.15 = bf16[2,2,24,1152]{3,2,0,1:T(8,128)(2,1)S(1)} collective-permute-done((bf16[2,2,24,1152]{3,2,0,1:T(8,128)(2,1)S(1)}, bf16[2,2,24,1152]{3,2,0,1:T(8,128)(2,1)S(1)}, u32[]{:S(2)}, u32[]{:S(2)}) %collective-permute-start.15) | collective-permute-done | bytes 221216 | tf_op jit(solution)/shard_map/ppermute | solution.py:218
  507.8 14.0 %collective-permute-done.30 = bf16[2,2,96,768]{3,2,1,0:T(8,128)(2,1)S(1)} collective-permute-done((bf16[2,2,96,768]{3,2,1,0:T(8,128)(2,1)S(1)}, bf16[2,2,96,768]{3,2,1,0:T(8,128)(2,1)S(1)}, u32[]{:S(2)}, u32[]{:S(2)}) %collective-permute-start.30) | collective-permute-done | bytes 589856 | tf_op jit(solution)/shard_map/ppermute | solution.py:218
  522.1 10.1 %collective-permute-done.25 = bf16[2,2,24,3072]{3,2,1,0:T(8,128)(2,1)S(1)} collective-permute-done((bf16[2,2,24,3072]{3,2,1,0:T(8,128)(2,1)S(1)}, bf16[2,2,24,3072]{3,2,1,0:T(8,128)(2,1)S(1)}, u32[]{:S(2)}, u32[]{:S(2)}) %collective-permute-start.25) | collective-permute-done | bytes 589856 | tf_op jit(solution)/shard_map/ppermute | solution.py:218
  533.0 9.2 %collective-permute-done.31 = bf16[2,96,768]{2,1,0:T(8,128)(2,1)S(1)} collective-permute-done((bf16[2,96,768]{2,1,0:T(8,128)(2,1)S(1)}, bf16[2,96,768]{2,1,0:T(8,128)(2,1)S(1)}, u32[]{:S(2)}, u32[]{:S(2)}) %collective-permute-start.31) | collective-permute-done | bytes 294944 | tf_op jit(solution)/shard_map/ppermute | solution.py:218
  546.4 3.3 collective-permute-start.27
  (349 shorter events, 144.0 us)
Async XLA Ops:
  0.6 46.8 %copy-start = (bf16[768,2304]{1,0:T(8,128)(2,1)S(1)}, bf16[768,2304]{1,0:T(8,128)(2,1)}, u32[]{:S(2)}) copy-start(bf16[768,2304]{1,0:T(8,128)(2,1)} %param.17) | copy-start | bytes 10616836
  0.7 33.7 %copy-start.67 = (f32[768]{0:T(1024)S(1)}, f32[768]{0:T(1024)}, u32[]{:S(2)}) copy-start(f32[768]{0:T(1024)} %param.18) | copy-start | bytes 9220
  3.4 40.4 %collective-permute-start = (bf16[1024,768]{0,1:T(8,128)(2,1)}, bf16[1024,768]{0,1:T(8,128)(2,1)}, u32[]{:S(2)}, u32[]{:S(2)}) collective-permute-start(bf16[1024,768]{0,1:T(8,128)(2,1)} %copy.158), channel_id=1, source_target_pairs={{0,0},{1,2},{2,1},{3,3},{4,4},{5,6},{6,5},{7,7},{8,8},{9,10},{10,9... | collective-permute-start | bytes 4718600 | tf_op jit(solution)/shard_map/ppermute | solution.py:254
  16.7 25.7 %collective-permute-start.2 = (s32[1,6]{1,0:T(1,128)}, s32[1,6]{1,0:T(1,128)}, u32[]{:S(2)}, u32[]{:S(2)}) collective-permute-start(s32[1,6]{1,0:T(1,128)} %param.14), channel_id=1, source_target_pairs={{0,0},{1,2},{2,1},{3,3},{4,4},{5,6},{6,5},{7,7},{8,8},{9,10},{10,9... | collective-permute-start | bytes 80 | tf_op jit(solution)/shard_map/ppermute | solution.py:253
  21.1 135.7 %collective-permute-start.4 = (bf16[1024,768]{0,1:T(8,128)(2,1)}, bf16[1024,768]{0,1:T(8,128)(2,1)}, u32[]{:S(2)}, u32[]{:S(2)}) collective-permute-start(bf16[1024,768]{0,1:T(8,128)(2,1)} %copy.165), channel_id=1, source_target_pairs={{0,0},{1,2},{2,1},{3,3},{4,4},{5,6},{6,5},{7,7},{8,8},{9,10},{10,9... | collective-permute-start | bytes 4718600 | tf_op jit(solution)/shard_map/ppermute | solution.py:255
  73.5 36.9 %collective-permute-start.1 = (bf16[2,12,64,1024]{3,2,1,0:T(8,128)(2,1)}, bf16[2,12,64,1024]{3,2,1,0:T(8,128)(2,1)}, u32[]{:S(2)}, u32[]{:S(2)}) collective-permute-start(bf16[2,12,64,1024]{3,2,1,0:T(8,128)(2,1)} %pad_maximum_fusion.1), channel_id=1, source_target_pairs={{0,2},{1,3},{2,0},{3,1},{4,6},{5,7},{6,4},{7,5},{8,10},{9,11},{10,... | collective-permute-start | bytes 9437192 | tf_op jit(solution)/shard_map/ppermute | solution.py:283
  114.5 19.4 %copy-start.71 = (bf16[768,768]{1,0:T(8,128)(2,1)S(1)}, bf16[768,768]{1,0:T(8,128)(2,1)}, u32[]{:S(2)}) copy-start(bf16[768,768]{1,0:T(8,128)(2,1)} %param.20) | copy-start | bytes 3538948
  137.5 43.9 %copy-start.3 = (f32[1024,768]{0,1:T(8,128)}, f32[1024,768]{0,1:T(8,128)S(1)}, u32[]{:S(2)}) copy-start(f32[1024,768]{0,1:T(8,128)S(1)} %get-tuple-element.181) | copy-start | bytes 9437188
  137.5 9.3 %slice-start.2 = ((s8[4718592]{0:T(1024)(128)(4,1)}), s8[524288]{0:T(1024)(128)(4,1)S(1)}, s32[]{:S(2)}) async-start(s8[4718592]{0:T(1024)(128)(4,1)} %bitcast.249), calls=%async_computation.2 | async-start | bytes 1048576
  138.3 8.6 %slice-start.3 = ((s8[4718592]{0:T(1024)(128)(4,1)}), s8[4194304]{0:T(1024)(128)(4,1)S(1)}, s32[]{:S(2)}) async-start(s8[4718592]{0:T(1024)(128)(4,1)} %bitcast.249), calls=%async_computation.3 | async-start | bytes 8388608
  172.5 8.8 %copy-start.76 = (bf16[1024,3072]{1,0:T(8,128)(2,1)S(1)}, bf16[1024,3072]{1,0:T(8,128)(2,1)}, u32[]{:S(2)}) copy-start(bf16[1024,3072]{1,0:T(8,128)(2,1)} %multiply_convert_fusion) | copy-start | bytes 18874372
  237.8 154.2 %collective-permute-start.3 = (bf16[1024,768]{0,1:T(8,128)(2,1)}, bf16[1024,768]{0,1:T(8,128)(2,1)}, u32[]{:S(2)}, u32[]{:S(2)}) collective-permute-start(bf16[1024,768]{0,1:T(8,128)(2,1)} %add_convert_fusion), channel_id=1, source_target_pairs={{0,0},{1,2},{2,1},{3,3},{4,4},{5,6},{6,5},{7,7},{8,8},{9,10},{10,9... | collective-permute-start | bytes 4718600 | tf_op jit(solution)/shard_map/ppermute | solution.py:305
  266.3 141.8 %collective-permute-start.28 = (bf16[2,2,2,2,96,768]{5,4,3,0,1,2:T(8,128)(2,1)}, bf16[2,2,2,2,96,768]{5,4,3,0,1,2:T(8,128)(2,1)}, u32[]{:S(2)}, u32[]{:S(2)}) collective-permute-start(bf16[2,2,2,2,96,768]{5,4,3,0,1,2:T(8,128)(2,1)} %bitcast.216), channel_id=1, source_target_pairs={{0,2},{1,3},{2,0},{3,1},{4,6},{5,7},{6,4},{7,5},{8,10},{9,11},{10,... | collective-permute-start | bytes 7077896 | tf_op jit(solution)/shard_map/ppermute | solution.py:218
  268.1 44.4 %collective-permute-start.18 = (bf16[2,2,2,2,24,768]{5,4,0,1,2,3:T(8,128)(2,1)}, bf16[2,2,2,2,24,768]{5,4,0,1,2,3:T(8,128)(2,1)}, u32[]{:S(2)}, u32[]{:S(2)}) collective-permute-start(bf16[2,2,2,2,24,768]{5,4,0,1,2,3:T(8,128)(2,1)} %bitcast.219), channel_id=1, source_target_pairs={{0,2},{1,3},{2,0},{3,1},{4,6},{5,7},{6,4},{7,5},{8,10},{9,11},{10,... | collective-permute-start | bytes 1769480 | tf_op jit(solution)/shard_map/ppermute | solution.py:218
  269.9 72.5 %collective-permute-start.6 = (bf16[2,6,64,1024]{3,2,1,0:T(8,128)(2,1)}, bf16[2,6,64,1024]{3,2,1,0:T(8,128)(2,1)}, u32[]{:S(2)}, u32[]{:S(2)}) collective-permute-start(bf16[2,6,64,1024]{3,2,1,0:T(8,128)(2,1)} %pad_maximum_fusion.3), channel_id=1, source_target_pairs={{0,2},{1,3},{2,0},{3,1},{4,6},{5,7},{6,4},{7,5},{8,10},{9,11},{10,... | collective-permute-start | bytes 4718600 | tf_op jit(solution)/shard_map/ppermute | solution.py:328
  271.2 73.4 %collective-permute-start.5 = (bf16[2,6,64,1024]{3,2,1,0:T(8,128)(2,1)}, bf16[2,6,64,1024]{3,2,1,0:T(8,128)(2,1)}, u32[]{:S(2)}, u32[]{:S(2)}) collective-permute-start(bf16[2,6,64,1024]{3,2,1,0:T(8,128)(2,1)} %pad_maximum_fusion.2), channel_id=1, source_target_pairs={{0,2},{1,3},{2,0},{3,1},{4,6},{5,7},{6,4},{7,5},{8,10},{9,11},{10,... | collective-permute-start | bytes 4718600 | tf_op jit(solution)/shard_map/ppermute | solution.py:328
  288.5 17.1 %copy-start.9 = (f32[12,64,1024]{2,1,0:T(8,128)S(1)}, f32[12,64,1024]{2,1,0:T(8,128)}, u32[]{:S(2)}) copy-start(f32[12,64,1024]{2,1,0:T(8,128)} %get-tuple-element.187) | copy-start | bytes 9437188
  288.5 17.2 %copy-start.19 = (f32[6,64,1024]{2,1,0:T(8,128)S(1)}, f32[6,64,1024]{2,1,0:T(8,128)}, u32[]{:S(2)}) copy-start(f32[6,64,1024]{2,1,0:T(8,128)} %get-tuple-element.41) | copy-start | bytes 4718596
  288.5 17.2 %copy-start.60 = (f32[6,64]{1,0:T(8,128)S(1)}, f32[6,64]{1,0:T(8,128)}, u32[]{:S(2)}) copy-start(f32[6,64]{1,0:T(8,128)} %mul.443) | copy-start | bytes 4612
  288.5 17.2 %copy-start.61 = (f32[6,64]{1,0:T(8,128)S(1)}, f32[6,64]{1,0:T(8,128)}, u32[]{:S(2)}) copy-start(f32[6,64]{1,0:T(8,128)} %mul.424) | copy-start | bytes 4612
  312.5 18.8 %copy-start.20 = (f32[6,64,1024]{2,1,0:T(8,128)S(1)}, f32[6,64,1024]{2,1,0:T(8,128)}, u32[]{:S(2)}) copy-start(f32[6,64,1024]{2,1,0:T(8,128)} %get-tuple-element.35) | copy-start | bytes 4718596
  312.5 18.8 %copy-start.50 = (f32[6,1024]{1,0:T(8,128)S(1)}, f32[6,1024]{1,0:T(8,128)}, u32[]{:S(2)}) copy-start(f32[6,1024]{1,0:T(8,128)} %get-tuple-element.168) | copy-start | bytes 73732
  312.5 18.8 %copy-start.51 = (f32[6,1024]{1,0:T(8,128)S(1)}, f32[6,1024]{1,0:T(8,128)}, u32[]{:S(2)}) copy-start(f32[6,1024]{1,0:T(8,128)} %get-tuple-element.169) | copy-start | bytes 73732
  313.9 10.0 %collective-permute-start.19 = (bf16[2,2,2,24,768]{4,3,0,1,2:T(8,128)(2,1)S(1)}, bf16[2,2,2,24,768]{4,3,0,1,2:T(8,128)(2,1)S(1)}, u32[]{:S(2)}, u32[]{:S(2)}) collective-permute-start(bf16[2,2,2,24,768]{4,3,0,1,2:T(8,128)(2,1)S(1)} %dynamic-slice_bitcast_fusion.9), channel_id=1, source_target_pairs={{0,1},{1,0},{2,3},{3,2},{4,5},{5,4},{6,7},{7,6},{8,9},{9,8},{10,11... | collective-permute-start | bytes 884744 | tf_op jit(solution)/shard_map/ppermute | solution.py:218
  324.0 5.8 %collective-permute-start.20 = (bf16[2,2,24,768]{3,2,0,1:T(8,128)(2,1)S(1)}, bf16[2,2,24,768]{3,2,0,1:T(8,128)(2,1)S(1)}, u32[]{:S(2)}, u32[]{:S(2)}) collective-permute-start(bf16[2,2,24,768]{3,2,0,1:T(8,128)(2,1)S(1)} %dynamic-slice_bitcast_fusion.14), channel_id=1, source_target_pairs={{0,4},{1,5},{2,6},{3,7},{4,0},{5,1},{6,2},{7,3},{8,12},{9,13},{10,... | collective-permute-start | bytes 442376 | tf_op jit(solution)/shard_map/ppermute | solution.py:218
  329.8 4.4 collective-permute-start.21
  334.9 5.9 %collective-permute-start.22 = (bf16[24,768]{1,0:T(8,128)(2,1)}, bf16[24,768]{1,0:T(8,128)(2,1)}, u32[]{:S(2)}, u32[]{:S(2)}) collective-permute-start(bf16[24,768]{1,0:T(8,128)(2,1)} %dynamic-slice_bitcast_fusion.20), channel_id=1, source_target_pairs={{0,16},{1,17},{2,18},{3,19},{4,20},{5,21},{6,22},{7,23},{8,24},{9,... | collective-permute-start | bytes 110600 | tf_op jit(solution)/shard_map/ppermute | solution.py:218
  340.8 73.2 %collective-permute-start.23 = (bf16[2,2,2,2,24,3072]{5,4,3,0,1,2:T(8,128)(2,1)}, bf16[2,2,2,2,24,3072]{5,4,3,0,1,2:T(8,128)(2,1)}, u32[]{:S(2)}, u32[]{:S(2)}) collective-permute-start(bf16[2,2,2,2,24,3072]{5,4,3,0,1,2:T(8,128)(2,1)} %bitcast.240), channel_id=1, source_target_pairs={{0,2},{1,3},{2,0},{3,1},{4,6},{5,7},{6,4},{7,5},{8,10},{9,11},{10,... | collective-permute-start | bytes 7077896 | tf_op jit(solution)/shard_map/ppermute | solution.py:218
  358.0 60.5 %collective-permute-start.13 = (bf16[2,2,2,2,24,1152]{5,4,0,1,3,2:T(8,128)(2,1)}, bf16[2,2,2,2,24,1152]{5,4,0,1,3,2:T(8,128)(2,1)}, u32[]{:S(2)}, u32[]{:S(2)}) collective-permute-start(bf16[2,2,2,2,24,1152]{5,4,0,1,3,2:T(8,128)(2,1)} %bitcast.218), channel_id=1, source_target_pairs={{0,2},{1,3},{2,0},{3,1},{4,6},{5,7},{6,4},{7,5},{8,10},{9,11},{10,... | collective-permute-start | bytes 2654216 | tf_op jit(solution)/shard_map/ppermute | solution.py:218
  387.2 34.2 %collective-permute-start.8 = (bf16[2,2,2,2,24,1280]{5,4,3,2,1,0:T(8,128)(2,1)}, bf16[2,2,2,2,24,1280]{5,4,3,2,1,0:T(8,128)(2,1)}, u32[]{:S(2)}, u32[]{:S(2)}) collective-permute-start(bf16[2,2,2,2,24,1280]{5,4,3,2,1,0:T(8,128)(2,1)} %dynamic-slice_bitcast_fusion.2), channel_id=1, source_target_pairs={{0,2},{1,3},{2,0},{3,1},{4,6},{5,7},{6,4},{7,5},{8,10},{9,11},{10,... | collective-permute-start | bytes 2949128 | tf_op jit(solution)/shard_map/ppermute | solution.py:218
  392.0 85.3 %collective-permute-start.7 = (bf16[1024,768]{0,1:T(8,128)(2,1)}, bf16[1024,768]{0,1:T(8,128)(2,1)}, u32[]{:S(2)}, u32[]{:S(2)}) collective-permute-start(bf16[1024,768]{0,1:T(8,128)(2,1)} %fusion.15), channel_id=1, source_target_pairs={{0,0},{1,2},{2,1},{3,3},{4,4},{5,6},{6,5},{7,7},{8,8},{9,10},{10,9... | collective-permute-start | bytes 4718600 | tf_op jit(solution)/shard_map/ppermute | solution.py:373
  412.5 87.7 %collective-permute-start.29 = (bf16[2,2,2,96,768]{4,3,2,0,1:T(8,128)(2,1)}, bf16[2,2,2,96,768]{4,3,2,0,1:T(8,128)(2,1)}, u32[]{:S(2)}, u32[]{:S(2)}) collective-permute-start(bf16[2,2,2,96,768]{4,3,2,0,1:T(8,128)(2,1)} %dynamic-slice_bitcast_fusion), channel_id=1, source_target_pairs={{0,4},{1,5},{2,6},{3,7},{4,0},{5,1},{6,2},{7,3},{8,12},{9,13},{10,... | collective-permute-start | bytes 3538952 | tf_op jit(solution)/shard_map/ppermute | solution.py:218
  417.9 84.5 %collective-permute-start.24 = (bf16[2,2,2,24,3072]{4,3,2,0,1:T(8,128)(2,1)}, bf16[2,2,2,24,3072]{4,3,2,0,1:T(8,128)(2,1)}, u32[]{:S(2)}, u32[]{:S(2)}) collective-permute-start(bf16[2,2,2,24,3072]{4,3,2,0,1:T(8,128)(2,1)} %dynamic-slice_bitcast_fusion.1), channel_id=1, source_target_pairs={{0,4},{1,5},{2,6},{3,7},{4,0},{5,1},{6,2},{7,3},{8,12},{9,13},{10,... | collective-permute-start | bytes 3538952 | tf_op jit(solution)/shard_map/ppermute | solution.py:218
  420.0 45.9 %collective-permute-start.14 = (bf16[2,2,2,24,1152]{4,3,0,1,2:T(8,128)(2,1)S(1)}, bf16[2,2,2,24,1152]{4,3,0,1,2:T(8,128)(2,1)S(1)}, u32[]{:S(2)}, u32[]{:S(2)}) collective-permute-start(bf16[2,2,2,24,1152]{4,3,0,1,2:T(8,128)(2,1)S(1)} %dynamic-slice_bitcast_fusion.6), channel_id=1, source_target_pairs={{0,4},{1,5},{2,6},{3,7},{4,0},{5,1},{6,2},{7,3},{8,12},{9,13},{10,... | collective-permute-start | bytes 1327112 | tf_op jit(solution)/shard_map/ppermute | solution.py:218
  422.9 43.2 %collective-permute-start.9 = (bf16[2,2,2,24,1280]{4,3,2,1,0:T(8,128)(2,1)S(1)}, bf16[2,2,2,24,1280]{4,3,2,1,0:T(8,128)(2,1)S(1)}, u32[]{:S(2)}, u32[]{:S(2)}) collective-permute-start(bf16[2,2,2,24,1280]{4,3,2,1,0:T(8,128)(2,1)S(1)} %dynamic-slice_bitcast_fusion.5), channel_id=1, source_target_pairs={{0,1},{1,0},{2,3},{3,2},{4,5},{5,4},{6,7},{7,6},{8,9},{9,8},{10,11... | collective-permute-start | bytes 1474568 | tf_op jit(solution)/shard_map/ppermute | solution.py:218
  466.0 6.6 %collective-permute-start.15 = (bf16[2,2,24,1152]{3,2,0,1:T(8,128)(2,1)S(1)}, bf16[2,2,24,1152]{3,2,0,1:T(8,128)(2,1)S(1)}, u32[]{:S(2)}, u32[]{:S(2)}) collective-permute-start(bf16[2,2,24,1152]{3,2,0,1:T(8,128)(2,1)S(1)} %dynamic-slice_bitcast_fusion.11), channel_id=1, source_target_pairs={{0,1},{1,0},{2,3},{3,2},{4,5},{5,4},{6,7},{7,6},{8,9},{9,8},{10,11... | collective-permute-start | bytes 663560 | tf_op jit(solution)/shard_map/ppermute | solution.py:218
  466.3 8.8 %copy-start.25 = (bf16[2,2,2,24,1280]{4,3,2,1,0:T(8,128)(2,1)}, bf16[2,2,2,24,1280]{4,3,2,1,0:T(8,128)(2,1)S(1)}, u32[]{:S(2)}) copy-start(bf16[2,2,2,24,1280]{4,3,2,1,0:T(8,128)(2,1)S(1)} %fusion.32) | copy-start | bytes 1474564
  473.5 6.3 %collective-permute-start.16 = (bf16[2,24,1152]{2,1,0:T(8,128)(2,1)}, bf16[2,24,1152]{2,1,0:T(8,128)(2,1)}, u32[]{:S(2)}, u32[]{:S(2)}) collective-permute-start(bf16[2,24,1152]{2,1,0:T(8,128)(2,1)} %dynamic-slice_bitcast_fusion.16), channel_id=1, source_target_pairs={{0,8},{1,9},{2,10},{3,11},{4,12},{5,13},{6,14},{7,15},{8,0},{9,1},... | collective-permute-start | bytes 331784 | tf_op jit(solution)/shard_map/ppermute | solution.py:218
  475.8 7.3 %collective-permute-start.10 = (bf16[2,2,24,1280]{3,2,1,0:T(8,128)(2,1)}, bf16[2,2,24,1280]{3,2,1,0:T(8,128)(2,1)}, u32[]{:S(2)}, u32[]{:S(2)}) collective-permute-start(bf16[2,2,24,1280]{3,2,1,0:T(8,128)(2,1)} %dynamic-slice_bitcast_fusion.10), channel_id=1, source_target_pairs={{0,4},{1,5},{2,6},{3,7},{4,0},{5,1},{6,2},{7,3},{8,12},{9,13},{10,... | collective-permute-start | bytes 737288 | tf_op jit(solution)/shard_map/ppermute | solution.py:218
  484.2 4.9 collective-permute-start.11
  484.7 7.7 %collective-permute-start.17 = (bf16[24,1152]{1,0:T(8,128)(2,1)S(1)}, bf16[24,1152]{1,0:T(8,128)(2,1)S(1)}, u32[]{:S(2)}, u32[]{:S(2)}) collective-permute-start(bf16[24,1152]{1,0:T(8,128)(2,1)S(1)} %dynamic-slice_bitcast_fusion.19), channel_id=1, source_target_pairs={{0,16},{1,17},{2,18},{3,19},{4,20},{5,21},{6,22},{7,23},{8,24},{9,... | collective-permute-start | bytes 165896 | tf_op jit(solution)/shard_map/ppermute | solution.py:218
  490.4 6.0 %collective-permute-start.12 = (bf16[24,1280]{1,0:T(8,128)(2,1)}, bf16[24,1280]{1,0:T(8,128)(2,1)}, u32[]{:S(2)}, u32[]{:S(2)}) collective-permute-start(bf16[24,1280]{1,0:T(8,128)(2,1)} %dynamic-slice_bitcast_fusion.18), channel_id=1, source_target_pairs={{0,16},{1,17},{2,18},{3,19},{4,20},{5,21},{6,22},{7,23},{8,24},{9,... | collective-permute-start | bytes 184328 | tf_op jit(solution)/shard_map/ppermute | solution.py:218
  502.3 19.5 %collective-permute-start.30 = (bf16[2,2,96,768]{3,2,1,0:T(8,128)(2,1)S(1)}, bf16[2,2,96,768]{3,2,1,0:T(8,128)(2,1)S(1)}, u32[]{:S(2)}, u32[]{:S(2)}) collective-permute-start(bf16[2,2,96,768]{3,2,1,0:T(8,128)(2,1)S(1)} %dynamic-slice_bitcast_fusion.3), channel_id=1, source_target_pairs={{0,8},{1,9},{2,10},{3,11},{4,12},{5,13},{6,14},{7,15},{8,0},{9,1},... | collective-permute-start | bytes 1769480 | tf_op jit(solution)/shard_map/ppermute | solution.py:218
  504.3 27.9 %collective-permute-start.25 = (bf16[2,2,24,3072]{3,2,1,0:T(8,128)(2,1)S(1)}, bf16[2,2,24,3072]{3,2,1,0:T(8,128)(2,1)S(1)}, u32[]{:S(2)}, u32[]{:S(2)}) collective-permute-start(bf16[2,2,24,3072]{3,2,1,0:T(8,128)(2,1)S(1)} %dynamic-slice_bitcast_fusion.4), channel_id=1, source_target_pairs={{0,8},{1,9},{2,10},{3,11},{4,12},{5,13},{6,14},{7,15},{8,0},{9,1},... | collective-permute-start | bytes 1769480 | tf_op jit(solution)/shard_map/ppermute | solution.py:218
  522.0 20.2 %collective-permute-start.31 = (bf16[2,96,768]{2,1,0:T(8,128)(2,1)S(1)}, bf16[2,96,768]{2,1,0:T(8,128)(2,1)S(1)}, u32[]{:S(2)}, u32[]{:S(2)}) collective-permute-start(bf16[2,96,768]{2,1,0:T(8,128)(2,1)S(1)} %dynamic-slice_bitcast_fusion.7), channel_id=1, source_target_pairs={{0,16},{1,17},{2,18},{3,19},{4,20},{5,21},{6,22},{7,23},{8,24},{9,... | collective-permute-start | bytes 884744 | tf_op jit(solution)/shard_map/ppermute | solution.py:218
  532.4 13.9 %collective-permute-start.26 = (bf16[2,24,3072]{2,1,0:T(8,128)(2,1)S(1)}, bf16[2,24,3072]{2,1,0:T(8,128)(2,1)S(1)}, u32[]{:S(2)}, u32[]{:S(2)}) collective-permute-start(bf16[2,24,3072]{2,1,0:T(8,128)(2,1)S(1)} %dynamic-slice_bitcast_fusion.8), channel_id=1, source_target_pairs={{0,16},{1,17},{2,18},{3,19},{4,20},{5,21},{6,22},{7,23},{8,24},{9,... | collective-permute-start | bytes 884744 | tf_op jit(solution)/shard_map/ppermute | solution.py:218
  542.3 7.3 %collective-permute-start.32 = (bf16[96,768]{1,0:T(8,128)(2,1)S(1)}, bf16[96,768]{1,0:T(8,128)(2,1)S(1)}, u32[]{:S(2)}, u32[]{:S(2)}) collective-permute-start(bf16[96,768]{1,0:T(8,128)(2,1)S(1)} %dynamic-slice_bitcast_fusion.12), channel_id=1, source_target_pairs={{0,1},{1,0},{2,3},{3,2},{4,5},{5,4},{6,7},{7,6},{8,9},{9,8},{10,11... | collective-permute-start | bytes 442376 | tf_op jit(solution)/shard_map/ppermute | solution.py:218
  546.4 6.4 %collective-permute-start.27 = (bf16[24,3072]{1,0:T(8,128)(2,1)S(1)}, bf16[24,3072]{1,0:T(8,128)(2,1)S(1)}, u32[]{:S(2)}, u32[]{:S(2)}) collective-permute-start(bf16[24,3072]{1,0:T(8,128)(2,1)S(1)} %dynamic-slice_bitcast_fusion.13), channel_id=1, source_target_pairs={{0,1},{1,0},{2,3},{3,2},{4,5},{5,4},{6,7},{7,6},{8,9},{9,8},{10,11... | collective-permute-start | bytes 442376 | tf_op jit(solution)/shard_map/ppermute | solution.py:218
  (66 other events, 218.2 us)

commit v2 on v1

v2 whole, which is shorter than its diff:
```python
import functools
import math

import jax
import jax.numpy as jnp
from jax import lax
from jax.experimental import pallas as pl
from jax.experimental.pallas import tpu as pltpu
from jax.sharding import PartitionSpec as P

H = 12
HD = 64
EPS = 1e-06
AXES = ("wide", "blk")
AUG = 16
BLOCKED = -512.0
LOG2E = math.log2(math.e)
NN = (((1,), (0,)), ((), ()))
NT = (((1,), (1,)), ((), ()))
TN = (((0,), (0,)), ((), ()))
TT = (((0,), (1,)), ((), ()))
BF16 = jnp.bfloat16
MESH = pl.DeviceIdType.MESH
F32 = jnp.float32
VMEM_LIMIT = 56 * 2**20


def mul(left, right, dims, kind=F32):
    return lax.dot_general(left, right, dims, preferred_element_type=F32).astype(kind)


def forward_kernel(bk, first, *refs):
    if first:
        q_ref, k_ref, v_ref, mq_ref, mk_ref, ones_ref, acc_ref, e_ref = refs
    else:
        q_ref, k_ref, v_ref, mq_ref, mk_ref, ones_ref, had_ref, e_ref, o_ref, linv_ref = refs
    keys = k_ref.shape[2]
    q = jnp.concatenate([q_ref[0], mq_ref[...]], axis=0)
    acc = None if first else had_ref[0]
    for i in range(keys // bk):
        cut = slice(i * bk, (i + 1) * bk)
        k = jnp.concatenate([k_ref[0, :, cut], mk_ref[:, cut]], axis=0)
        v = jnp.concatenate([v_ref[0, :, cut], ones_ref[:, cut]], axis=0)
        e = jnp.exp2(mul(k, q, TN)).astype(BF16)
        e_ref[0, cut, :] = e
        part = mul(v, e, NN)
        acc = part if acc is None else acc + part
    if first:
        acc_ref[0] = acc
    else:
        linv = 1.0 / acc[HD : HD + 1]
        o_ref[0] = (acc[:HD] * linv).astype(BF16)
        linv_ref[0] = jnp.broadcast_to(linv, linv_ref.shape[1:])


def head_block(*tail):
    return pl.BlockSpec((1,) + tail, lambda h: (h,) + (0,) * len(tail))


def whole_block(shape):
    return pl.BlockSpec(shape, lambda h: (0,) * len(shape))


def key_block(keys):
    return math.gcd(keys, 512)


def attend(q, k, v, mask_q, mask_k, ones, had=None):
    heads, _, rows = q.shape
    keys = k.shape[2]
    first = had is None
    ins = [q, k, v, mask_q, mask_k, ones]
    specs = [head_block(HD, rows), head_block(HD, keys), head_block(HD, keys)]
    specs += [whole_block(a.shape) for a in (mask_q, mask_k, ones)]
    e_shape = jax.ShapeDtypeStruct((heads, keys, rows), BF16)
    e_spec = head_block(keys, rows)
    if first:
        outs = [jax.ShapeDtypeStruct((heads, HD + AUG, rows), F32), e_shape]
        out_specs = [head_block(HD + AUG, rows), e_spec]
    else:
        ins.append(had)
        specs.append(head_block(HD + AUG, rows))
        outs = [
            e_shape,
            jax.ShapeDtypeStruct((heads, HD, rows), BF16),
            jax.ShapeDtypeStruct((heads, 8, rows), F32),
        ]
        out_specs = [e_spec, head_block(HD, rows), head_block(8, rows)]
    return pl.pallas_call(
        functools.partial(forward_kernel, key_block(keys), first),
        grid=(heads,),
        in_specs=specs,
        out_specs=out_specs,
        out_shape=outs,
        compiler_params=pltpu.CompilerParams(vmem_limit_bytes=VMEM_LIMIT),
        cost_estimate=pl.CostEstimate(
            flops=heads * rows * keys * 1024,
            bytes_accessed=heads * rows * keys * 2,
            transcendentals=heads * rows * keys,
        ),
        name="attend_first" if first else "attend_last",
    )(*ins)


def backward_kernel(bk, first, *refs):
    if first:
        e_ref, do_ref, o_ref, linv_ref, q_ref, k_ref, v_ref, ones_ref, dq_ref, dk_ref, dv_ref = refs
    else:
        e_ref, do_ref, o_ref, linv_ref, q_ref, k_ref, v_ref, ones_ref, had_ref, dq_ref, dk_ref, dv_ref = refs
    keys = k_ref.shape[2]
    low = (do_ref[0] * linv_ref[0, :1]).astype(BF16)
    delta = -jnp.sum(low.astype(F32) * o_ref[0].astype(F32), axis=0, keepdims=True)
    top = delta.astype(BF16).astype(F32)
    row = lax.broadcasted_iota(jnp.int32, (AUG, delta.shape[1]), 0)
    extra = jnp.where(row == 0, top, jnp.where(row == 1, delta - top, 0.0)).astype(BF16)
    do = jnp.concatenate([low, extra], axis=0)
    q = q_ref[0]
    acc = None if first else had_ref[0]
    for i in range(keys // bk):
        cut = slice(i * bk, (i + 1) * bk)
        k = k_ref[0, :, cut]
        v = jnp.concatenate([v_ref[0, :, cut], ones_ref[:, cut]], axis=0)
        e = e_ref[0, cut, :]
        ds = (e.astype(F32) * mul(v, do, TN)).astype(BF16)
        part = mul(k, ds, NN)
        acc = part if acc is None else acc + part
        dk_ref[0, :, cut] = mul(q, ds, NT).astype(dk_ref.dtype)
        dv_ref[0, :, cut] = mul(low, e, NT).astype(dv_ref.dtype)
    dq_ref[0] = acc


def attend_back(e, do, o, linv, q, k, v, ones, start, heads, kind, had=None):
    _, keys, rows = e.shape
    first = had is None

    def block(*tail):
        return pl.BlockSpec((1,) + tail, lambda h: (h + start,) + (0,) * len(tail))

    ins = [e, do, o, linv, q, k, v, ones]
    specs = [block(keys, rows), block(HD, rows), block(HD, rows), block(8, rows), block(HD, rows)]
    specs += [block(HD, keys), block(HD, keys), whole_block(ones.shape)]
    if not first:
        ins.append(had)
        specs.append(head_block(HD, rows))
    return pl.pallas_call(
        functools.partial(backward_kernel, key_block(keys), first),
        grid=(heads,),
        in_specs=specs,
        out_specs=[head_block(HD, rows), head_block(HD, keys), head_block(HD, keys)],
        out_shape=[
            jax.ShapeDtypeStruct((heads, HD, rows), F32),
            jax.ShapeDtypeStruct((heads, HD, keys), kind),
            jax.ShapeDtypeStruct((heads, HD, keys), kind),
        ],
        compiler_params=pltpu.CompilerParams(vmem_limit_bytes=VMEM_LIMIT),
        cost_estimate=pl.CostEstimate(
            flops=heads * rows * keys * 2300,
            bytes_accessed=heads * rows * keys * 2,
            transcendentals=0,
        ),
        name="attend_back_first" if first else "attend_back_last",
    )(*ins)


def norm(value, axis):
    mean = jnp.mean(value, axis=axis, keepdims=True)
    centred = value - mean
    scale = lax.rsqrt(jnp.mean(centred * centred, axis=axis, keepdims=True) + EPS)
    return centred * scale, scale


def norm_back(grad, unit, scale, axis):
    mean = jnp.mean(grad, axis=axis, keepdims=True)
    along = jnp.mean(grad * unit, axis=axis, keepdims=True)
    return scale * (grad - mean - unit * along)


def gelu_parts(u):
    root = math.sqrt(2.0 / math.pi)
    square = u * u
    t = jnp.tanh(u * (root + (root * 0.044715) * square))
    half = 0.5 + 0.5 * t
    slope = half + (u * (0.5 - 0.5 * t * t)) * (root + (3 * root * 0.044715) * square)
    return u * half, slope


def params(**more):
    return pltpu.CompilerParams(vmem_limit_bytes=VMEM_LIMIT, **more)


def fixed(shape):
    return pl.BlockSpec(shape, lambda *_: (0,) * len(shape))


SCALAR = pl.BlockSpec(memory_space=pltpu.SMEM)


def pre_kernel(swapped, *refs):
    if swapped:
        flag_ref, here_ref, came_ref, *refs = refs
        x_low = jnp.where(flag_ref[0] == 1, came_ref[...], here_ref[...])
        *refs, x_ref = refs
        x_ref[...] = x_low
    else:
        here_ref, *refs = refs
        x_low = here_ref[...]
    gain_ref, bias_ref, w_ref, gq_ref, gk_ref, h_ref, q_ref, k_ref, v_ref, scale_ref = refs
    rows, width = x_low.shape
    unit, _ = norm(x_low.astype(F32), -1)
    h = (unit * gain_ref[...] + bias_ref[...]).astype(BF16)
    h_ref[...] = h.T

    def heads(part):
        value = mul(w_ref[part * width : (part + 1) * width, :], h, NT)
        return value.reshape(width // HD, HD, rows)

    unit_k, scale_k = norm(heads(1), 1)
    k_ref[...] = (unit_k * gk_ref[...]).astype(BF16)
    scale_ref[1] = scale_k
    v_ref[...] = heads(2).astype(BF16)
    unit_q, scale_q = norm(heads(0), 1)
    q_ref[...] = (unit_q * gq_ref[...]).astype(BF16)
    scale_ref[0] = scale_q


def project(tokens, gain, bias, w_t, gain_q, gain_k, flag=None, came=None):
    rows, width = tokens.shape
    block = math.gcd(rows, 256)
    row = pl.BlockSpec((block, width), lambda i: (i, 0))
    head = pl.BlockSpec((H, HD, block), lambda i: (0, 0, i))
    swapped = flag is not None
    ins = ([flag, tokens, came] if swapped else [tokens]) + [gain, bias, w_t, gain_q, gain_k]
    specs = ([SCALAR, row, row] if swapped else [row]) + [fixed(a.shape) for a in ins[-5:]]
    head_shape = jax.ShapeDtypeStruct((H, HD, rows), BF16)
    outs = [jax.ShapeDtypeStruct((width, rows), BF16), head_shape, head_shape, head_shape]
    outs.append(jax.ShapeDtypeStruct((2, H, 1, rows), F32))
    out_specs = [pl.BlockSpec((width, block), lambda i: (0, i)), head, head, head]
    out_specs.append(pl.BlockSpec((2, H, 1, block), lambda i: (0, 0, 0, i)))
    if swapped:
        outs.append(jax.ShapeDtypeStruct((rows, width), BF16))
        out_specs.append(row)
    return pl.pallas_call(
        functools.partial(pre_kernel, swapped),
        grid=(rows // block,),
        in_specs=specs,
        out_specs=out_specs,
        out_shape=outs,
        compiler_params=params(),
        cost_estimate=pl.CostEstimate(
            flops=2 * rows * w_t.size, bytes_accessed=12 * rows * width, transcendentals=0
        ),
        name="project",
    )(*ins)


def fold(value):
    if value.shape[-2] % 16 == 0:
        return value
    half = value.shape[-1] // 2
    low = value[..., 16:, :]
    low = jnp.concatenate([low[..., :half], low[..., half:]], axis=-2)
    return jnp.concatenate([value[..., :16, :], low], axis=-1)


def unfold(out_ref, value, start=0):
    count = value.shape[-1] * 2 // 3
    half = count // 2
    out_ref[:16, start : start + count] = value[:, :count]
    out_ref[16:, start : start + half] = value[:8, count:]
    out_ref[16:, start + half : start + count] = value[8:, count:]


def spread(value, core, keep_ref, give_ref, lead):
    rows, columns = value.shape
    value = value.reshape((lead, 2, 2, rows // (4 * lead), columns))
    mine = core == 0
    shape = keep_ref.shape
    keep = jnp.where(mine, value[:, 0], value[:, 1])
    give = jnp.where(mine, value[:, 1], value[:, 0])
    keep_ref[...] = fold(keep).astype(BF16).reshape(shape)
    give_ref[...] = fold(give).astype(BF16).reshape(shape)


def middle_kernel(split, *refs):
    if split:
        core_ref, *refs = refs
        core = core_ref[0]
    x_ref, o_ref, dy_ref, w_out_ref, gain_ref, bias_ref, w_up_ref, w_down_ref, *refs = refs
    out_ref, dx1_ref, do_ref, dgain_ref, dbias_ref, *refs = refs
    grads, refs = (refs[:6], refs[6:]) if split else (refs[:3], refs[3:])
    x1_ref, h2_ref, h2t_ref, acc_ref, dh2_ref, g_ref, du_ref, da_ref = refs
    step = pl.program_id(0)
    rows = x_ref.shape[0]
    block = math.gcd(rows, 256)
    cuts = [slice(i, i + block) for i in range(0, rows, block)]

    def leave(value, which, lead):
        if split:
            spread(value, core, grads[2 * which], grads[2 * which + 1], lead)
        else:
            grads[which][...] = value

    @pl.when(step == 0)
    def _():
        for cut in cuts:
            x1 = x_ref[cut, :].astype(F32) + mul(o_ref[:, cut], w_out_ref[...], TN)
            x1_ref[cut, :] = x1
            acc_ref[cut, :] = x1
            h2 = (norm(x1, -1)[0] * gain_ref[...] + bias_ref[...]).astype(BF16)
            h2_ref[cut, :] = h2
            h2t_ref[:, cut] = h2.T

    for cut in cuts:
        dy = dy_ref[cut, :]
        value, slope = gelu_parts(mul(h2_ref[cut, :], w_up_ref[...], NN))
        g = value.astype(BF16)
        g_ref[cut, :] = g
        acc_ref[cut, :] += mul(g, w_down_ref[...], NN)
        du = (mul(dy, w_down_ref[...], NT) * slope).astype(BF16)
        du_ref[cut, :] = du
        part = mul(du, w_up_ref[...], NT)
        dh2_ref[cut, :] = jnp.where(step == 0, part, dh2_ref[cut, :] + part)
    leave(mul(h2t_ref[...], du_ref[...], NN), 0, 8)
    leave(mul(g_ref[...], dy_ref[...], TN), 1, 2)

    @pl.when(step == pl.num_programs(0) - 1)
    def _():
        dgain, dbias = 0.0, 0.0
        for cut in cuts:
            out_ref[cut, :] = acc_ref[cut, :].astype(BF16)
            unit, scale = norm(x1_ref[cut, :], -1)
            dh2 = dh2_ref[cut, :]
            dgain += jnp.sum(dh2 * unit, axis=0, keepdims=True)
            dbias += jnp.sum(dh2, axis=0, keepdims=True)
            dx1 = dy_ref[cut, :].astype(F32) + norm_back(dh2 * gain_ref[...], unit, scale, -1)
            dx1_ref[cut, :] = dx1
            da = dx1.astype(BF16)
            da_ref[cut, :] = da
            do_ref[:, cut] = mul(w_out_ref[...], da, NT)
        dgain_ref[...] = dgain
        dbias_ref[...] = dbias
        leave(mul(o_ref[...], da_ref[...], NN), 2, 8)


def middle(x, o, dy, w_out, gain, bias, w_up, w_down, core=None):
    rows, width = x.shape
    inner = w_up.shape[1]
    steps = 4
    chunk = inner // steps
    split = core is not None
    ins = ([core] if split else []) + [x, o, dy, w_out, gain, bias, w_up, w_down]
    specs = [SCALAR] if split else []
    specs += [fixed(a.shape) for a in ins[-8:-2]]
    specs += [pl.BlockSpec((width, chunk), lambda f: (0, f)), pl.BlockSpec((chunk, width), lambda f: (f, 0))]
    outs = [
        jax.ShapeDtypeStruct((rows, width), BF16),
        jax.ShapeDtypeStruct((rows, width), F32),
        jax.ShapeDtypeStruct((width, rows), F32),
        jax.ShapeDtypeStruct((1, width), F32),
        jax.ShapeDtypeStruct((1, width), F32),
    ]
    out_specs = [fixed(a.shape) for a in outs]
    if split:
        up = jax.ShapeDtypeStruct((4, 2, 2, 16, inner * 3 // 2), BF16)
        down = jax.ShapeDtypeStruct((4, 2, 2, inner // 32, width), BF16)
        out = jax.ShapeDtypeStruct((4, 2, 2, 16, width * 3 // 2), BF16)
        outs += [up, up, down, down, out, out]
        up_spec = pl.BlockSpec((4, 2, 2, 16, chunk * 3 // 2), lambda f: (0, 0, 0, 0, f))
        down_spec = pl.BlockSpec((1, 2, 2, inner // 32, width), lambda f: (f, 0, 0, 0, 0))
        out_specs += [up_spec, up_spec, down_spec, down_spec, fixed(out.shape), fixed(out.shape)]
    else:
        outs += [jax.ShapeDtypeStruct(a.shape, F32) for a in (w_up, w_down, w_out)]
        out_specs += [*specs[-2:], fixed(w_out.shape)]
    return pl.pallas_call(
        functools.partial(middle_kernel, split),
        grid=(steps,),
        in_specs=specs,
        out_specs=out_specs,
        out_shape=outs,
        scratch_shapes=[
            pltpu.VMEM((rows, width), F32),
            pltpu.VMEM((rows, width), BF16),
            pltpu.VMEM((width, rows), BF16),
            pltpu.VMEM((rows, width), F32),
            pltpu.VMEM((rows, width), F32),
            pltpu.VMEM((rows, chunk), BF16),
            pltpu.VMEM((rows, chunk), BF16),
            pltpu.VMEM((rows, width), BF16),
        ],
        compiler_params=params(),
        cost_estimate=pl.CostEstimate(
            flops=6 * rows * (2 * w_up.size + w_out.size),
            bytes_accessed=40 * rows * width,
            transcendentals=rows * inner,
        ),
        name="middle",
    )(*ins)


def head_backs(d_q, d_k, d_v, q, k, inv_q, inv_k, gain_q, gain_k, scale_q, scale_k):
    d_q = d_q * (1.0 / math.sqrt(HD))
    d_k = d_k * (1.0 / LOG2E)
    unit_q = q.astype(F32) * inv_q
    unit_k = k.astype(F32) * inv_k
    sum_q = jnp.sum(d_q * unit_q, axis=2, keepdims=True)
    sum_k = jnp.sum(d_k * unit_k, axis=2, keepdims=True)
    d_q = norm_back(d_q * gain_q, unit_q, scale_q, 1).astype(BF16)
    d_k = norm_back(d_k * gain_k, unit_k, scale_k, 1).astype(BF16)
    return jnp.stack([d_q, d_k, d_v.astype(BF16)]), sum_q, sum_k


def post_kernel(*refs):
    *ins, scale_ref, h_ref, d_ref, sum_q_ref, sum_k_ref, grad_ref = refs
    values = [ref[...] for ref in ins]
    d, sum_q_ref[...], sum_k_ref[...] = head_backs(*values, scale_ref[0], scale_ref[1])
    d_ref[...] = d
    grad_ref[...] = mul(h_ref[...], d.reshape(-1, d.shape[-1]), NT)


def post(d_q, d_k, d_v, q, k, inv_q, inv_k, gain_q, gain_k, scales, h_t):
    heads, _, rows = d_q.shape
    width = h_t.shape[0]
    some = 4
    here = pl.BlockSpec((some, HD, rows), lambda i: (i, 0, 0))
    gain = pl.BlockSpec((some, HD, 1), lambda i: (i, 0, 0))
    columns = 3 * some * HD
    return pl.pallas_call(
        post_kernel,
        grid=(heads // some,),
        in_specs=[here] * 5
        + [gain] * 4
        + [pl.BlockSpec((2, some, 1, rows), lambda i: (0, i, 0, 0)), fixed(h_t.shape)],
        out_specs=[
            pl.BlockSpec((3, some, HD, rows), lambda i: (0, i, 0, 0)),
            gain,
            gain,
            pl.BlockSpec((width, columns), lambda i: (0, i)),
        ],
        out_shape=[
            jax.ShapeDtypeStruct((3, heads, HD, rows), BF16),
            jax.ShapeDtypeStruct((heads, HD, 1), F32),
            jax.ShapeDtypeStruct((heads, HD, 1), F32),
            jax.ShapeDtypeStruct((width, 3 * heads * HD), F32),
        ],
        compiler_params=params(),
        cost_estimate=pl.CostEstimate(
            flops=6 * rows * width * heads * HD,
            bytes_accessed=30 * rows * heads * HD,
            transcendentals=0,
        ),
        name="post",
    )(d_q, d_k, d_v, q, k, inv_q, inv_k, gain_q, gain_k, scales, h_t)


def token_grads(d, w, x, dx1, gain):
    d_h = mul(w, d.reshape(-1, d.shape[-1]), NN).T
    unit, scale = norm(x.astype(F32), -1)
    d_x = dx1 + norm_back(d_h * gain, unit, scale, -1)
    dgain = jnp.sum(d_h * unit, axis=0, keepdims=True)
    dbias = jnp.sum(d_h, axis=0, keepdims=True)
    return d_x.astype(BF16), dgain, dbias


def last_kernel(d_ref, w_ref, x_ref, dx1_ref, gain_ref, out_ref, dgain_ref, dbias_ref):
    out_ref[...], dgain, dbias = token_grads(
        d_ref[...], w_ref[...], x_ref[...], dx1_ref[...], gain_ref[...]
    )
    first = pl.program_id(0) == 0
    dgain_ref[...] = jnp.where(first, dgain, dgain_ref[...] + dgain)
    dbias_ref[...] = jnp.where(first, dbias, dbias_ref[...] + dbias)


def last(d, w, x, dx1, gain):
    rows, width = x.shape
    block = math.gcd(rows, 256)
    row = pl.BlockSpec((block, width), lambda i: (i, 0))
    return pl.pallas_call(
        last_kernel,
        grid=(rows // block,),
        in_specs=[
            pl.BlockSpec(d.shape[:3] + (block,), lambda i: (0, 0, 0, i)),
            fixed(w.shape),
            row,
            row,
            fixed(gain.shape),
        ],
        out_specs=[row, fixed((1, width)), fixed((1, width))],
        out_shape=[
            jax.ShapeDtypeStruct((rows, width), BF16),
            jax.ShapeDtypeStruct((1, width), F32),
            jax.ShapeDtypeStruct((1, width), F32),
        ],
        compiler_params=params(),
        name="last",
    )(d, w, x, dx1, gain)


class Here:
    def __init__(self):
        wide, self.y = lax.axis_index("wide"), lax.axis_index("blk")
        self.core, self.x, self.z = wide % 2, wide // 2 % 2, wide // 4

    def device(self, z=None, x=None, core=None, y=None):
        z = self.z if z is None else z
        x = self.x if x is None else x
        core = self.core if core is None else core
        return (z * 4 + x * 2 + core, self.y if y is None else y)

    def other_core(self):
        return self.device(core=1 - self.core)

    def plane(self, k):
        x = 1 - self.x if k % 2 else self.x
        y = 1 - self.y if k // 2 else self.y
        return x, y

    def column(self, k):
        z = self.z
        return (z, z + 1 - 2 * (z % 2), (z + 2) % 4, 3 - z)[k]

    def partner(self, kind, k):
        if kind == "column":
            return self.device(z=self.column(k))
        x, y = self.plane(k)
        return self.device(x=x, y=y)

    def partners(self):
        every = [self.partner(kind, k) for kind in ("plane", "column") for k in (1, 2, 3)]
        return [self.other_core()] + every

    def part(self, ref, kind, k):
        if kind == "column":
            return ref.at[self.column(k)]
        x, y = self.plane(k)
        return ref.at[:, x, y] if len(ref.shape) == 5 else ref.at[x, y]


def greet(others):
    barrier = pltpu.get_barrier_semaphore()
    for other in others:
        pl.semaphore_signal(barrier, inc=1, device_id=other, device_id_type=MESH)
    pl.semaphore_wait(barrier, len(others))


def remote(source, target, sems, at, to):
    return pltpu.make_async_remote_copy(
        src_ref=source,
        dst_ref=target,
        send_sem=sems[0].at[at],
        recv_sem=sems[1].at[at],
        device_id=to,
        device_id_type=MESH,
    )


class Sum:
    def __init__(self, here, first, give, keep, refs, sems):
        self.here, self.give, self.keep = here, give, keep
        self.kinds = ("plane", "column") if first == "plane" else ("column", "plane")
        self.came0, self.whole, self.came1, self.some, self.came2 = refs
        self.sems = sems

    def copies(self, stage):
        here = self.here
        if stage == 0:
            return [remote(self.give, self.came0, self.sems, 0, here.other_core())]
        kind = self.kinds[stage - 1]
        source, target = ((self.whole, self.came1), (self.some, self.came2))[stage - 1]
        return [
            remote(
                here.part(source, kind, k),
                target.at[k - 1],
                self.sems,
                3 * stage - 3 + k,
                here.partner(kind, k),
            )
            for k in (1, 2, 3)
        ]

    def start(self, stage):
        for copy in self.copies(stage):
            copy.start()

    def wait(self, stage):
        for copy in self.copies(stage):
            copy.wait()

    def add_first(self):
        def body(i, _):
            total = self.keep[i].astype(F32) + self.came0[i].astype(F32)
            self.whole[i] = total.astype(self.whole.dtype)
            return 0

        self.wait(0)
        lax.fori_loop(0, 4, body, 0)
        self.start(1)

    def add_second(self):
        own = self.here.part(self.whole, self.kinds[0], 0)

        def body(i, _):
            total = own[i].astype(F32)
            for k in range(3):
                total += self.came1[k, i].astype(F32)
            self.some[i] = total.astype(self.some.dtype)
            return 0

        self.wait(1)
        lax.fori_loop(0, self.some.shape[0], body, 0)
        self.start(2)

    def add_third(self):
        self.wait(2)
        total = self.here.part(self.some, self.kinds[1], 0)[...].astype(F32)
        for k in range(3):
            total += self.came2[k].astype(F32)
        return total


def sum_scratch(first, tail, kind=BF16, in_place=True):
    lead = (4,) if first == "plane" else (2, 2)
    shapes = [(4, 2, 2), (4, 2, 2), (3,) + lead, lead, (3,)]
    return [pltpu.VMEM(shape + tail, kind) for shape in shapes] + [
        pltpu.SemaphoreType.DMA((7,)),
        pltpu.SemaphoreType.DMA((7,)),
    ]


BATCH = 4


def head_back(here, h, ins, far_out, far_in, far_sems, kept):
    e_far, e_near, do_ref, o_ref, linv_ref, q_ref, k_ref, k_far, v_far, v_near, ones_ref = ins
    low = (do_ref[0] * linv_ref[0, :1]).astype(BF16)
    delta = -jnp.sum(low.astype(F32) * o_ref[0].astype(F32), axis=0, keepdims=True)
    top = delta.astype(BF16).astype(F32)
    row = lax.broadcasted_iota(jnp.int32, (AUG, delta.shape[1]), 0)
    extra = jnp.where(row == 0, top, jnp.where(row == 1, delta - top, 0.0)).astype(BF16)
    do = jnp.concatenate([low, extra], axis=0)
    q = q_ref[h]
    slot = h % BATCH
    keys = k_far.shape[2]
    bk = key_block(keys)
    acc = None
    for which in ("far", "near"):
        for i in range(keys // bk):
            cut = slice(i * bk, (i + 1) * bk)
            k = k_far[0, :, cut] if which == "far" else k_ref[h, :, cut]
            v = (v_far if which == "far" else v_near)[0, :, cut]
            e = (e_far if which == "far" else e_near)[0, cut, :]
            v = jnp.concatenate([v, ones_ref[:, cut]], axis=0)
            ds = (e.astype(F32) * mul(v, do, TN)).astype(BF16)
            part = mul(k, ds, NN)
            acc = part if acc is None else acc + part
            d_k, d_v = mul(q, ds, NT), mul(low, e, NT)
            if which == "far":
                far_out[slot, 0, :, cut] = d_k.astype(BF16)
                far_out[slot, 1, :, cut] = d_v.astype(BF16)
            else:
                kept[slot, 1, :, cut] = d_k
                kept[slot, 2, :, cut] = d_v
        if which == "far":
            remote(far_out.at[slot], far_in.at[h], far_sems, h, here.other_core()).start()
    kept[slot, 0] = acc


def backward_all_kernel(*refs):
    attn, refs = refs[:11], refs[11:]
    gain_refs, refs = refs[:4], refs[4:]
    scale_ref, h_ref, *refs = refs
    up_keep, up_give, down_keep, down_give, out_keep, out_give, *refs = refs
    d_ref, sum_q_ref, sum_k_ref, keep_c, give_c, *refs = refs
    up_out, down_out, out_out, qkv_a, qkv_b, *refs = refs
    far_out, far_in, far_send, far_recv, kept, load_sem, *refs = refs
    here = Here()
    step = pl.program_id(0)
    far_sems = (far_send, far_recv)

    def take(first, give, keep=None):
        nonlocal refs
        mine, sems, refs = refs[:5], refs[5:7], refs[7:]
        return Sum(here, first, give, mine[1] if keep is None else keep, mine, sems)

    chunk = up_keep.shape[-1] // 4
    up_p = (slice(None),) * 4 + (pl.ds(0, chunk),)
    up_c = (slice(None),) * 4 + (pl.ds(chunk, 3 * chunk),)
    sums = [
        take("plane", down_give),
        take("plane", out_give),
        take("plane", up_give.at[up_p]),
        take("column", up_give.at[up_c]),
    ]
    loads = [
        pltpu.make_async_copy(source, total.whole, load_sem.at[i])
        for i, (source, total) in enumerate(
            zip((down_keep, out_keep, up_keep.at[up_p], up_keep.at[up_c]), sums)
        )
    ]
    give_a, give_b, *refs = refs
    more = [take("plane", give_a), take("plane", give_b)]
    heads = H // BATCH

    @pl.when(step == 0)
    def _():
        greet(here.partners())
        for load, total in zip(loads, sums):
            load.start()
            total.start(0)

    def far_copy(h):
        return remote(far_out.at[h % BATCH], far_in.at[h], far_sems, h, here.other_core())

    @pl.when((step % BATCH == 0) & (step > 0))
    def _():
        base = step - BATCH
        for i in range(BATCH):
            far_copy(base + i).wait()
        for i in range(0, BATCH, 2):
            two = pl.ds(base + i, 2)
            some = slice(i, i + 2)
            d_k = kept[some, 1] + far_in[two, 0].astype(F32)
            d_v = kept[some, 2] + far_in[two, 1].astype(F32)
            d, sum_q, sum_k = head_backs(
                kept[some, 0],
                d_k,
                d_v,
                attn[5][two],
                attn[6][two],
                *[ref[some] for ref in gain_refs],
                scale_ref[0, some],
                scale_ref[1, some],
            )
            d_ref[:, some] = d
            sum_q_ref[some] = sum_q
            sum_k_ref[some] = sum_k
        grad = mul(h_ref[...], d_ref[...].reshape(-1, d_ref.shape[-1]), NT)
        for i, (keep, give) in enumerate(
            ((more[0].keep, give_a), (more[1].keep, give_b), (keep_c, give_c))
        ):

            @pl.when(step == BATCH * (i + 1))
            def _():
                spread(grad, here.core, keep, give, 8)
                if i < 2:
                    more[i].start(0)

    @pl.when(step < H)
    def _():
        head_back(here, step, attn, far_out, far_in, far_sems, kept)

    @pl.when(step == 2)
    def _():
        for load, total in zip(loads, sums):
            load.wait()
            total.add_first()

    @pl.when(step == 5)
    def _():
        more[0].add_first()

    @pl.when(step == 8)
    def _():
        for total in sums:
            total.add_second()

    @pl.when(step == 9)
    def _():
        more[0].add_second()
        more[1].add_first()

    @pl.when(step == 11)
    def _():
        more[1].add_second()

    @pl.when(step == H)
    def _():
        down_out[...] = sums[0].add_third()
        unfold(out_out, sums[1].add_third())
        unfold(up_out, sums[2].add_third())
        rest = sums[3].add_third()
        for i in range(3):
            unfold(up_out, rest[:, i * chunk : (i + 1) * chunk], (i + 1) * chunk * 2 // 3)
        unfold(qkv_a, more[0].add_third())
        unfold(qkv_b, more[1].add_third())


def once(shape):
    return pl.BlockSpec(shape, lambda *_: (0,) * len(shape), pipeline_mode=pl.Buffered(1))


ANYWHERE = pl.BlockSpec(memory_space=pl.ANY)


def backward_all(
    e_far, e_near, d_o, o, linv, q, k, k_far, v_far, v, ones, gains, scales, h_t, up, down, out
):
    _, keys, rows = e_far.shape
    width = h_t.shape[0]
    inner = up[0].shape[-1] * 2 // 3

    def head(*tail):
        return pl.BlockSpec((1,) + tail, lambda s: (jnp.minimum(s, H - 1),) + (0,) * len(tail))

    def batch(s):
        return jnp.maximum(s // BATCH - 1, 0)

    gain = pl.BlockSpec((BATCH, HD, 1), lambda s: (batch(s), 0, 0))
    specs = [head(keys, rows), head(keys, rows), head(HD, rows), head(HD, rows), head(8, rows)]
    specs += [once(q.shape), once(k.shape), head(HD, keys), head(HD, keys), head(HD, keys)]
    specs += [once(ones.shape)] + [gain] * 4
    specs.append(pl.BlockSpec((2, BATCH, 1, rows), lambda s: (0, batch(s), 0, 0)))
    specs.append(once(h_t.shape))
    specs += [ANYWHERE] * 6
    part = (16, 3 * BATCH * HD * 3 // 2)
    third = jax.ShapeDtypeStruct((4, 2, 2) + part, BF16)
    shard = width // 32
    outs = [
        jax.ShapeDtypeStruct((3, H, HD, rows), BF16),
        jax.ShapeDtypeStruct((H, HD, 1), F32),
        jax.ShapeDtypeStruct((H, HD, 1), F32),
        third,
        third,
        jax.ShapeDtypeStruct((shard, inner), F32),
        jax.ShapeDtypeStruct((inner // 32, width), F32),
        jax.ShapeDtypeStruct((shard, width), F32),
        jax.ShapeDtypeStruct((shard, 3 * BATCH * HD), F32),
        jax.ShapeDtypeStruct((shard, 3 * BATCH * HD), F32),
    ]
    out_specs = [pl.BlockSpec((3, BATCH, HD, rows), lambda s: (0, batch(s), 0, 0)), gain, gain]
    out_specs += [once(a.shape) for a in outs[3:]]
    chunk = inner * 3 // 8
    scratch = [
        pltpu.VMEM((BATCH, 2, HD, keys), BF16),
        pltpu.VMEM((H, 2, HD, keys), BF16),
        pltpu.SemaphoreType.DMA((H,)),
        pltpu.SemaphoreType.DMA((H,)),
        pltpu.VMEM((BATCH, 3, HD, rows), F32),
        pltpu.SemaphoreType.DMA((4,)),
        *sum_scratch("plane", (inner // 32, width)),
        *sum_scratch("plane", (16, width * 3 // 2)),
        *sum_scratch("plane", (16, chunk)),
        *sum_scratch("column", (16, 3 * chunk)),
        pltpu.VMEM((4, 2, 2) + part, BF16),
        pltpu.VMEM((4, 2, 2) + part, BF16),
        *sum_scratch("plane", part),
        *sum_scratch("plane", part),
    ]
    return pl.pallas_call(
        backward_all_kernel,
        grid=(H + 1,),
        in_specs=specs,
        out_specs=out_specs,
        out_shape=outs,
        scratch_shapes=scratch,
        compiler_params=pltpu.CompilerParams(
            vmem_limit_bytes=61 * 2**20, collective_id=0, has_side_effects=True
        ),
        name="backward_all",
    )(
        e_far, e_near, d_o, o, linv, q, k, k_far, v_far, v, ones, *gains, scales, h_t,
        *up, *down, *out,
    )


def tail_kernel(*refs):
    d_ref, w_ref, x_ref, dx1_ref, gain_ref, *refs = refs
    sum_q_ref, sum_k_ref, dgain2_ref, dbias2_ref, keep_ref, give_ref, *refs = refs
    out_ref, qkv_ref, table_ref, *refs = refs
    made, vectors, keep_t, give_t, stay_sem, swap_send, swap_recv, *refs = refs
    here = Here()
    step = pl.program_id(0)
    steps = pl.num_programs(0)
    block = x_ref.shape[0]
    swapped = here.core != here.y
    opposite = here.device(core=here.y, y=here.core)
    rest = Sum(here, "column", give_ref, keep_ref, refs[:5], refs[5:7])
    table = Sum(here, "plane", give_t, keep_t, refs[7:12], refs[12:14])

    @pl.when(step == 0)
    def _():
        greet(here.partners() + [here.device(core=1 - here.core, y=1 - here.y)])
        rest.start(0)

    def stay(i):
        cut = pl.ds(i * block, block)
        return pltpu.make_async_copy(made.at[cut], out_ref.at[cut], stay_sem.at[i])

    def move(i):
        cut = pl.ds(i * block, block)
        return remote(made.at[cut], out_ref.at[cut], (swap_send, swap_recv), i, opposite)

    new, dgain, dbias = token_grads(
        d_ref[...], w_ref[...], x_ref[...], dx1_ref[...], gain_ref[...]
    )
    made[pl.ds(pl.multiple_of(step * block, block), block), :] = new
    first = step == 0
    vectors[0:1, :] = jnp.where(first, dgain, vectors[0:1, :] + dgain)
    vectors[1:2, :] = jnp.where(first, dbias, vectors[1:2, :] + dbias)

    @pl.when(swapped)
    def _():
        move(step).start()

    @pl.when(jnp.logical_not(swapped))
    def _():
        stay(step).start()

    @pl.when(step == 0)
    def _():
        rest.add_first()

    @pl.when(step == steps - 1)
    def _():
        width = x_ref.shape[1]
        rows = [vectors[0:1, :], vectors[1:2, :], dgain2_ref[...], dbias2_ref[...]]
        rows.append(jnp.zeros((124, width), F32))
        columns = jnp.concatenate(rows, axis=0).T
        lane = lax.broadcasted_iota(jnp.int32, columns.shape, 1)
        columns = jnp.where(lane == 4, sum_q_ref[...].reshape(width, 1), columns)
        columns = jnp.where(lane == 5, sum_k_ref[...].reshape(width, 1), columns)
        columns = columns.reshape(8, 2, 2, width // 32, 128)
        mine = here.core == 0
        keep_t[...] = jnp.where(mine, columns[:, 0], columns[:, 1]).reshape(keep_t.shape)
        give_t[...] = jnp.where(mine, columns[:, 1], columns[:, 0]).reshape(keep_t.shape)
        table.start(0)
        table.add_first()
        table.add_second()
        rest.add_second()
        table_ref[...] = table.add_third()
        unfold(qkv_ref, rest.add_third())

        @pl.when(swapped)
        def _():
            for i in range(steps):
                move(i).wait()

        @pl.when(jnp.logical_not(swapped))
        def _():
            for i in range(steps):
                stay(i).wait()


def tail(d, w, x, dx1, gain, sum_q, sum_k, dgain2, dbias2, keep, give):
    rows, width = x.shape
    block = math.gcd(rows, 256)
    steps = rows // block
    row = pl.BlockSpec((block, width), lambda i: (i, 0))
    shard = width // 32
    part = keep.shape[-2:]
    return pl.pallas_call(
        tail_kernel,
        grid=(steps,),
        in_specs=[
            pl.BlockSpec(d.shape[:3] + (block,), lambda i: (0, 0, 0, i)),
            once(w.shape),
            row,
            row,
            once(gain.shape),
            once(sum_q.shape),
            once(sum_k.shape),
            once(dgain2.shape),
            once(dbias2.shape),
            once(keep.shape),
            ANYWHERE,
        ],
        out_specs=[ANYWHERE, once((shard, 3 * BATCH * HD)), once((shard, 128))],
        out_shape=[
            jax.ShapeDtypeStruct((rows, width), BF16),
            jax.ShapeDtypeStruct((shard, 3 * BATCH * HD), F32),
            jax.ShapeDtypeStruct((shard, 128), F32),
        ],
        scratch_shapes=[
            pltpu.VMEM((rows, width), BF16),
            pltpu.VMEM((8, width), F32),
            pltpu.VMEM((4, 2, 2, shard, 128), F32),
            pltpu.VMEM((4, 2, 2, shard, 128), F32),
            pltpu.SemaphoreType.DMA((steps,)),
            pltpu.SemaphoreType.DMA((steps,)),
            pltpu.SemaphoreType.DMA((steps,)),
            *sum_scratch("column", part),
            *sum_scratch("plane", (shard, 128), F32),
        ],
        compiler_params=pltpu.CompilerParams(
            vmem_limit_bytes=VMEM_LIMIT, collective_id=1, has_side_effects=True
        ),
        name="tail",
    )(d, w, x, dx1, gain, sum_q, sum_k, dgain2, dbias2, keep, give)


def place(index):
    return index // 8, index // 4 % 2, index // 2 % 2, index % 2


def device(z, x, core, y):
    return ((z * 2 + x) * 2 + core) * 2 + y


def pairs(other):
    every = [(i, device(*other(*place(i)))) for i in range(32)]
    return [(i, j) for i, j in every if i != j]


SWAP = pairs(lambda z, x, c, y: (z, x, y, c))
CORE = pairs(lambda z, x, c, y: (z, x, 1 - c, y))


def send(value, where):
    return lax.ppermute(value, AXES, where)


def after(values, *done):
    return lax.optimization_barrier((values, done))[0]


def segments(lengths, group, mine, rows):
    count = lengths.shape[1]
    at = jnp.arange(count)
    ends = jnp.sum(jnp.where(at[:, None] <= at[None, :], lengths[0][:, None], 0), axis=0)
    spots = jnp.arange(group, dtype=jnp.int32)
    segment = jnp.sum((spots[None, :] >= ends[:, None]).astype(jnp.int32), axis=0)
    is_in = jnp.arange(AUG)[:, None] == segment[None, :]
    mask_k = is_in.astype(BF16)
    mask_q = jnp.where(is_in, 0.0, BLOCKED).astype(BF16)
    mask_q = lax.dynamic_slice_in_dim(mask_q, mine * rows, rows, axis=1)
    ones = jnp.broadcast_to((jnp.arange(AUG) < 2)[:, None], (AUG, group)).astype(BF16)
    return mask_q, mask_k, ones


def ungroup(grads):
    parts = [g.reshape(-1, 3, BATCH * HD) for g in grads]
    return jnp.concatenate(parts, axis=2).reshape(parts[0].shape[0], -1)


def on_chips(tokens, lengths, gains, w_t, w_qkv, w_out, w_up, w_down, cotangent):
    ln1_gain, ln1_bias, ln2_gain, ln2_bias, fold_q, fold_k, inv_q, inv_k, gain_q, gain_k = gains
    rows, width = tokens.shape
    wide, y = lax.axis_index("wide"), lax.axis_index("blk")
    core = wide % 2
    swapped = core != y
    flag = swapped.astype(jnp.int32).reshape(1)
    core_at = core.astype(jnp.int32).reshape(1)

    def swap(value):
        return jnp.where(swapped, send(value, SWAP), value)

    lengths = swap(lengths)
    came = send(tokens, SWAP)
    cotangent_came = send(after(cotangent, came), SWAP)
    mask_q, mask_k, ones = segments(lengths, 2 * rows, core, rows)
    mask_near = lax.dynamic_slice_in_dim(mask_k, core * rows, rows, axis=1)
    mask_far = lax.dynamic_slice_in_dim(mask_k, (1 - core) * rows, rows, axis=1)
    ones = ones[:, :rows]

    h_t, q, k, v, scales, tokens = project(
        tokens, ln1_gain, ln1_bias, w_t, fold_q, fold_k, flag, came
    )
    k_far, v_far = send(k, CORE), send(v, CORE)
    had, e_near = attend(q, k, v, mask_q, mask_near, ones)
    e_far, o, linv = attend(q, k_far, v_far, mask_q, mask_far, ones, had)
    cotangent = jnp.where(swapped, cotangent_came, cotangent)
    output, dx1, d_o, dgain2, dbias2, *grads = middle(
        tokens, o.reshape(width, rows), cotangent, w_out, ln2_gain, ln2_bias, w_up, w_down, core_at
    )
    d_o = d_o.reshape(H, HD, rows)
    output = swap(output)
    gains = [inv_q, inv_k, gain_q, gain_k]
    d, sum_q, sum_k, keep, give, up, down, out, qkv_a, qkv_b = backward_all(
        e_far, e_near, d_o, o, linv, q, k, k_far, v_far, v, ones, gains, scales, h_t,
        grads[0:2], grads[2:4], grads[4:6],
    )
    grad_tokens, qkv_c, table = tail(
        d, w_qkv, tokens, dx1, ln1_gain, sum_q, sum_k, dgain2, dbias2, keep, give
    )
    sums = [table[:, i] for i in (0, 1, 4, 5, 2, 3)]
    return output, grad_tokens, sums, ungroup([qkv_a, qkv_b, qkv_c]), out, up, down


def anywhere(tokens, lengths, gains, w_t, w_qkv, w_out, w_up, w_down, cotangent):
    ln1_gain, ln1_bias, ln2_gain, ln2_bias, fold_q, fold_k, inv_q, inv_k, gain_q, gain_k = gains
    rows, width = tokens.shape
    parts = lax.axis_size("blk")
    mask_q, mask_k, ones = segments(lengths, rows * parts, lax.axis_index("blk"), rows)
    h_t, q, k, v, scales = project(tokens, ln1_gain, ln1_bias, w_t, fold_q, fold_k)
    k_all = lax.all_gather(k, "blk", axis=2, tiled=True)
    v_all = lax.all_gather(v, "blk", axis=2, tiled=True)
    had, e_all = attend(q, k_all, v_all, mask_q, mask_k, ones)
    linv = jnp.broadcast_to(1.0 / had[:, HD : HD + 1], (H, 8, rows))
    o = (had[:, :HD] * linv[:, :1]).astype(BF16)
    output, dx1, d_o, dgain2, dbias2, up, down, out = middle(
        tokens, o.reshape(width, rows), cotangent, w_out, ln2_gain, ln2_bias, w_up, w_down
    )
    d_o = d_o.reshape(H, HD, rows)
    d_q, d_k, d_v = attend_back(e_all, d_o, o, linv, q, k_all, v_all, ones, 0, H, F32)
    pair = jnp.stack([d_k, d_v]).reshape(2, H, HD, parts, rows)
    pair = jnp.transpose(pair, (3, 0, 1, 2, 4)).astype(BF16)
    pair = lax.psum_scatter(pair, "blk", scatter_dimension=0, tiled=False).astype(F32)
    d, sum_q, sum_k, grad = post(
        d_q, pair[0], pair[1], q, k, inv_q, inv_k, gain_q, gain_k, scales, h_t
    )
    grad_tokens, dgain1, dbias1 = last(d, w_qkv, tokens, dx1, ln1_gain)
    scatter = functools.partial(lax.psum_scatter, axis_name=AXES, scatter_dimension=0, tiled=True)
    sums = [
        scatter(g.reshape(width)) for g in (dgain1, dbias1, sum_q, sum_k, dgain2, dbias2)
    ]
    grad = ungroup(jnp.split(grad, H // BATCH, axis=1))
    return output, grad_tokens, sums, scatter(grad), scatter(out), scatter(up), scatter(down)


def shards(
    tokens,
    lengths,
    ln1_gain,
    ln1_bias,
    w_qkv,
    q_gain,
    k_gain,
    w_out,
    ln2_gain,
    ln2_bias,
    w_up,
    w_down,
    cotangent,
):
    width = tokens.shape[1]
    fold_q, fold_k = LOG2E / math.sqrt(HD), 1.0
    gains = [g.reshape(1, width) for g in (ln1_gain, ln1_bias, ln2_gain, ln2_bias)]
    gains += [
        g.reshape(H, HD, 1)
        for g in (
            q_gain * fold_q,
            k_gain * fold_k,
            1.0 / (q_gain * fold_q),
            1.0 / (k_gain * fold_k),
            q_gain,
            k_gain,
        )
    ]
    known = lax.axis_size("blk") == 2 and lax.axis_size("wide") == 16
    run = on_chips if known else anywhere
    output, grad_tokens, sums, s_qkv, s_out, s_up, s_down = run(
        tokens, lengths, gains, w_qkv.T, w_qkv, w_out, w_up, w_down, cotangent
    )
    return (
        output,
        grad_tokens,
        sums[0],
        sums[1],
        s_qkv,
        sums[2],
        sums[3],
        s_out,
        sums[4],
        sums[5],
        s_up,
        s_down,
    )


def solution(mesh):
    split = P(AXES, None)
    in_specs = (split, P("wide", None)) + (P(),) * 10 + (split,)
    vector = P(AXES)
    out_specs = (
        split,
        split,
        vector,
        vector,
        split,
        vector,
        vector,
        split,
        vector,
        vector,
        split,
        split,
    )
    return jax.shard_map(shards, mesh=mesh, in_specs=in_specs, out_specs=out_specs, check_vma=False)
```

time: 564 us -> 266 us (0.47); the launches traced: 554 us -> 265 us
  Pallas kernels: 103 us -> 220 us
  waiting for transfers between devices: 105 us -> 0.02 us
  matrix products: 92.3 us -> 0 us
  other arithmetic: 81.7 us -> 3.55 us
  starting transfers between devices: 84.1 us -> 16.2 us
  local copies, waits for them, and re-layouts: 85 us -> 24.3 us
    pallas_call x4, Pallas kernels: 66.6 us -> 183 us  [the longest x1 93.1 us: backward_all(): pl.pallas_call(backward_all_kernel, grid=(H + 1,), in_specs=specs, out_sp...]
    ppermute x33 -> x6, waiting for transfers between devices: 105 us -> 0.02 us  [send(): return lax.ppermute(value, AXES, where)]
    dot_general x13 -> x0, matrix products: 92.3 us -> none  [mul(): lax.dot_general(left, right, dims, preferred_element_type=F32).astype(kind)]
    ppermute x33 -> x6, starting transfers between devices: 84.1 us -> 16.2 us  [send(): return lax.ppermute(value, AXES, where)]
    convert_element_type x30 -> x3, other arithmetic: 33.6 us -> 0.66 us  [the longest x1 0.62 us: segments(): mask_q = jnp.where(is_in, 0.0, BLOCKED).astype(BF16)]
    reduce_sum x13 -> x2, other arithmetic: 26.6 us -> 0.18 us  [the longest x1 0.1 us: segments(): jnp.sum((spots[None, :] >= ends[:, None]).astype(jnp.int32), axis=0)]
    slice x9 -> x2, local copies, waits for them, and re-layouts: 16 us -> 1.45 us  [the longest x1 0.78 us: on_chips(): sums = [table[:, i] for i in (0, 1, 4, 5, 2, 3)]]
    dynamic_slice x9 -> x1, local copies, waits for them, and re-layouts: 13.6 us -> 0.64 us  [on_chips(): mask_near = lax.dynamic_slice_in_dim(mask_k, core * rows, rows, axis=1)]
  transfers between devices with their start and end apart: 33 -> 6, of which waited for: 13 -> 0; matrix products, arithmetic and copies ran while one was open for 36% -> 8% of each run, Pallas kernels for 13% -> 58%
where the time goes in v2:
time: 266 us; the launch traced here: 265 us
  Pallas kernels  220 us (83%)
  local copies, waits for them, and re-layouts  24.3 us (9%)
  starting transfers between devices  16.2 us (6%)
  other arithmetic  3.55 us (1%)
    pallas_call x1, Pallas kernels, backward_all(): pl.pallas_call(backward_all_kernel, grid=(H + 1,), in_specs=specs, out_sp...  93.1 us
    pallas_call x1, Pallas kernels, middle(): pl.pallas_call(functools.partial(middle_kernel, split), grid=(steps,), in...  46.2 us
    pallas_call x2, Pallas kernels, attend(): pl.pallas_call(functools.partial(forward_kernel, key_block(keys), first),...  36.7 us
    pallas_call x1, Pallas kernels, tail(): pl.pallas_call(tail_kernel, grid=(steps,), in_specs=[pl.BlockSpec(d.shape...  33.7 us
    ppermute x6, starting transfers between devices, send(): return lax.ppermute(value, AXES, where)  16.2 us
    unnamed x38, local copies, waits for them, and re-layouts  12.2 us
    pallas_call x1, Pallas kernels, project(): pl.pallas_call(functools.partial(pre_kernel, swapped), grid=(rows // bloc...  10.1 us
  transfers between devices with their start and end apart: 6, of which 0 were waited for; matrix products, arithmetic and copies ran while one was open for 8% of the time, Pallas kernels for 58%

profile of v2, /device:TPU:0, one launch (start us, length us, event | category | flops | bytes accessed | tf_op | source)
XLA Modules:
  0.0 264.7 jit_solution(4127692609285863126)
XLA Ops:
  0.6 1.9 collective-permute-start
  2.5 0.6 collective-permute-start.3
  3.2 1.3 reshape.88.refs_3_.refs_4_
  4.4 1.3 reshape.89.refs_4_
  5.7 0.0 copy-start.15
  5.7 0.0 copy-start
  5.7 5.9 %copy.33 = bf16[768,2304]{0,1:T(8,128)(2,1)} copy(bf16[768,2304]{1,0:T(8,128)(2,1)} %refs_1_.3) | data formatting | bytes 7077888 | tf_op args[4]
  11.6 1.0 reshape.105.refs_6_
  12.7 1.0 reshape.106.refs_7_.refs_14_
  13.7 0.6 reshape.93.refs_5_
  14.3 0.6 reshape.94.refs_6_
  14.9 0.0 collective-permute-done.3
  14.9 0.1 select_reduce_fusion
  15.0 0.1 convert_reduce_fusion
  15.1 0.6 constant_dynamic-slice_fusion.1
  15.8 0.0 collective-permute-done.refs_2_
  15.8 0.8 collective-permute-start.4
  16.5 10.1 %project.1 = (bf16[768,1024]{1,0:T(8,128)(2,1)}, bf16[12,64,1024]{2,1,0:T(8,128)(2,1)}, bf16[12,64,1024]{2,1,0:T(8,128)(2,1)}, bf16[12,64,1024]{2,1,0:T(8,128)(2...) custom-call(s32[1]{0:T(128)} %bitcast.1.refs_0_, bf16[1024,768]{1,0:T(8,128)(2,1)} %refs_1_.2, ...), custom_call_target="tpu_custom_call" | custom-call | flops 3623878656 | bytes 9437184 | tf_op jit(solution)/shard_map/project/pallas_call | solution.py:242
  26.6 12.1 %collective-permute-start.1 = (bf16[12,64,1024]{2,1,0:T(8,128)(2,1)}, bf16[12,64,1024]{2,1,0:T(8,128)(2,1)S(1)}, u32[]{:S(2)}, u32[]{:S(2)}) collective-permute-start(bf16[12,64,1024]{2,1,0:T(8,128)(2,1)} %get-tuple-element.50.refs_1_.refs_6_), channel_id=1, source_target_pairs={{0,2},{1,3},{2,0},{3,1},{4,6},{5,7},{6,4},{7,5},{8,10},{9,11},{10,... | collective-permute-start | bytes 4718600 | tf_op jit(solution)/shard_map/ppermute | solution.py:1008
  38.7 0.1 collective-permute-start.2
  38.8 0.6 select_convert_fusion.refs_3_
  39.4 0.7 slice.25.refs_5_.refs_10_
  40.1 17.4 %attend_first.1 = (f32[12,80,1024]{2,1,0:T(8,128)}, bf16[12,1024,1024]{2,1,0:T(8,128)(2,1)}) custom-call(bf16[12,64,1024]{2,1,0:T(8,128)(2,1)} %get-tuple-element.49.refs_0_.refs_5_, bf16[12,64,1024]{2,1,0:T(8,128)(2,1)} %get-tuple-element.50.refs_1_.refs_6_, bf16[12,64,1024]{2,1,0:T(8,128)(2,1)} %get-tuple-element.51.refs_2_.refs_9_, ...), custom_call_target="tpu_custom_call" | custom-call | flops 12884901888 | bytes 25165824 | tf_op jit(solution)/shard_map/attend_first/pallas_call | solution.py:89
  57.5 0.0 collective-permute-done.4
  57.5 1.3 broadcast_select_fusion.1.refs_3_
  58.8 0.0 collective-permute-done.1.refs_1_.refs_7_
  58.8 0.0 collective-permute-done.2.refs_2_.refs_8_
  58.8 1.1 copy-done.3
  59.9 0.6 copy-done.4
  60.5 19.3 %attend_last.1 = (bf16[12,1024,1024]{2,1,0:T(8,128)(2,1)}, bf16[12,64,1024]{2,1,0:T(8,128)(2,1)}, f32[12,8,1024]{2,1,0:T(8,128)}) custom-call(bf16[12,64,1024]{2,1,0:T(8,128)(2,1)} %get-tuple-element.49.refs_0_.refs_5_, bf16[12,64,1024]{2,1,0:T(8,128)(2,1)} %copy-done.3, bf16[12,64,1024]{2,1,0:T(8,128)(2,1)} %copy-done.4, ...), custom_call_target="tpu_custom_call" | custom-call | flops 12884901888 | bytes 25165824 | tf_op jit(solution)/shard_map/attend_last/pallas_call | solution.py:89
  79.8 46.2 %middle.1 = (bf16[1024,768]{1,0:T(8,128)(2,1)}, f32[1024,768]{1,0:T(8,128)}, f32[768,1024]{1,0:T(8,128)}, f32[1,768]{1,0:T(1,128)}, f32[1,768]{1,0:T(1,128)}, /*...) custom-call(s32[1]{0:T(128)} %bitcast.refs_0_, ...), custom_call_target="tpu_custom_call" | custom-call | flops 32614907904 | bytes 31457280 | tf_op jit(solution)/shard_map/middle/pallas_call | solution.py:374
  126.0 0.8 collective-permute-start.5
  126.8 1.0 reshape.109.refs_13_
  127.8 1.0 reshape.107.refs_11_
  128.8 1.0 reshape.108.refs_12_
  129.9 93.1 %backward_all.1 = (bf16[3,12,64,1024]{3,2,1,0:T(8,128)(2,1)}, f32[12,64,1]{2,1,0:T(8,128)}, f32[12,64,1]{2,1,0:T(8,128)}, bf16[4,2,2,16,1152]{4,3,2,1,0:T(8,128)...) custom-call(bf16[12,1024,1024]{2,1,0:T(8,128)(2,1)} %get-tuple-eleme, ...), custom_call_target="tpu_custom_call" | custom-call | tf_op jit(solution)/shard_map/backward_all/pallas_call | solution.py:848
  223.0 33.7 %tail.1 = (bf16[1024,768]{1,0:T(8,128)(2,1)}, f32[24,768]{1,0:T(8,128)}, f32[24,128]{1,0:T(8,128)}) custom-call(bf16[3,12,64,1024]{3,2,1,0:T(8,128)(2,1)} %get-tuple-element.68.refs_0_, bf16[768,2304]{1,0:T(8,128)(2,1)} %refs_1_.3, bf16[1024,768]{1,0:T(8,128)(2,1)} %get-tuple-element.48.refs_1_.refs_2_, f32[1024,768]{1,0:T(8,128)} %get-tuple-element.69.refs_3_, ...), custom_call_target="tpu_custom_call" | custom-call | tf_op jit(solution)/shard_map/tail/pallas_call | solution.py:950
  256.8 1.0 reshape.101
  257.9 0.1 pad_maximum_fusion
  258.0 0.7 copy.40
  258.7 0.8 slice_reduce_fusion
  259.5 0.0 collective-permute-done.5
  259.5 1.3 broadcast_select_fusion
  260.8 0.7 copy-done.2
  261.5 1.1 copy.45
  262.6 0.6 copy.46
  263.3 0.7 copy.47
  264.0 0.7 copy.48
  (34 shorter events, 0.2 us)
Async XLA Ops:
  0.6 15.1 %collective-permute-start = (bf16[1024,768]{1,0:T(8,128)(2,1)}, bf16[1024,768]{1,0:T(8,128)(2,1)}, u32[]{:S(2)}, u32[]{:S(2)}) collective-permute-start(bf16[1024,768]{1,0:T(8,128)(2,1)} %refs_1_.2), channel_id=1, source_target_pairs={{1,2},{2,1},{5,6},{6,5},{9,10},{10,9},{13,14},{14,13},{17,18},{18,... | collective-permute-start | bytes 4718600 | tf_op jit(solution)/shard_map/ppermute | solution.py:1008
  2.5 12.4 %collective-permute-start.3 = (s32[1,6]{1,0:T(1,128)}, s32[1,6]{1,0:T(1,128)S(1)}, u32[]{:S(2)}, u32[]{:S(2)}) collective-permute-start(s32[1,6]{1,0:T(1,128)} %param.14), channel_id=1, source_target_pairs={{1,2},{2,1},{5,6},{6,5},{9,10},{10,9},{13,14},{14,13},{17,18},{18,... | collective-permute-start | bytes 80 | tf_op jit(solution)/shard_map/ppermute | solution.py:1008
  5.7 5.9 %copy-start.11 = (f32[768]{0:T(1024)S(1)}, f32[768]{0:T(1024)}, u32[]{:S(2)}) copy-start(f32[768]{0:T(1024)} %param.18) | copy-start | bytes 9220
  5.7 6.9 %copy-start.12 = (f32[768]{0:T(1024)S(1)}, f32[768]{0:T(1024)}, u32[]{:S(2)}) copy-start(f32[768]{0:T(1024)} %param.19) | copy-start | bytes 9220
  5.7 8.0 %copy-start.13 = (f32[768]{0:T(1024)S(1)}, f32[768]{0:T(1024)}, u32[]{:S(2)}) copy-start(f32[768]{0:T(1024)} %param.21) | copy-start | bytes 9220
  5.7 8.6 %copy-start.14 = (f32[768]{0:T(1024)S(1)}, f32[768]{0:T(1024)}, u32[]{:S(2)}) copy-start(f32[768]{0:T(1024)} %param.22) | copy-start | bytes 9220
  5.7 9.2 %copy-start.15 = (s32[1,6]{1,0:T(1,128)S(1)}, s32[1,6]{1,0:T(1,128)}, u32[]{:S(2)}) copy-start(s32[1,6]{1,0:T(1,128)} %param.14) | copy-start | bytes 76
  5.7 10.0 %copy-start = (bf16[1024,768]{1,0:T(8,128)(2,1)S(1)}, bf16[1024,768]{1,0:T(8,128)(2,1)}, u32[]{:S(2)}) copy-start(bf16[1024,768]{1,0:T(8,128)(2,1)} %param.25) | copy-start | bytes 4718596
  15.8 41.7 %collective-permute-start.4 = (bf16[1024,768]{1,0:T(8,128)(2,1)S(1)}, bf16[1024,768]{1,0:T(8,128)(2,1)S(1)}, u32[]{:S(2)}, u32[]{:S(2)}) collective-permute-start(bf16[1024,768]{1,0:T(8,128)(2,1)S(1)} %copy-done), channel_id=1, source_target_pairs={{1,2},{2,1},{5,6},{6,5},{9,10},{10,9},{13,14},{14,13},{17,18},{18,... | collective-permute-start | bytes 4718600 | tf_op jit(solution)/shard_map/ppermute | solution.py:1008
  26.6 32.2 %collective-permute-start.1 = (bf16[12,64,1024]{2,1,0:T(8,128)(2,1)}, bf16[12,64,1024]{2,1,0:T(8,128)(2,1)S(1)}, u32[]{:S(2)}, u32[]{:S(2)}) collective-permute-start(bf16[12,64,1024]{2,1,0:T(8,128)(2,1)} %get-tuple-element.50.refs_1_.refs_6_), channel_id=1, source_target_pairs={{0,2},{1,3},{2,0},{3,1},{4,6},{5,7},{6,4},{7,5},{8,10},{9,11},{10,... | collective-permute-start | bytes 4718600 | tf_op jit(solution)/shard_map/ppermute | solution.py:1008
  38.7 20.1 %collective-permute-start.2 = (bf16[12,64,1024]{2,1,0:T(8,128)(2,1)}, bf16[12,64,1024]{2,1,0:T(8,128)(2,1)S(1)}, u32[]{:S(2)}, u32[]{:S(2)}) collective-permute-start(bf16[12,64,1024]{2,1,0:T(8,128)(2,1)} %get-tuple-element.51.refs_2_.refs_9_), channel_id=1, source_target_pairs={{0,2},{1,3},{2,0},{3,1},{4,6},{5,7},{6,4},{7,5},{8,10},{9,11},{10,... | collective-permute-start | bytes 4718600 | tf_op jit(solution)/shard_map/ppermute | solution.py:1008
  58.8 1.1 copy-start.3
  58.8 1.7 copy-start.4
  126.0 133.5 %collective-permute-start.5 = (bf16[1024,768]{1,0:T(8,128)(2,1)}, bf16[1024,768]{1,0:T(8,128)(2,1)S(1)}, u32[]{:S(2)}, u32[]{:S(2)}) collective-permute-start(bf16[1024,768]{1,0:T(8,128)(2,1)} %get-tuple-element.55), channel_id=1, source_target_pairs={{1,2},{2,1},{5,6},{6,5},{9,10},{10,9},{13,14},{14,13},{17,18},{18,... | collective-permute-start | bytes 4718600 | tf_op jit(solution)/shard_map/ppermute | solution.py:1008
  223.0 34.8 %copy-start.10 = (f32[24,768]{1,0:T(8,128)S(1)}, f32[24,768]{1,0:T(8,128)}, u32[]{:S(2)}) copy-start(f32[24,768]{1,0:T(8,128)} %get-tuple-element.79) | copy-start | bytes 221188
  223.0 34.9 %copy-start.9 = (f32[24,768]{1,0:T(8,128)S(1)}, f32[24,768]{1,0:T(8,128)}, u32[]{:S(2)}) copy-start(f32[24,768]{1,0:T(8,128)} %get-tuple-element.78) | copy-start | bytes 221188
  256.8 2.0 copy-start.5
  256.8 2.8 %copy-start.1 = (bf16[1024,768]{1,0:T(8,128)(2,1)S(1)}, bf16[1024,768]{1,0:T(8,128)(2,1)}, u32[]{:S(2)}) copy-start(bf16[1024,768]{1,0:T(8,128)(2,1)} %get-tuple-element.55) | copy-start | bytes 4718596
  259.5 2.0 copy-start.2
  261.5 1.2 copy-start.8
  261.5 1.8 copy-start.7
  261.5 2.5 copy-start.6

commit v3 on v2

v3 whole, which is shorter than its diff:
```python
import functools
import math

import jax
import jax.numpy as jnp
from jax import lax
from jax.experimental import pallas as pl
from jax.experimental.pallas import tpu as pltpu
from jax.sharding import PartitionSpec as P

H = 12
HD = 64
EPS = 1e-06
AXES = ("wide", "blk")
AUG = 16
BLOCKED = -512.0
LOG2E = math.log2(math.e)
NN = (((1,), (0,)), ((), ()))
NT = (((1,), (1,)), ((), ()))
TN = (((0,), (0,)), ((), ()))
TT = (((0,), (1,)), ((), ()))
BF16 = jnp.bfloat16
MESH = pl.DeviceIdType.MESH
F32 = jnp.float32
VMEM_LIMIT = 56 * 2**20


def mul(left, right, dims, kind=F32):
    return lax.dot_general(left, right, dims, preferred_element_type=F32).astype(kind)


def ones_rows(columns):
    return (lax.broadcasted_iota(jnp.int32, (AUG, columns), 0) < 2).astype(BF16)


def key_block(keys):
    return math.gcd(keys, 512)


def forward_kernel(count, *refs):
    q_ref, mq_ref, *refs = refs
    parts, (o_ref, linv_ref, *e_refs) = refs[: 3 * count], refs[3 * count :]
    keys = parts[0].shape[2]
    bk = key_block(keys)
    ones = ones_rows(bk)
    for h in range(q_ref.shape[0]):
        q = jnp.concatenate([q_ref[h], mq_ref[...]], axis=0)
        acc = None
        for p in range(count):
            k_ref, v_ref, mk_ref = parts[3 * p : 3 * p + 3]
            for i in range(keys // bk):
                cut = slice(i * bk, (i + 1) * bk)
                k = jnp.concatenate([k_ref[h, :, cut], mk_ref[:, cut]], axis=0)
                v = jnp.concatenate([v_ref[h, :, cut], ones], axis=0)
                e = jnp.exp2(mul(k, q, TN)).astype(BF16)
                e_refs[p][h, cut, :] = e
                part = mul(v, e, NN)
                acc = part if acc is None else acc + part
        linv = 1.0 / acc[HD : HD + 1]
        o_ref[h] = (acc[:HD] * linv).astype(BF16)
        linv_ref[h] = jnp.broadcast_to(linv, linv_ref.shape[1:])


def attend(q, mask_q, parts):
    heads, _, rows = q.shape
    keys = parts[0][0].shape[2]
    some = 2 if len(parts) * keys * rows <= 1 << 21 else 1

    def head(*tail):
        return pl.BlockSpec((some,) + tail, lambda h: (h,) + (0,) * len(tail))

    specs = [head(HD, rows), fixed(mask_q.shape)]
    for part in parts:
        specs += [head(HD, keys), head(HD, keys), fixed(part[2].shape)]
    return pl.pallas_call(
        functools.partial(forward_kernel, len(parts)),
        grid=(heads // some,),
        in_specs=specs,
        out_specs=[head(HD, rows), head(8, rows)] + [head(keys, rows)] * len(parts),
        out_shape=[
            jax.ShapeDtypeStruct((heads, HD, rows), BF16),
            jax.ShapeDtypeStruct((heads, 8, rows), F32),
        ]
        + [jax.ShapeDtypeStruct((heads, keys, rows), BF16)] * len(parts),
        compiler_params=params(),
        cost_estimate=pl.CostEstimate(
            flops=heads * rows * keys * len(parts) * 1024,
            bytes_accessed=heads * rows * keys * len(parts) * 2,
            transcendentals=heads * rows * keys * len(parts),
        ),
        name="attend",
    )(q, mask_q, *[a for part in parts for a in part])


def scaled_gradient(do_ref, o_ref, linv_ref, h):
    low = (do_ref[h] * linv_ref[h, :1]).astype(BF16)
    delta = -jnp.sum(low.astype(F32) * o_ref[h].astype(F32), axis=0, keepdims=True)
    top = delta.astype(BF16).astype(F32)
    row = lax.broadcasted_iota(jnp.int32, (AUG, delta.shape[1]), 0)
    extra = jnp.where(row == 0, top, jnp.where(row == 1, delta - top, 0.0)).astype(BF16)
    return low, jnp.concatenate([low, extra], axis=0)


def block_back(e, low, do, q, k, v):
    v = jnp.concatenate([v, ones_rows(v.shape[1])], axis=0)
    ds = (e.astype(F32) * mul(v, do, TN)).astype(BF16)
    return mul(k, ds, NN), mul(q, ds, NT), mul(low, e, NT)


def backward_kernel(e_ref, do_ref, o_ref, linv_ref, q_ref, k_ref, v_ref, dq_ref, dk_ref, dv_ref):
    keys = k_ref.shape[2]
    bk = key_block(keys)
    low, do = scaled_gradient(do_ref, o_ref, linv_ref, 0)
    acc = None
    for i in range(keys // bk):
        cut = slice(i * bk, (i + 1) * bk)
        part, dk_ref[0, :, cut], dv_ref[0, :, cut] = block_back(
            e_ref[0, cut, :], low, do, q_ref[0], k_ref[0, :, cut], v_ref[0, :, cut]
        )
        acc = part if acc is None else acc + part
    dq_ref[0] = acc


def attend_back(e, do, o, linv, q, k, v):
    heads, keys, rows = e.shape

    def head(*tail):
        return pl.BlockSpec((1,) + tail, lambda h: (h,) + (0,) * len(tail))

    specs = [head(keys, rows), head(HD, rows), head(HD, rows), head(8, rows), head(HD, rows)]
    return pl.pallas_call(
        backward_kernel,
        grid=(heads,),
        in_specs=specs + [head(HD, keys)] * 2,
        out_specs=[head(HD, rows), head(HD, keys), head(HD, keys)],
        out_shape=[
            jax.ShapeDtypeStruct((heads, HD, rows), F32),
            jax.ShapeDtypeStruct((heads, HD, keys), F32),
            jax.ShapeDtypeStruct((heads, HD, keys), F32),
        ],
        compiler_params=params(),
        name="attend_back",
    )(e, do, o, linv, q, k, v)


def norm(value, axis):
    mean = jnp.mean(value, axis=axis, keepdims=True)
    centred = value - mean
    scale = lax.rsqrt(jnp.mean(centred * centred, axis=axis, keepdims=True) + EPS)
    return centred * scale, scale


def norm_back(grad, unit, scale, axis):
    mean = jnp.mean(grad, axis=axis, keepdims=True)
    along = jnp.mean(grad * unit, axis=axis, keepdims=True)
    return scale * (grad - mean - unit * along)


def gelu_parts(u):
    root = math.sqrt(2.0 / math.pi)
    square = u * u
    t = jnp.tanh(u * (root + (root * 0.044715) * square))
    half = 0.5 + 0.5 * t
    slope = half + (u * (0.5 - 0.5 * t * t)) * (root + (3 * root * 0.044715) * square)
    return u * half, slope


def params(**more):
    return pltpu.CompilerParams(vmem_limit_bytes=VMEM_LIMIT, **more)


def fixed(shape):
    return pl.BlockSpec(shape, lambda *_: (0,) * len(shape))


SCALAR = pl.BlockSpec(memory_space=pltpu.SMEM)
ANYWHERE = pl.BlockSpec(memory_space=pl.ANY)


def normed(x, gain, bias):
    return (norm(x.astype(F32), -1)[0] * gain + bias).astype(BF16)


def heads_of(h, w_ref, gains_ref):
    width = h.shape[1]

    def part(i):
        value = mul(w_ref[i * width : (i + 1) * width, :], h, NT)
        return value.reshape(width // HD, HD, h.shape[0])

    unit_k, scale_k = norm(part(1), 1)
    k = (unit_k * gains_ref[:, :, 1:2]).astype(BF16)
    v = part(2).astype(BF16)
    unit_q, scale_q = norm(part(0), 1)
    q = (unit_q * gains_ref[:, :, 0:1]).astype(BF16)
    return q, k, v, scale_q, scale_k


def project_kernel(x_ref, vec_ref, w_ref, gains_ref, h_ref, q_ref, k_ref, v_ref, scale_ref):
    h = normed(x_ref[...], vec_ref[0:1, :], vec_ref[1:2, :])
    h_ref[...] = h.T
    q_ref[...], k_ref[...], v_ref[...], scale_ref[0], scale_ref[1] = heads_of(h, w_ref, gains_ref)


def project(tokens, vectors, w_t, gains):
    rows, width = tokens.shape
    block = math.gcd(rows, 256)
    head = pl.BlockSpec((H, HD, block), lambda i: (0, 0, i))
    head_shape = jax.ShapeDtypeStruct((H, HD, rows), BF16)
    return pl.pallas_call(
        project_kernel,
        grid=(rows // block,),
        in_specs=[pl.BlockSpec((block, width), lambda i: (i, 0))]
        + [fixed(a.shape) for a in (vectors, w_t, gains)],
        out_specs=[
            pl.BlockSpec((width, block), lambda i: (0, i)),
            head,
            head,
            head,
            pl.BlockSpec((2, H, 1, block), lambda i: (0, 0, 0, i)),
        ],
        out_shape=[
            jax.ShapeDtypeStruct((width, rows), BF16),
            head_shape,
            head_shape,
            head_shape,
            jax.ShapeDtypeStruct((2, H, 1, rows), F32),
        ],
        compiler_params=params(),
        name="project",
    )(tokens, vectors, w_t, gains)


def fold(value):
    if value.shape[-2] % 16 == 0:
        return value
    half = value.shape[-1] // 2
    low = value[..., 16:, :]
    low = jnp.concatenate([low[..., :half], low[..., half:]], axis=-2)
    return jnp.concatenate([value[..., :16, :], low], axis=-1)


def unfold(out_ref, value, start=0):
    count = value.shape[-1] * 2 // 3
    half = count // 2
    out_ref[:16, start : start + count] = value[:, :count]
    out_ref[16:, start : start + half] = value[:8, count:]
    out_ref[16:, start + half : start + count] = value[8:, count:]


def spread(value, core, keep_ref, give_ref, lead):
    rows, columns = value.shape
    value = value.reshape((lead, 2, 2, rows // (4 * lead), columns))
    mine = core == 0
    keep = jnp.where(mine, value[:, 0], value[:, 1])
    give = jnp.where(mine, value[:, 1], value[:, 0])
    keep_ref[...] = fold(keep).astype(BF16).reshape(keep_ref.shape)
    give_ref[...] = fold(give).astype(BF16).reshape(give_ref.shape)


def middle_kernel(split, *refs):
    x_ref, o_ref, dy_ref, w_out_ref, vec_ref, w_up_ref, w_down_ref, *refs = refs
    if split:
        dy_here, (dy_came, *refs) = dy_ref, refs
    out_ref, dx1_ref, do_ref, dgain_ref, dbias_ref, *refs = refs
    grads, refs = (refs[:6], refs[6:]) if split else (refs[:3], refs[3:])
    x1_ref, h2_ref, h2t_ref, acc_ref, dh2_ref, g_ref, du_ref, da_ref, *refs = refs
    step = pl.program_id(0)
    rows = x_ref.shape[0]
    block = math.gcd(rows, 256)
    cuts = [slice(i, i + block) for i in range(0, rows, block)]
    if split:
        here = Here()
        keep_up, keep_down, keep_out, give_out, came_up, came_down = grads
        give_up, give_down, up_send, up_recv, down_send, down_recv, dy_ref, dy_sem = refs
        swapped = here.core != here.y

        def copies(f):
            to = here.other_core()
            return [
                remote(give_up.at[f % 2], came_up.at[f], (up_send, up_recv), f, to),
                remote(give_down.at[f % 2], came_down.at[f], (down_send, down_recv), f, to),
            ]

    @pl.when(step == 0)
    def _():
        if split:
            greet([here.other_core()])

            @pl.when(swapped)
            def _():
                pltpu.make_async_copy(dy_came, dy_ref, dy_sem.at[0]).start()

            @pl.when(jnp.logical_not(swapped))
            def _():
                pltpu.make_async_copy(dy_here, dy_ref, dy_sem.at[0]).start()

        for cut in cuts:
            x1 = x_ref[cut, :].astype(F32) + mul(o_ref[:, cut], w_out_ref[...], TN)
            x1_ref[cut, :] = x1
            acc_ref[cut, :] = x1
            h2 = normed(x1, vec_ref[2:3, :], vec_ref[3:4, :])
            h2_ref[cut, :] = h2
            h2t_ref[:, cut] = h2.T
        if split:
            pltpu.make_async_copy(dy_here, dy_ref, dy_sem.at[0]).wait()

    for cut in cuts:
        dy = dy_ref[cut, :]
        value, slope = gelu_parts(mul(h2_ref[cut, :], w_up_ref[...], NN))
        g = value.astype(BF16)
        g_ref[cut, :] = g
        acc_ref[cut, :] += mul(g, w_down_ref[...], NN)
        du = (mul(dy, w_down_ref[...], NT) * slope).astype(BF16)
        du_ref[cut, :] = du
        part = mul(du, w_up_ref[...], NT)
        dh2_ref[cut, :] = jnp.where(step == 0, part, dh2_ref[cut, :] + part)
    grad_up = mul(h2t_ref[...], du_ref[...], NN)
    grad_down = mul(g_ref[...], dy_ref[...], TN)
    if split:

        @pl.when(step >= 2)
        def _():
            for copy in copies(step - 2):
                copy.wait_send()

        spread(grad_up, here.core, keep_up, give_up.at[step % 2], 8)
        spread(grad_down, here.core, keep_down, give_down.at[step % 2], 2)
        for copy in copies(step):
            copy.start()
    else:
        grads[0][...] = grad_up
        grads[1][...] = grad_down

    @pl.when(step == pl.num_programs(0) - 1)
    def _():
        dgain, dbias = 0.0, 0.0
        for cut in cuts:
            out_ref[cut, :] = acc_ref[cut, :].astype(BF16)
            unit, scale = norm(x1_ref[cut, :], -1)
            dh2 = dh2_ref[cut, :]
            dgain += jnp.sum(dh2 * unit, axis=0, keepdims=True)
            dbias += jnp.sum(dh2, axis=0, keepdims=True)
            dx1 = dy_ref[cut, :].astype(F32) + norm_back(dh2 * vec_ref[2:3, :], unit, scale, -1)
            dx1_ref[cut, :] = dx1
            da = dx1.astype(BF16)
            da_ref[cut, :] = da
            do_ref[:, cut] = mul(w_out_ref[...], da, NT)
        dgain_ref[...] = dgain
        dbias_ref[...] = dbias
        grad_out = mul(o_ref[...], da_ref[...], NN)
        if split:
            spread(grad_out, here.core, keep_out, give_out, 8)
            for f in range(FF_STEPS):
                for copy in copies(f):
                    copy.wait_recv()
                    if f >= FF_STEPS - 2:
                        copy.wait_send()
        else:
            grads[2][...] = grad_out


FF_STEPS = 4


def middle(x, o, dy, w_out, vectors, w_up, w_down, came=None):
    rows, width = x.shape
    inner = w_up.shape[1]
    chunk = inner // FF_STEPS
    split = came is not None
    ins = [x, o, dy, w_out, vectors, w_up, w_down]
    specs = [fixed(a.shape) for a in ins[:5]]
    specs += [pl.BlockSpec((width, chunk), lambda f: (0, f)), pl.BlockSpec((chunk, width), lambda f: (f, 0))]
    weights = specs[-2:]
    if split:
        ins.append(came)
        specs[2] = ANYWHERE
        specs.append(ANYWHERE)
    outs = [
        jax.ShapeDtypeStruct((rows, width), BF16),
        jax.ShapeDtypeStruct((rows, width), F32),
        jax.ShapeDtypeStruct((width, rows), F32),
        jax.ShapeDtypeStruct((1, width), F32),
        jax.ShapeDtypeStruct((1, width), F32),
    ]
    out_specs = [fixed(a.shape) for a in outs]
    scratch = [
        pltpu.VMEM((rows, width), F32),
        pltpu.VMEM((rows, width), BF16),
        pltpu.VMEM((width, rows), BF16),
        pltpu.VMEM((rows, width), F32),
        pltpu.VMEM((rows, width), F32),
        pltpu.VMEM((rows, chunk), BF16),
        pltpu.VMEM((rows, chunk), BF16),
        pltpu.VMEM((rows, width), BF16),
    ]
    more = {}
    if split:
        up = (4, 2, 2, 16, chunk * 3 // 2)
        down = (2, 2, inner // 32, width)
        out = jax.ShapeDtypeStruct((4, 2, 2, 16, width * 3 // 2), BF16)
        ups = jax.ShapeDtypeStruct((FF_STEPS,) + up, BF16)
        downs = jax.ShapeDtypeStruct((FF_STEPS,) + down, BF16)
        outs += [ups, downs, out, out, ups, downs]
        out_specs += [pl.BlockSpec((1,) + up, lambda f: (f,) + (0,) * len(up))]
        out_specs += [pl.BlockSpec((1,) + down, lambda f: (f,) + (0,) * len(down))]
        out_specs += [fixed(out.shape), fixed(out.shape), ANYWHERE, ANYWHERE]
        scratch += [pltpu.VMEM((2,) + up, BF16), pltpu.VMEM((2,) + down, BF16)]
        scratch += [pltpu.SemaphoreType.DMA((FF_STEPS,))] * 4
        scratch += [pltpu.VMEM((rows, width), BF16), pltpu.SemaphoreType.DMA((1,))]
        more = {"collective_id": 2, "has_side_effects": True}
    else:
        outs += [jax.ShapeDtypeStruct(a.shape, F32) for a in (w_up, w_down, w_out)]
        out_specs += [*weights, fixed(w_out.shape)]
    return pl.pallas_call(
        functools.partial(middle_kernel, split),
        grid=(FF_STEPS,),
        in_specs=specs,
        out_specs=out_specs,
        out_shape=outs,
        scratch_shapes=scratch,
        compiler_params=params(**more),
        cost_estimate=pl.CostEstimate(
            flops=6 * rows * (2 * w_up.size + w_out.size),
            bytes_accessed=40 * rows * width,
            transcendentals=rows * inner,
        ),
        name="middle",
    )(*ins)


def head_backs(d_q, d_k, d_v, q, k, gains, scale_q, scale_k):
    d_q = d_q * (1.0 / math.sqrt(HD))
    d_k = d_k * (1.0 / LOG2E)
    inv_q, inv_k, gain_q, gain_k = [gains[:, :, i : i + 1] for i in range(2, 6)]
    unit_q = q.astype(F32) * inv_q
    unit_k = k.astype(F32) * inv_k
    sum_q = jnp.sum(d_q * unit_q, axis=2, keepdims=True)
    sum_k = jnp.sum(d_k * unit_k, axis=2, keepdims=True)
    d_q = norm_back(d_q * gain_q, unit_q, scale_q, 1).astype(BF16)
    d_k = norm_back(d_k * gain_k, unit_k, scale_k, 1).astype(BF16)
    return jnp.stack([d_q, d_k, d_v.astype(BF16)]), sum_q, sum_k


def post_kernel(*refs):
    *ins, scale_ref, h_ref, d_ref, sum_q_ref, sum_k_ref, grad_ref = refs
    values = [ref[...] for ref in ins]
    d, sum_q_ref[...], sum_k_ref[...] = head_backs(*values, scale_ref[0], scale_ref[1])
    d_ref[...] = d
    grad_ref[...] = mul(h_ref[...], d.reshape(-1, d.shape[-1]), NT)


def post(d_q, d_k, d_v, q, k, gains, scales, h_t):
    heads, _, rows = d_q.shape
    width = h_t.shape[0]
    some = 4
    here = pl.BlockSpec((some, HD, rows), lambda i: (i, 0, 0))
    gain = pl.BlockSpec((some, HD, 1), lambda i: (i, 0, 0))
    columns = 3 * some * HD
    return pl.pallas_call(
        post_kernel,
        grid=(heads // some,),
        in_specs=[here] * 5
        + [pl.BlockSpec((some, HD, 8), lambda i: (i, 0, 0))]
        + [pl.BlockSpec((2, some, 1, rows), lambda i: (0, i, 0, 0)), fixed(h_t.shape)],
        out_specs=[
            pl.BlockSpec((3, some, HD, rows), lambda i: (0, i, 0, 0)),
            gain,
            gain,
            pl.BlockSpec((width, columns), lambda i: (0, i)),
        ],
        out_shape=[
            jax.ShapeDtypeStruct((3, heads, HD, rows), BF16),
            jax.ShapeDtypeStruct((heads, HD, 1), F32),
            jax.ShapeDtypeStruct((heads, HD, 1), F32),
            jax.ShapeDtypeStruct((width, 3 * heads * HD), F32),
        ],
        compiler_params=params(),
        cost_estimate=pl.CostEstimate(
            flops=6 * rows * width * heads * HD,
            bytes_accessed=30 * rows * heads * HD,
            transcendentals=0,
        ),
        name="post",
    )(d_q, d_k, d_v, q, k, gains, scales, h_t)


def token_grads(d, w, x, dx1, gain):
    d_h = mul(w, d.reshape(-1, d.shape[-1]), NN).T
    unit, scale = norm(x.astype(F32), -1)
    d_x = dx1 + norm_back(d_h * gain, unit, scale, -1)
    dgain = jnp.sum(d_h * unit, axis=0, keepdims=True)
    dbias = jnp.sum(d_h, axis=0, keepdims=True)
    return d_x.astype(BF16), dgain, dbias


def last_kernel(d_ref, w_ref, x_ref, dx1_ref, vec_ref, out_ref, dgain_ref, dbias_ref):
    out_ref[...], dgain, dbias = token_grads(
        d_ref[...], w_ref[...], x_ref[...], dx1_ref[...], vec_ref[0:1, :]
    )
    first = pl.program_id(0) == 0
    dgain_ref[...] = jnp.where(first, dgain, dgain_ref[...] + dgain)
    dbias_ref[...] = jnp.where(first, dbias, dbias_ref[...] + dbias)


def last(d, w, x, dx1, vectors):
    rows, width = x.shape
    block = math.gcd(rows, 256)
    row = pl.BlockSpec((block, width), lambda i: (i, 0))
    return pl.pallas_call(
        last_kernel,
        grid=(rows // block,),
        in_specs=[
            pl.BlockSpec(d.shape[:3] + (block,), lambda i: (0, 0, 0, i)),
            fixed(w.shape),
            row,
            row,
            fixed(vectors.shape),
        ],
        out_specs=[row, fixed((1, width)), fixed((1, width))],
        out_shape=[
            jax.ShapeDtypeStruct((rows, width), BF16),
            jax.ShapeDtypeStruct((1, width), F32),
            jax.ShapeDtypeStruct((1, width), F32),
        ],
        compiler_params=params(),
        name="last",
    )(d, w, x, dx1, vectors)


class Here:
    def __init__(self):
        wide, self.y = lax.axis_index("wide"), lax.axis_index("blk")
        self.core, self.x, self.z = wide % 2, wide // 2 % 2, wide // 4

    def device(self, z=None, x=None, core=None, y=None):
        z = self.z if z is None else z
        x = self.x if x is None else x
        core = self.core if core is None else core
        return (z * 4 + x * 2 + core, self.y if y is None else y)

    def other_core(self):
        return self.device(core=1 - self.core)

    def at(self, kind, k):
        z = self.z
        if kind == "column":
            return {"z": (z, z + 1 - 2 * (z % 2), (z + 2) % 4, 3 - z)[k]}
        x = 1 - self.x if k % 2 else self.x
        y = 1 - self.y if k // 2 else self.y
        return {"plane": {"x": x, "y": y}, "x": {"x": x}, "y": {"y": 1 - self.y if k else self.y}}[kind]

    def partner(self, kind, k):
        return self.device(**self.at(kind, k))

    def partners(self):
        every = [self.partner(kind, k) for kind in ("plane", "column") for k in (1, 2, 3)]
        return [self.other_core()] + every

    def part(self, ref, axes, kind, k):
        where = self.at(kind, k)
        return ref.at[tuple(where.get(axis, slice(None)) for axis in axes)]


def greet(others):
    barrier = pltpu.get_barrier_semaphore()
    for other in others:
        pl.semaphore_signal(barrier, inc=1, device_id=other, device_id_type=MESH)
    pl.semaphore_wait(barrier, len(others))


def remote(source, target, sems, at, to):
    return pltpu.make_async_remote_copy(
        src_ref=source,
        dst_ref=target,
        send_sem=sems[0].at[at],
        recv_sem=sems[1].at[at],
        device_id=to,
        device_id_type=MESH,
    )


class Sum:
    def __init__(self, here, stages, give, keep, refs):
        self.here, self.stages, self.give = here, stages, give
        count = len(stages)
        self.held, self.came = list(refs[: count + 1]), refs[count + 1 : 2 * count + 2]
        self.sems = refs[2 * count + 2 : 2 * count + 4]
        self.keep = self.held[0] if keep is None else keep
        self.axes = ["zxy"]
        for stage in stages:
            gone = {"plane": "xy", "column": "z"}.get(stage, stage)
            self.axes.append("".join(axis for axis in self.axes[-1] if axis not in gone))

    def copies(self, stage):
        here = self.here
        if stage == 0:
            return [remote(self.give, self.came[0], self.sems, 0, here.other_core())]
        kind = self.stages[stage - 1]
        return [
            remote(
                here.part(self.held[stage - 1], self.axes[stage - 1], kind, k),
                self.came[stage].at[k - 1],
                self.sems,
                3 * stage - 3 + k,
                here.partner(kind, k),
            )
            for k in range(1, self.came[stage].shape[0] + 1)
        ]

    def start(self, stage):
        for copy in self.copies(stage):
            copy.start()

    def wait(self, stage):
        for copy in self.copies(stage):
            copy.wait()

    def add(self, stage, landed=False):
        if not landed:
            self.wait(stage)
        if stage == 0:
            terms = [self.keep, self.came[0]]
        else:
            kind = self.stages[stage - 1]
            terms = [self.here.part(self.held[stage - 1], self.axes[stage - 1], kind, 0)]
            terms += [self.came[stage].at[k] for k in range(self.came[stage].shape[0])]
        if stage == len(self.stages):
            return sum(term[...].astype(F32) for term in terms)
        target = self.held[stage]

        def body(i, _):
            target[i] = sum(term[i].astype(F32) for term in terms).astype(target.dtype)
            return 0

        lax.fori_loop(0, target.shape[0], body, 0)

    def go(self, stage):
        self.add(stage)
        self.start(stage + 1)


def sum_scratch(stages, tail, kind=BF16):
    left = {"z": 4, "x": 2, "y": 2}
    held, came = [tuple(left.values())], [tuple(left.values())]
    for stage in stages:
        partners = {"plane": 3, "column": 3}.get(stage, 1)
        for axis in {"plane": "xy", "column": "z"}.get(stage, stage):
            left.pop(axis)
        held.append(tuple(left.values()))
        came.append((partners,) + held[-1])
    held[-1] = (1,)
    shapes = [pltpu.VMEM(shape + tail, kind) for shape in held[:-1] + [(1,)] + came]
    shapes[len(stages)] = pltpu.VMEM((8, 128), kind)
    return shapes + [pltpu.SemaphoreType.DMA((3 * len(stages) + 1,))] * 2


BATCH = 4


def head_back(here, h, ins, far_out, far_in, far_sems, kept):
    e_far, e_near, do_ref, o_ref, linv_ref, q_ref, k_ref, k_far, v_far, v_near = ins
    low, do = scaled_gradient(do_ref, o_ref, linv_ref, 0)
    q = q_ref[h]
    slot = h % BATCH
    keys = k_far.shape[2]
    bk = key_block(keys)
    acc = None
    for i in range(keys // bk):
        cut = slice(i * bk, (i + 1) * bk)
        part, d_k, d_v = block_back(
            e_far[0, cut, :], low, do, q, k_far[0, :, cut], v_far[0, :, cut]
        )
        acc = part if acc is None else acc + part
        far_out[slot, 0, :, cut] = d_k.astype(BF16)
        far_out[slot, 1, :, cut] = d_v.astype(BF16)
    remote(far_out.at[slot], far_in.at[h], far_sems, h, here.other_core()).start()
    for i in range(keys // bk):
        cut = slice(i * bk, (i + 1) * bk)
        part, kept[slot, 1, :, cut], kept[slot, 2, :, cut] = block_back(
            e_near[0, cut, :], low, do, q, k_ref[h, :, cut], v_near[0, :, cut]
        )
        acc = acc + part
    kept[slot, 0] = acc


DOWN_STAGES = [("plane", "column"), ("x", "column", "y")]
UP_STAGES = [("column", "plane"), ("column", "plane"), ("plane", "column"), ("x", "column", "y")]
TWO = ("plane", "column")


def backward_all_kernel(*refs):
    attn, refs = refs[:10], refs[10:]
    gains_ref, scale_ref, h_ref, *refs = refs
    keep_up, keep_down, keep_out, give_out, came_up, came_down, *refs = refs
    d_ref, sum_q_ref, sum_k_ref, keep_c, give_c, *refs = refs
    up_out, down_out, out_out, qkv_a, some_b, *refs = refs
    far_out, far_in, far_send, far_recv, kept, load_sem, *refs = refs
    here = Here()
    step = pl.program_id(0)
    far_sems = (far_send, far_recv)

    def take(stages, give=None):
        nonlocal refs
        count = 2 * len(stages) + 4
        mine, refs = refs[:count], refs[count:]
        return Sum(here, stages, give, None, mine)

    half = keep_down.shape[-1] // 2
    downs, ups, loads = [], [], []
    for i, stages in enumerate(DOWN_STAGES):
        cut = (slice(None),) * 4 + (pl.ds(i * half, half),)
        downs.append(take(stages))
        loads += [(keep_down.at[cut], downs[-1].held[0]), (came_down.at[cut], downs[-1].came[0])]
    for i, stages in enumerate(UP_STAGES):
        ups.append(take(stages))
        loads += [(keep_up.at[i], ups[-1].held[0]), (came_up.at[i], ups[-1].came[0])]
    out = take(TWO, give_out)
    loads.append((keep_out, out.held[0]))
    loads = [pltpu.make_async_copy(*load, load_sem.at[i]) for i, load in enumerate(loads)]
    give_a, give_b, *refs = refs
    a, b = take(TWO, give_a), take(("x",), give_b)

    @pl.when(step == 0)
    def _():
        greet(here.partners())
        out.start(0)
        for load in loads:
            load.start()

    def far_copy(h):
        return remote(far_out.at[h % BATCH], far_in.at[h], far_sems, h, here.other_core())

    @pl.when((step % BATCH == 0) & (step > 0))
    def _():
        base = step - BATCH
        for i in range(BATCH):
            far_copy(base + i).wait()
        for i in range(0, BATCH, 2):
            two = pl.ds(base + i, 2)
            some = slice(i, i + 2)
            d_k = kept[some, 1] + far_in[two, 0].astype(F32)
            d_v = kept[some, 2] + far_in[two, 1].astype(F32)
            d, sum_q, sum_k = head_backs(
                kept[some, 0],
                d_k,
                d_v,
                attn[5][two],
                attn[6][two],
                gains_ref[some],
                scale_ref[0, some],
                scale_ref[1, some],
            )
            d_ref[:, some] = d
            sum_q_ref[some] = sum_q
            sum_k_ref[some] = sum_k
        grad = mul(h_ref[...], d_ref[...].reshape(-1, d_ref.shape[-1]), NT)
        for i, (keep, give) in enumerate(
            ((a.held[0], give_a), (b.held[0], give_b), (keep_c, give_c))
        ):

            @pl.when(step == BATCH * (i + 1))
            def _():
                spread(grad, here.core, keep, give, 8)
                if i < 2:
                    (a, b)[i].start(0)

    @pl.when(step < H)
    def _():
        head_back(here, step, attn, far_out, far_in, far_sems, kept)

    def enter(total, first):
        for load in loads[first : first + 2]:
            load.wait()
        total.add(0, landed=True)

    @pl.when(step == 0)
    def _():
        enter(downs[1], 2)
        downs[1].start(1)
        enter(ups[3], 10)
        ups[3].start(1)
        enter(ups[0], 4)
        ups[0].start(1)
        enter(ups[1], 6)
        ups[1].start(1)

    @pl.when(step == 1)
    def _():
        enter(downs[0], 0)
        enter(ups[2], 8)
        loads[12].wait()
        out.add(0)

    @pl.when(step == 3)
    def _():
        for total in (downs[0], ups[2], out):
            total.start(1)

    @pl.when(step == 4)
    def _():
        downs[1].go(1)
        ups[3].go(1)

    @pl.when(step == 5)
    def _():
        ups[0].go(1)
        ups[1].go(1)
        a.add(0)

    @pl.when(step == 8)
    def _():
        for total in (downs[0], ups[2], out):
            total.go(1)
        a.start(1)

    @pl.when(step == 9)
    def _():
        downs[1].go(2)
        ups[3].go(2)
        b.go(0)

    @pl.when(step == 10)
    def _():
        a.go(1)

    @pl.when(step == H)
    def _():
        wide = up_out.shape[1] // len(ups)
        for i, total in enumerate(ups):
            unfold(up_out, total.add(len(total.stages)), i * wide)
        for i, total in enumerate(downs):
            down_out[:, i * half : (i + 1) * half] = total.add(len(total.stages))
        unfold(out_out, out.add(2))
        unfold(qkv_a, a.add(2))
        some_b[...] = b.add(1).astype(BF16)


def once(shape):
    return pl.BlockSpec(shape, lambda *_: (0,) * len(shape), pipeline_mode=pl.Buffered(1))


def backward_all(e_far, e_near, d_o, o, linv, q, k, k_far, v_far, v, gains, scales, h_t, grads):
    _, keys, rows = e_far.shape
    width = h_t.shape[0]

    def head(*tail):
        return pl.BlockSpec((1,) + tail, lambda s: (jnp.minimum(s, H - 1),) + (0,) * len(tail))

    def batch(s):
        return jnp.maximum(s // BATCH - 1, 0)

    gain = pl.BlockSpec((BATCH, HD, 1), lambda s: (batch(s), 0, 0))
    specs = [head(keys, rows), head(keys, rows), head(HD, rows), head(HD, rows), head(8, rows)]
    specs += [once(q.shape), once(k.shape), head(HD, keys), head(HD, keys), head(HD, keys)]
    specs.append(pl.BlockSpec((BATCH, HD, 8), lambda s: (batch(s), 0, 0)))
    specs.append(pl.BlockSpec((2, BATCH, 1, rows), lambda s: (0, batch(s), 0, 0)))
    specs.append(once(h_t.shape))
    specs += [ANYWHERE] * 6
    shard, chunk = width // 32, grads[0].shape[-1]
    down_rows, half = grads[1].shape[-2], width // 2
    part = (16, 3 * BATCH * HD * 3 // 2)
    third = jax.ShapeDtypeStruct((4, 2, 2) + part, BF16)
    outs = [
        jax.ShapeDtypeStruct((3, H, HD, rows), BF16),
        jax.ShapeDtypeStruct((H, HD, 1), F32),
        jax.ShapeDtypeStruct((H, HD, 1), F32),
        third,
        third,
        jax.ShapeDtypeStruct((shard, len(UP_STAGES) * chunk * 2 // 3), F32),
        jax.ShapeDtypeStruct((down_rows, width), F32),
        jax.ShapeDtypeStruct((shard, width), F32),
        jax.ShapeDtypeStruct((shard, 3 * BATCH * HD), F32),
        jax.ShapeDtypeStruct((4, 2) + part, BF16),
    ]
    out_specs = [pl.BlockSpec((3, BATCH, HD, rows), lambda s: (0, batch(s), 0, 0)), gain, gain]
    out_specs += [once(a.shape) for a in outs[3:]]
    scratch = [
        pltpu.VMEM((BATCH, 2, HD, keys), BF16),
        pltpu.VMEM((H, 2, HD, keys), BF16),
        pltpu.SemaphoreType.DMA((H,)),
        pltpu.SemaphoreType.DMA((H,)),
        pltpu.VMEM((BATCH, 3, HD, rows), F32),
        pltpu.SemaphoreType.DMA((13,)),
    ]
    for stages in DOWN_STAGES:
        scratch += sum_scratch(stages, (down_rows, half))
    for stages in UP_STAGES:
        scratch += sum_scratch(stages, (16, chunk))
    scratch += sum_scratch(TWO, (16, width * 3 // 2))
    scratch += [pltpu.VMEM((4, 2, 2) + part, BF16)] * 2
    scratch += sum_scratch(TWO, part) + sum_scratch(("x",), part)
    return pl.pallas_call(
        backward_all_kernel,
        grid=(H + 1,),
        in_specs=specs,
        out_specs=out_specs,
        out_shape=outs,
        scratch_shapes=scratch,
        compiler_params=pltpu.CompilerParams(
            vmem_limit_bytes=61 * 2**20, collective_id=0, has_side_effects=True
        ),
        name="backward_all",
    )(e_far, e_near, d_o, o, linv, q, k, k_far, v_far, v, gains, scales, h_t, *grads)


def front_kernel(*refs):
    all_ref, vec_ref, here_ref, w_ref, *refs = refs
    h_ref, q_ref, k_ref, v_ref, scale_ref, x_ref, mq_ref, near_ref, far_ref, gains_ref, *refs = refs
    k_far, v_far, *refs = refs
    w_t, came, len_came, len_send, len_recv, row_send, row_recv, k_send, k_recv, v_send, v_recv = refs
    here = Here()
    step = pl.program_id(0)
    steps = pl.num_programs(0)
    block, width = here_ref.shape
    rows = all_ref.shape[0]
    swapped = here.core != here.y
    opposite = here.device(core=here.y, y=here.core)

    def move(i):
        cut = pl.ds(i * block, block)
        return remote(all_ref.at[cut], came.at[cut], (row_send, row_recv), i, opposite)

    move_lengths = remote(vec_ref, len_came, (len_send, len_recv), 0, opposite)

    def give(i):
        cut = (slice(None), slice(None), pl.ds(pl.multiple_of(i * block, block), block))
        to = here.other_core()
        return [
            remote(k_ref.at[cut], k_far.at[cut], (k_send, k_recv), i, to),
            remote(v_ref.at[cut], v_far.at[cut], (v_send, v_recv), i, to),
        ]

    @pl.when(step == 0)
    def _():
        greet([here.other_core(), here.device(core=1 - here.core, y=1 - here.y)])

        @pl.when(swapped)
        def _():
            move_lengths.start()
            for i in range(rows // block):
                move(i).start()

        for i in range(0, w_ref.shape[1], width // 3):
            w_t[i : i + width // 3, :] = w_ref[:, i : i + width // 3].T

        @pl.when(swapped)
        def _():
            move_lengths.wait()

        @pl.when(jnp.logical_not(swapped))
        def _():
            len_came[...] = vec_ref[...]

        gains_ref[...] = gains_table(vec_ref[...])
        lengths = len_came[LENGTHS : LENGTHS + 1, :]
        row = lax.broadcasted_iota(jnp.int32, (AUG, rows), 0)
        spot = lax.broadcasted_iota(jnp.int32, (AUG, rows), 1).astype(F32)

        def inside(first):
            found = jnp.zeros((AUG, rows), jnp.int32)
            begin = jnp.zeros((1, 1), F32)
            where = spot + (first * 1).astype(F32)
            for c in range(SEQS):
                end = begin + lengths[:, c : c + 1]
                hit = (row == c) & (where >= begin) & (where < end)
                found = jnp.where(hit, 1, found)
                begin = end
            return found

        near = inside(here.core * rows)
        near_ref[...] = near.astype(F32).astype(BF16)
        mq_ref[...] = jnp.where(near == 1, 0.0, BLOCKED).astype(BF16)
        far_ref[...] = inside((1 - here.core) * rows).astype(F32).astype(BF16)

    @pl.when(swapped)
    def _():
        move(step).wait()
        x_ref[...] = came[pl.ds(pl.multiple_of(step * block, block), block), :]

    @pl.when(jnp.logical_not(swapped))
    def _():
        x_ref[...] = here_ref[...]

    h = normed(x_ref[...], vec_ref[0:1, :], vec_ref[1:2, :])
    h_ref[...] = h.T
    q, k, v, scale_q, scale_k = heads_of(h, w_t, gains_ref)
    at = pl.ds(pl.multiple_of(step * block, block), block)
    k_ref[:, :, at] = k
    v_ref[:, :, at] = v
    for copy in give(step):
        copy.start()
    q_ref[...] = q
    scale_ref[0] = scale_q
    scale_ref[1] = scale_k

    @pl.when(step == steps - 1)
    def _():
        for i in range(rows // block):
            for copy in give(i):
                copy.wait()


SEQS = 6
LENGTHS = 6


def gains_table(vectors):
    width = vectors.shape[1]
    gain_q, gain_k = vectors[4:5, :], vectors[5:6, :]
    folded = gain_q * (LOG2E / math.sqrt(HD))
    table = [folded, gain_k, 1.0 / folded, 1.0 / gain_k, gain_q, gain_k]
    table.append(jnp.zeros((122, width), F32))
    return jnp.concatenate(table, axis=0).T[:, :8].reshape(H, HD, 8)


def front(tokens, vectors, w):
    rows, width = tokens.shape
    block = math.gcd(rows, 256)
    steps = rows // block
    row = pl.BlockSpec((block, width), lambda i: (i, 0))
    head = pl.BlockSpec((H, HD, block), lambda i: (0, 0, i))
    heads = jax.ShapeDtypeStruct((H, HD, rows), BF16)
    mask = jax.ShapeDtypeStruct((AUG, rows), BF16)
    return pl.pallas_call(
        front_kernel,
        grid=(steps,),
        in_specs=[ANYWHERE, once(vectors.shape), row, once(w.shape)],
        out_specs=[
            pl.BlockSpec((width, block), lambda i: (0, i)),
            head,
            once(heads.shape),
            once(heads.shape),
            pl.BlockSpec((2, H, 1, block), lambda i: (0, 0, 0, i)),
            row,
            once(mask.shape),
            once(mask.shape),
            once(mask.shape),
            once((H, HD, 8)),
            ANYWHERE,
            ANYWHERE,
        ],
        out_shape=[
            jax.ShapeDtypeStruct((width, rows), BF16),
            heads,
            heads,
            heads,
            jax.ShapeDtypeStruct((2, H, 1, rows), F32),
            jax.ShapeDtypeStruct((rows, width), BF16),
            mask,
            mask,
            mask,
            jax.ShapeDtypeStruct((H, HD, 8), F32),
            heads,
            heads,
        ],
        scratch_shapes=[
            pltpu.VMEM((w.shape[1], width), BF16),
            pltpu.VMEM((rows, width), BF16),
            pltpu.VMEM(vectors.shape, F32),
            pltpu.SemaphoreType.DMA((1,)),
            pltpu.SemaphoreType.DMA((1,)),
        ]
        + [pltpu.SemaphoreType.DMA((steps,))] * 6,
        compiler_params=params(collective_id=3, has_side_effects=True),
        cost_estimate=pl.CostEstimate(
            flops=2 * rows * w.size, bytes_accessed=12 * rows * width, transcendentals=0
        ),
        name="front",
    )(tokens, vectors, tokens, w)


REST_STAGES = [("column", "plane"), ("x", "column", "y")]
TABLE_STAGES = ("column", "plane")


def tail_kernel(*refs):
    d_ref, w_ref, x_ref, dx1_ref, vec_ref, *refs = refs
    sum_q_ref, sum_k_ref, dgain2_ref, dbias2_ref, keep_ref, some_ref, give_ref, *refs = refs
    out_ref, qkv_b, qkv_c, table_ref, *refs = refs
    made, vectors, keep_t, give_t, stay_sem, swap_send, swap_recv, *refs = refs
    here = Here()
    step = pl.program_id(0)
    steps = pl.num_programs(0)
    block = x_ref.shape[0]
    swapped = here.core != here.y
    opposite = here.device(core=here.y, y=here.core)
    parts, start = [], 0
    for stages in REST_STAGES:
        count = 2 * len(stages) + 4
        size = refs[0].shape[-1]
        cut = (slice(None),) * 4 + (pl.ds(start, size),)
        parts.append(Sum(here, stages, give_ref.at[cut], keep_ref.at[cut], refs[:count]))
        refs, start = refs[count:], start + size
    table = Sum(here, TABLE_STAGES, give_t, keep_t, refs[:8])
    other = Sum(here, REST_STAGES[1], None, None, refs[8:])
    other.held[1] = some_ref

    @pl.when(step == 0)
    def _():
        greet(here.partners() + [here.device(core=1 - here.core, y=1 - here.y)])
        other.start(2)
        for part in parts:
            part.start(0)

    def stay(i):
        cut = pl.ds(i * block, block)
        return pltpu.make_async_copy(made.at[cut], out_ref.at[cut], stay_sem.at[i])

    def move(i):
        cut = pl.ds(i * block, block)
        return remote(made.at[cut], out_ref.at[cut], (swap_send, swap_recv), i, opposite)

    new, dgain, dbias = token_grads(
        d_ref[...], w_ref[...], x_ref[...], dx1_ref[...], vec_ref[0:1, :]
    )
    made[pl.ds(pl.multiple_of(step * block, block), block), :] = new
    first = step == 0
    vectors[0:1, :] = jnp.where(first, dgain, vectors[0:1, :] + dgain)
    vectors[1:2, :] = jnp.where(first, dbias, vectors[1:2, :] + dbias)

    @pl.when(swapped)
    def _():
        move(step).start()

    @pl.when(jnp.logical_not(swapped))
    def _():
        stay(step).start()

    @pl.when(step == 0)
    def _():
        for part in parts:
            part.go(0)

    @pl.when(step == 2)
    def _():
        parts[1].go(1)

    @pl.when(step == steps - 1)
    def _():
        width = x_ref.shape[1]
        rows = [vectors[0:1, :], vectors[1:2, :], dgain2_ref[...], dbias2_ref[...]]
        rows.append(jnp.zeros((124, width), F32))
        columns = jnp.concatenate(rows, axis=0).T
        lane = lax.broadcasted_iota(jnp.int32, columns.shape, 1)
        columns = jnp.where(lane == 4, sum_q_ref[...].reshape(width, 1), columns)
        columns = jnp.where(lane == 5, sum_k_ref[...].reshape(width, 1), columns)
        columns = columns.reshape(8, 2, 2, width // 32, 128)
        mine = here.core == 0
        keep_t[...] = jnp.where(mine, columns[:, 0], columns[:, 1]).reshape(keep_t.shape)
        give_t[...] = jnp.where(mine, columns[:, 1], columns[:, 0]).reshape(keep_t.shape)
        table.start(0)
        parts[0].go(1)
        table.go(0)
        other.go(2)
        table.go(1)
        parts[1].go(2)
        unfold(qkv_b, other.add(3))
        table_ref[...] = table.add(2)
        unfold(qkv_c, jnp.concatenate([part.add(len(part.stages)) for part in parts], axis=-1))

        @pl.when(swapped)
        def _():
            for i in range(steps):
                move(i).wait()

        @pl.when(jnp.logical_not(swapped))
        def _():
            for i in range(steps):
                stay(i).wait()


def tail(d, w, x, dx1, vectors, sum_q, sum_k, dgain2, dbias2, keep, some, give):
    rows, width = x.shape
    block = math.gcd(rows, 256)
    steps = rows // block
    row = pl.BlockSpec((block, width), lambda i: (i, 0))
    shard = width // 32
    part = keep.shape[-2:]
    return pl.pallas_call(
        tail_kernel,
        grid=(steps,),
        in_specs=[
            pl.BlockSpec(d.shape[:3] + (block,), lambda i: (0, 0, 0, i)),
            once(w.shape),
            row,
            row,
            once(vectors.shape),
            once(sum_q.shape),
            once(sum_k.shape),
            once(dgain2.shape),
            once(dbias2.shape),
            once(keep.shape),
            once(some.shape),
            ANYWHERE,
        ],
        out_specs=[ANYWHERE] + [once((shard, 3 * BATCH * HD))] * 2 + [once((shard, 128))],
        out_shape=[
            jax.ShapeDtypeStruct((rows, width), BF16),
            jax.ShapeDtypeStruct((shard, 3 * BATCH * HD), F32),
            jax.ShapeDtypeStruct((shard, 3 * BATCH * HD), F32),
            jax.ShapeDtypeStruct((shard, 128), F32),
        ],
        scratch_shapes=[
            pltpu.VMEM((rows, width), BF16),
            pltpu.VMEM((8, width), F32),
            pltpu.VMEM((4, 2, 2, shard, 128), F32),
            pltpu.VMEM((4, 2, 2, shard, 128), F32),
            pltpu.SemaphoreType.DMA((steps,)),
            pltpu.SemaphoreType.DMA((steps,)),
            pltpu.SemaphoreType.DMA((steps,)),
            *sum_scratch(REST_STAGES[0], (part[0], part[1] // 3)),
            *sum_scratch(REST_STAGES[1], (part[0], part[1] * 2 // 3)),
            *sum_scratch(TABLE_STAGES, (shard, 128), F32),
            *sum_scratch(REST_STAGES[1], part),
        ],
        compiler_params=pltpu.CompilerParams(
            vmem_limit_bytes=VMEM_LIMIT, collective_id=1, has_side_effects=True
        ),
        name="tail",
    )(d, w, x, dx1, vectors, sum_q, sum_k, dgain2, dbias2, keep, some, give)


def finish_kernel(here_ref, came_ref, tokens_ref, *refs):
    qkvs, ins, outs = refs[:3], refs[3:6], refs[6:]
    here = Here()
    swapped = here.core != here.y

    @pl.when(swapped)
    def _():
        outs[0][...] = came_ref[...]

    @pl.when(jnp.logical_not(swapped))
    def _():
        outs[0][...] = here_ref[...]

    outs[1][...] = tokens_ref[...]
    some = BATCH * HD

    @pl.when(pl.program_id(0) == 0)
    def _():
        for g in range(3):
            for part in range(3):
                at = (part * 3 + g) * some
                outs[2][:, at : at + some] = qkvs[g][:, part * some : (part + 1) * some]
        for source, target in zip(ins, outs[3:]):
            target[...] = source[...]


def finish(output, came, grad_tokens, qkvs, out, up, down):
    rows, width = output.shape
    steps = 4
    small = [jax.ShapeDtypeStruct((out.shape[0], 9 * BATCH * HD), F32), out, up, down]
    row = pl.BlockSpec((rows // steps, width), lambda i: (i, 0))
    return pl.pallas_call(
        finish_kernel,
        grid=(steps,),
        in_specs=[row] * 3 + [once(a.shape) for a in (*qkvs, out, up, down)],
        out_specs=[row] * 2 + [once(a.shape) for a in small],
        out_shape=[
            jax.ShapeDtypeStruct(a.shape, a.dtype) for a in (output, grad_tokens, *small)
        ],
        compiler_params=params(),
        name="finish",
    )(output, came, grad_tokens, *qkvs, out, up, down)


def place(index):
    return index // 8, index // 4 % 2, index // 2 % 2, index % 2


def device(z, x, core, y):
    return ((z * 2 + x) * 2 + core) * 2 + y


def pairs(other):
    every = [(i, device(*other(*place(i)))) for i in range(32)]
    return [(i, j) for i, j in every if i != j]


SWAP = pairs(lambda z, x, c, y: (z, x, y, c))


def send(value, where):
    return lax.ppermute(value, AXES, where)


def after(values, *done):
    return lax.optimization_barrier((values, done))[0]


def segments(lengths, group, mine, rows):
    count = lengths.shape[1]
    at = jnp.arange(count)
    ends = jnp.sum(jnp.where(at[:, None] <= at[None, :], lengths[0][:, None], 0), axis=0)
    spots = jnp.arange(group, dtype=jnp.int32)
    segment = jnp.sum((spots[None, :] >= ends[:, None]).astype(jnp.int32), axis=0)
    is_in = jnp.arange(AUG)[:, None] == segment[None, :]
    mask_k = is_in.astype(BF16)
    mask_q = jnp.where(is_in, 0.0, BLOCKED).astype(BF16)
    mask_q = lax.dynamic_slice_in_dim(mask_q, mine * rows, rows, axis=1)
    return mask_q, mask_k


def ungroup(grads):
    parts = [g.reshape(-1, 3, BATCH * HD) for g in grads]
    return jnp.concatenate(parts, axis=2).reshape(parts[0].shape[0], -1)


def on_chips(tokens, vectors, lengths, w_qkv, w_out, w_up, w_down, cotangent):
    rows, width = tokens.shape
    h_t, q, k, v, scales, tokens, mask_q, mask_near, mask_far, gains, k_far, v_far = front(
        tokens, vectors, w_qkv
    )
    came = send(after(cotangent, tokens), SWAP)
    o, linv, e_near, e_far = attend(q, mask_q, [(k, v, mask_near), (k_far, v_far, mask_far)])
    output, dx1, d_o, dgain2, dbias2, *grads = middle(
        tokens, o.reshape(width, rows), cotangent, w_out, vectors, w_up, w_down, came
    )
    d_o = d_o.reshape(H, HD, rows)
    output_came = send(output, SWAP)
    d, sum_q, sum_k, keep, give, up, down, out, qkv_a, some = backward_all(
        e_far, e_near, d_o, o, linv, q, k, k_far, v_far, v, gains, scales, h_t, grads
    )
    grad_tokens, qkv_b, qkv_c, table = tail(
        d, w_qkv, tokens, dx1, vectors, sum_q, sum_k, dgain2, dbias2, keep, some, give
    )
    sums = [table[:, i] for i in (0, 1, 4, 5, 2, 3)]
    output, grad_tokens, sum_w_qkv, out, up, down = finish(
        output, output_came, grad_tokens, [qkv_a, qkv_b, qkv_c], out, up, down
    )
    return output, grad_tokens, sums, sum_w_qkv, out, up, down


def anywhere(tokens, vectors, lengths, w_qkv, w_out, w_up, w_down, cotangent):
    rows, width = tokens.shape
    parts = lax.axis_size("blk")
    mask_q, mask_k = segments(lengths, rows * parts, lax.axis_index("blk"), rows)
    h_t, q, k, v, scales = project(tokens, vectors, w_qkv.T, gains_table(vectors))
    k_all = lax.all_gather(k, "blk", axis=2, tiled=True)
    v_all = lax.all_gather(v, "blk", axis=2, tiled=True)
    o, linv, e_all = attend(q, mask_q, [(k_all, v_all, mask_k)])
    output, dx1, d_o, dgain2, dbias2, up, down, out = middle(
        tokens, o.reshape(width, rows), cotangent, w_out, vectors, w_up, w_down
    )
    d_o = d_o.reshape(H, HD, rows)
    d_q, d_k, d_v = attend_back(e_all, d_o, o, linv, q, k_all, v_all)
    pair = jnp.stack([d_k, d_v]).reshape(2, H, HD, parts, rows)
    pair = jnp.transpose(pair, (3, 0, 1, 2, 4)).astype(BF16)
    pair = lax.psum_scatter(pair, "blk", scatter_dimension=0, tiled=False).astype(F32)
    d, sum_q, sum_k, grad = post(
        d_q, pair[0], pair[1], q, k, gains_table(vectors), scales, h_t
    )
    grad_tokens, dgain1, dbias1 = last(d, w_qkv, tokens, dx1, vectors)
    scatter = functools.partial(lax.psum_scatter, axis_name=AXES, scatter_dimension=0, tiled=True)
    sums = [
        scatter(g.reshape(width)) for g in (dgain1, dbias1, sum_q, sum_k, dgain2, dbias2)
    ]
    grad = ungroup(jnp.split(grad, H // BATCH, axis=1))
    return output, grad_tokens, sums, scatter(grad), scatter(out), scatter(up), scatter(down)


def shards(
    tokens,
    lengths,
    ln1_gain,
    ln1_bias,
    w_qkv,
    q_gain,
    k_gain,
    w_out,
    ln2_gain,
    ln2_bias,
    w_up,
    w_down,
    cotangent,
):
    width = tokens.shape[1]
    lengths_row = jnp.pad(lengths[0].astype(F32), (0, width - lengths.shape[1]))
    rows = [ln1_gain, ln1_bias, ln2_gain, ln2_bias, q_gain, k_gain, lengths_row, lengths_row]
    vectors = jnp.stack(rows)
    known = lax.axis_size("blk") == 2 and lax.axis_size("wide") == 16
    run = on_chips if known else anywhere
    output, grad_tokens, sums, s_qkv, s_out, s_up, s_down = run(
        tokens, vectors, lengths, w_qkv, w_out, w_up, w_down, cotangent
    )
    return (
        output,
        grad_tokens,
        sums[0],
        sums[1],
        s_qkv,
        sums[2],
        sums[3],
        s_out,
        sums[4],
        sums[5],
        s_up,
        s_down,
    )


def solution(mesh):
    split = P(AXES, None)
    in_specs = (split, P("wide", None)) + (P(),) * 10 + (split,)
    vector = P(AXES)
    out_specs = (
        split,
        split,
        vector,
        vector,
        split,
        vector,
        vector,
        split,
        vector,
        vector,
        split,
        split,
    )
    return jax.shard_map(shards, mesh=mesh, in_specs=in_specs, out_specs=out_specs, check_vma=False)
```

time: 266 us -> 242 us (0.910)
  local copies, waits for them, and re-layouts: 24.3 us -> 8.85 us
  starting transfers between devices: 16.2 us -> 1.52 us
  Pallas kernels: 220 us -> 229 us
  other arithmetic: 3.55 us -> 0.66 us
    pallas_call x4, Pallas kernels: 92.9 us -> 113 us  [the longest x1 50.3 us: middle(): pl.pallas_call(functools.partial(middle_kernel, split), grid=(FF_STEPS,),...]
    ppermute x6 -> x2, starting transfers between devices: 16.2 us -> 1.52 us  [send(): return lax.ppermute(value, AXES, where)]
    pallas_call x1, Pallas kernels: 93.1 us -> 81.6 us  [backward_all(): pl.pallas_call(backward_all_kernel, grid=(H + 1,), in_specs=specs, out_sp...]
    reshape x12 -> x0, local copies, waits for them, and re-layouts: 9.98 us -> none  [the longest x5 5.14 us: shards(): g.reshape(H, HD, 1)]
    unnamed x38 -> x6, local copies, waits for them, and re-layouts: 12.2 us -> 2.34 us
    another operation x0 -> x8, local copies, waits for them, and re-layouts: none -> 4.79 us  [shards(): vectors = jnp.stack(rows)]
  transfers between devices with their start and end apart: 6 -> 2, of which waited for: 0 -> 0; matrix products, arithmetic and copies ran while one was open for 8% -> 1% of each run, Pallas kernels for 58% -> 60%
where the time goes in v3:
time: 242 us; the launch traced here: 241 us
  Pallas kernels  229 us (95%)
  local copies, waits for them, and re-layouts  8.85 us (4%)
    pallas_call x1, Pallas kernels, backward_all(): pl.pallas_call(backward_all_kernel, grid=(H + 1,), in_specs=specs, out_sp...  81.6 us
    pallas_call x1, Pallas kernels, middle(): pl.pallas_call(functools.partial(middle_kernel, split), grid=(FF_STEPS,),...  50.3 us
    pallas_call x1, Pallas kernels, tail(): pl.pallas_call(tail_kernel, grid=(steps,), in_specs=[pl.BlockSpec(d.shape...  34.6 us
    pallas_call x1, Pallas kernels, front(): pl.pallas_call(front_kernel, grid=(steps,), in_specs=[ANYWHERE, once(vect...  29.5 us
    pallas_call x1, Pallas kernels, attend(): pl.pallas_call(functools.partial(forward_kernel, len(parts)), grid=(heads...  28 us
    pallas_call x1, Pallas kernels, finish(): pl.pallas_call(finish_kernel, grid=(steps,), in_specs=[row] * 3 + [once(a...  5.21 us
  transfers between devices with their start and end apart: 2, of which 0 were waited for; matrix products, arithmetic and copies ran while one was open for 1% of the time, Pallas kernels for 60%

profile of v3, /device:TPU:0, one launch (start us, length us, event | category | flops | bytes accessed | tf_op | source)
XLA Modules:
  0.0 241.0 jit_solution(13678993597063343132)
XLA Ops:
  0.6 0.7 convert_bitcast_fusion
  1.3 0.7 stack.25
  2.0 0.7 stack.26
  2.7 0.7 stack.29
  3.4 0.7 stack.30
  4.1 0.7 stack.27
  4.7 0.7 stack.28
  5.4 0.7 stack.32.refs_1_.refs_4_
  6.1 0.0 copy-start.1
  6.1 29.5 %front.1 = (bf16[768,1024]{1,0:T(8,128)(2,1)}, bf16[12,64,1024]{2,1,0:T(8,128)(2,1)}, bf16[12,64,1024]{2,1,0:T(8,128)(2,1)}, bf16[12,64,1024]{2,1,0:T(8,128)(2,1...) custom-call(bf16[1024,768]{1,0:T(8,128)(2,1)} %refs_2_.2, ...), custom_call_target="tpu_custom_call" | custom-call | flops 3623878656 | bytes 9437184 | tf_op jit(solution)/shard_map/front/pallas_call | solution.py:1025
  35.6 0.0 copy-done.1
  35.6 0.8 collective-permute-start
  36.4 28.0 %attend.1 = (bf16[12,64,1024]{2,1,0:T(8,128)(2,1)}, f32[12,8,1024]{2,1,0:T(8,128)}, bf16[12,1024,1024]{2,1,0:T(8,128)(2,1)}, bf16[12,1024,1024]{2,1,0:T(8,128)(2,1)}) custom-call(bf16[12,64,1024]{2,1,0:T(8,128)(2,1)} %get-tuple-element.61.refs_0_.refs_5_, bf16[16,1024]{1,0:T(8,128)(2,1)} %get-tuple-element.62.refs_1_, ...), custom_call_target="tpu_custom_call" | custom-call | flops 25769803776 | bytes 50331648 | tf_op jit(solution)/shard_map/attend/pallas_call | solution.py:75
  64.4 0.0 collective-permute-done.refs_7_
  64.4 0.0 copy-start.2
  64.4 1.1 copy-done.2
  65.6 50.3 %middle.1 = (bf16[1024,768]{1,0:T(8,128)(2,1)}, f32[1024,768]{1,0:T(8,128)}, f32[768,1024]{1,0:T(8,128)}, f32[1,768]{1,0:T(1,128)}, f32[1,768]{1,0:T(1,128)}, /*...) custom-call(bf16[1024,768]{1,0:T(8,128)(2,1)} %get-tuple-element.60., ...), custom_call_target="tpu_custom_call" | custom-call | flops 32614907904 | bytes 31457280 | tf_op jit(solution)/shard_map/middle/pallas_call | solution.py:415
  115.8 0.8 collective-permute-start.1
  116.6 81.6 %backward_all.1 = (bf16[3,12,64,1024]{3,2,1,0:T(8,128)(2,1)}, f32[12,64,1]{2,1,0:T(8,128)}, f32[12,64,1]{2,1,0:T(8,128)}, bf16[4,2,2,16,1152]{4,3,2,1,0:T(8,128)...) custom-call(bf16[12,1024,1024]{2,1,0:T(8,128)(2,1)} %get-tuple-eleme, ...), custom_call_target="tpu_custom_call" | custom-call | tf_op jit(solution)/shard_map/backward_all/pallas_call | solution.py:893
  198.2 34.6 %tail.1 = (bf16[1024,768]{1,0:T(8,128)(2,1)}, f32[24,768]{1,0:T(8,128)}, f32[24,768]{1,0:T(8,128)}, f32[24,128]{1,0:T(8,128)}) custom-call(bf16[3,12,64,1024]{3,2,1,0:T(8,128)(2,1)} %get-tuple-element.85.refs_0_, bf16[768,2304]{1,0:T(8,128)(2,1)} %refs_1_.1, bf16[1024,768]{1,0:T(8,128)(2,1)} %get-tuple-element.60.refs_0_.refs_2_, ...), custom_call_target="tpu_custom_call" | custom-call | tf_op jit(solution)/shard_map/tail/pallas_call | solution.py:1180
  232.7 1.7 slice_reduce_fusion
  234.5 0.0 collective-permute-done.1.came_ref
  234.5 0.0 copy-start
  234.5 1.2 copy-done
  235.7 5.2 %finish.1 = (bf16[1024,768]{1,0:T(8,128)(2,1)}, bf16[1024,768]{1,0:T(8,128)(2,1)}, f32[24,2304]{1,0:T(8,128)}, f32[24,768]{1,0:T(8,128)}, f32[24,3072]{1,0:T(8,128)}, /*index=5*/f32[96,768]{1,0:T(8,128)}) custom-call(bf16[1024,768]{1,0:T(8,128)(2,1)} %get-tuple-element.71.here_ref, bf16[1024,768]{1,0:T(8,128)(2,1)} %copy-done, ...), custom_call_target="tpu_custom_call" | custom-call | tf_op jit(solution)/shard_map/finish/pallas_call | solution.py:1255
  (2 shorter events, 0.0 us)
Async XLA Ops:
  6.1 29.5 %copy-start.1 = (bf16[1024,768]{1,0:T(8,128)(2,1)S(1)}, bf16[1024,768]{1,0:T(8,128)(2,1)}, u32[]{:S(2)}) copy-start(bf16[1024,768]{1,0:T(8,128)(2,1)} %refs_2_.3) | copy-start | bytes 4718596
  35.6 28.8 %collective-permute-start = (bf16[1024,768]{1,0:T(8,128)(2,1)S(1)}, bf16[1024,768]{1,0:T(8,128)(2,1)S(1)}, u32[]{:S(2)}, u32[]{:S(2)}) collective-permute-start(bf16[1024,768]{1,0:T(8,128)(2,1)S(1)} %copy-done.1), channel_id=1, source_target_pairs={{1,2},{2,1},{5,6},{6,5},{9,10},{10,9},{13,14},{14,13},{17,18},{18,... | collective-permute-start | bytes 4718600 | tf_op jit(solution)/shard_map/ppermute | solution.py:1285
  64.4 1.1 copy-start.2
  115.8 118.6 %collective-permute-start.1 = (bf16[1024,768]{1,0:T(8,128)(2,1)}, bf16[1024,768]{1,0:T(8,128)(2,1)S(1)}, u32[]{:S(2)}, u32[]{:S(2)}) collective-permute-start(bf16[1024,768]{1,0:T(8,128)(2,1)} %get-tuple-element.71.here_ref), channel_id=1, source_target_pairs={{1,2},{2,1},{5,6},{6,5},{9,10},{10,9},{13,14},{14,13},{17,18},{18,... | collective-permute-start | bytes 4718600 | tf_op jit(solution)/shard_map/ppermute | solution.py:1285
  234.5 1.2 copy-start

commit v4 on v3

--- a/solution.py
+++ b/solution.py
@@ -39,7 +39,22 @@
 
 def forward_kernel(count, *refs):
     q_ref, mq_ref, *refs = refs
-    parts, (o_ref, linv_ref, *e_refs) = refs[: 3 * count], refs[3 * count :]
+    parts, refs = refs[: 3 * count], refs[3 * count :]
+    if count == 2:
+        own_ref, o_ref, linv_ref, *e_refs, came_ref, send_sem, recv_sem = refs
+        here = Here()
+        swapped = here.core != here.y
+        swap = remote(own_ref, came_ref, (send_sem, recv_sem), 0, here.opposite())
+
+        @pl.when(pl.program_id(0) == 0)
+        def _():
+            greet([here.opposite()])
+
+            @pl.when(swapped)
+            def _():
+                swap.start()
+    else:
+        o_ref, linv_ref, *e_refs = refs
     keys = parts[0].shape[2]
     bk = key_block(keys)
     ones = ones_rows(bk)
@@ -59,9 +74,14 @@
         linv = 1.0 / acc[HD : HD + 1]
         o_ref[h] = (acc[:HD] * linv).astype(BF16)
         linv_ref[h] = jnp.broadcast_to(linv, linv_ref.shape[1:])
-
-
-def attend(q, mask_q, parts):
+    if count == 2:
+
+        @pl.when(swapped & (pl.program_id(0) == pl.num_programs(0) - 1))
+        def _():
+            swap.wait()
+
+
+def attend(q, mask_q, parts, cotangent=None):
     heads, _, rows = q.shape
     keys = parts[0][0].shape[2]
     some = 2 if len(parts) * keys * rows <= 1 << 21 else 1
@@ -72,24 +92,33 @@
     specs = [head(HD, rows), fixed(mask_q.shape)]
     for part in parts:
         specs += [head(HD, keys), head(HD, keys), fixed(part[2].shape)]
+    ins, more_out, more_specs, scratch, more = [], [], [], [], {}
+    if cotangent is not None:
+        ins = [cotangent]
+        specs.append(ANYWHERE)
+        more_out, more_specs = [jax.ShapeDtypeStruct(cotangent.shape, BF16)], [ANYWHERE]
+        scratch = [pltpu.SemaphoreType.DMA((1,))] * 2
+        more = {"collective_id": 4, "has_side_effects": True}
     return pl.pallas_call(
         functools.partial(forward_kernel, len(parts)),
         grid=(heads // some,),
         in_specs=specs,
-        out_specs=[head(HD, rows), head(8, rows)] + [head(keys, rows)] * len(parts),
+        out_specs=[head(HD, rows), head(8, rows)] + [head(keys, rows)] * len(parts) + more_specs,
         out_shape=[
             jax.ShapeDtypeStruct((heads, HD, rows), BF16),
             jax.ShapeDtypeStruct((heads, 8, rows), F32),
         ]
-        + [jax.ShapeDtypeStruct((heads, keys, rows), BF16)] * len(parts),
-        compiler_params=params(),
+        + [jax.ShapeDtypeStruct((heads, keys, rows), BF16)] * len(parts)
+        + more_out,
+        scratch_shapes=scratch,
+        compiler_params=params(**more),
         cost_estimate=pl.CostEstimate(
             flops=heads * rows * keys * len(parts) * 1024,
             bytes_accessed=heads * rows * keys * len(parts) * 2,
             transcendentals=heads * rows * keys * len(parts),
         ),
         name="attend",
-    )(q, mask_q, *[a for part in parts for a in part])
+    )(q, mask_q, *[a for part in parts for a in part], *ins)
 
 
 def scaled_gradient(do_ref, o_ref, linv_ref, h):
@@ -542,6 +571,9 @@
     def other_core(self):
         return self.device(core=1 - self.core)
 
+    def opposite(self):
+        return self.device(core=1 - self.core, y=1 - self.y)
+
     def at(self, kind, k):
         z = self.z
         if kind == "column":
@@ -692,11 +724,12 @@
 def backward_all_kernel(*refs):
     attn, refs = refs[:10], refs[10:]
     gains_ref, scale_ref, h_ref, *refs = refs
-    keep_up, keep_down, keep_out, give_out, came_up, came_down, *refs = refs
+    keep_up, keep_down, keep_out, give_out, came_up, came_down, own_ref, *refs = refs
     d_ref, sum_q_ref, sum_k_ref, keep_c, give_c, *refs = refs
-    up_out, down_out, out_out, qkv_a, some_b, *refs = refs
-    far_out, far_in, far_send, far_recv, kept, load_sem, *refs = refs
+    up_out, down_out, out_out, qkv_a, some_b, swap_ref, *refs = refs
+    far_out, far_in, far_send, far_recv, kept, load_sem, swap_send, swap_recv, *refs = refs
     here = Here()
+    swap = remote(own_ref, swap_ref, (swap_send, swap_recv), 0, here.opposite())
     step = pl.program_id(0)
     far_sems = (far_send, far_recv)
 
@@ -723,8 +756,13 @@
 
     @pl.when(step == 0)
     def _():
-        greet(here.partners())
+        greet(here.partners() + [here.opposite()])
         out.start(0)
+
+        @pl.when(here.core != here.y)
+        def _():
+            swap.start()
+
         for load in loads:
             load.start()
 
@@ -797,12 +835,12 @@
         for total in (downs[0], ups[2], out):
             total.start(1)
 
-    @pl.when(step == 4)
+    @pl.when(step == 5)
     def _():
         downs[1].go(1)
         ups[3].go(1)
 
-    @pl.when(step == 5)
+    @pl.when(step == 6)
     def _():
         ups[0].go(1)
         ups[1].go(1)
@@ -835,12 +873,18 @@
         unfold(qkv_a, a.add(2))
         some_b[...] = b.add(1).astype(BF16)
 
+        @pl.when(here.core != here.y)
+        def _():
+            swap.wait()
+
 
 def once(shape):
     return pl.BlockSpec(shape, lambda *_: (0,) * len(shape), pipeline_mode=pl.Buffered(1))
 
 
-def backward_all(e_far, e_near, d_o, o, linv, q, k, k_far, v_far, v, gains, scales, h_t, grads):
+def backward_all(
+    e_far, e_near, d_o, o, linv, q, k, k_far, v_far, v, gains, scales, h_t, grads, output
+):
     _, keys, rows = e_far.shape
     width = h_t.shape[0]
 
@@ -856,7 +900,7 @@
     specs.append(pl.BlockSpec((BATCH, HD, 8), lambda s: (batch(s), 0, 0)))
     specs.append(pl.BlockSpec((2, BATCH, 1, rows), lambda s: (0, batch(s), 0, 0)))
     specs.append(once(h_t.shape))
-    specs += [ANYWHERE] * 6
+    specs += [ANYWHERE] * 7
     shard, chunk = width // 32, grads[0].shape[-1]
     down_rows, half = grads[1].shape[-2], width // 2
     part = (16, 3 * BATCH * HD * 3 // 2)
@@ -874,7 +918,8 @@
         jax.ShapeDtypeStruct((4, 2) + part, BF16),
     ]
     out_specs = [pl.BlockSpec((3, BATCH, HD, rows), lambda s: (0, batch(s), 0, 0)), gain, gain]
-    out_specs += [once(a.shape) for a in outs[3:]]
+    out_specs += [once(a.shape) for a in outs[3:]] + [ANYWHERE]
+    outs.append(jax.ShapeDtypeStruct(output.shape, BF16))
     scratch = [
         pltpu.VMEM((BATCH, 2, HD, keys), BF16),
         pltpu.VMEM((H, 2, HD, keys), BF16),
@@ -882,6 +927,8 @@
         pltpu.SemaphoreType.DMA((H,)),
         pltpu.VMEM((BATCH, 3, HD, rows), F32),
         pltpu.SemaphoreType.DMA((13,)),
+        pltpu.SemaphoreType.DMA((1,)),
+        pltpu.SemaphoreType.DMA((1,)),
     ]
     for stages in DOWN_STAGES:
         scratch += sum_scratch(stages, (down_rows, half))
@@ -901,7 +948,7 @@
             vmem_limit_bytes=61 * 2**20, collective_id=0, has_side_effects=True
         ),
         name="backward_all",
-    )(e_far, e_near, d_o, o, linv, q, k, k_far, v_far, v, gains, scales, h_t, *grads)
+    )(e_far, e_near, d_o, o, linv, q, k, k_far, v_far, v, gains, scales, h_t, *grads, output)
 
 
 def front_kernel(*refs):
@@ -1016,7 +1063,7 @@
 
 def front(tokens, vectors, w):
     rows, width = tokens.shape
-    block = math.gcd(rows, 256)
+    block = math.gcd(rows, 128)
     steps = rows // block
     row = pl.BlockSpec((block, width), lambda i: (i, 0))
     head = pl.BlockSpec((H, HD, block), lambda i: (0, 0, i))
@@ -1265,30 +1312,6 @@
     )(output, came, grad_tokens, *qkvs, out, up, down)
 
 
-def place(index):
-    return index // 8, index // 4 % 2, index // 2 % 2, index % 2
-
-
-def device(z, x, core, y):
-    return ((z * 2 + x) * 2 + core) * 2 + y
-
-
-def pairs(other):
-    every = [(i, device(*other(*place(i)))) for i in range(32)]
-    return [(i, j) for i, j in every if i != j]
-
-
-SWAP = pairs(lambda z, x, c, y: (z, x, y, c))
-
-
-def send(value, where):
-    return lax.ppermute(value, AXES, where)
-
-
-def after(values, *done):
-    return lax.optimization_barrier((values, done))[0]
-
-
 def segments(lengths, group, mine, rows):
     count = lengths.shape[1]
     at = jnp.arange(count)
@@ -1312,15 +1335,14 @@
     h_t, q, k, v, scales, tokens, mask_q, mask_near, mask_far, gains, k_far, v_far = front(
         tokens, vectors, w_qkv
     )
-    came = send(after(cotangent, tokens), SWAP)
-    o, linv, e_near, e_far = attend(q, mask_q, [(k, v, mask_near), (k_far, v_far, mask_far)])
+    parts = [(k, v, mask_near), (k_far, v_far, mask_far)]
+    o, linv, e_near, e_far, came = attend(q, mask_q, parts, cotangent)
     output, dx1, d_o, dgain2, dbias2, *grads = middle(
         tokens, o.reshape(width, rows), cotangent, w_out, vectors, w_up, w_down, came
     )
     d_o = d_o.reshape(H, HD, rows)
-    output_came = send(output, SWAP)
-    d, sum_q, sum_k, keep, give, up, down, out, qkv_a, some = backward_all(
-        e_far, e_near, d_o, o, linv, q, k, k_far, v_far, v, gains, scales, h_t, grads
+    d, sum_q, sum_k, keep, give, up, down, out, qkv_a, some, output_came = backward_all(
+        e_far, e_near, d_o, o, linv, q, k, k_far, v_far, v, gains, scales, h_t, grads, output
     )
     grad_tokens, qkv_b, qkv_c, table = tail(
         d, w_qkv, tokens, dx1, vectors, sum_q, sum_k, dgain2, dbias2, keep, some, give
@@ -1377,8 +1399,11 @@
 ):
     width = tokens.shape[1]
     lengths_row = jnp.pad(lengths[0].astype(F32), (0, width - lengths.shape[1]))
-    rows = [ln1_gain, ln1_bias, ln2_gain, ln2_bias, q_gain, k_gain, lengths_row, lengths_row]
-    vectors = jnp.stack(rows)
+    rows = [ln1_gain, ln1_bias, ln2_gain, ln2_bias, q_gain, k_gain, lengths_row]
+    at = lax.broadcasted_iota(jnp.int32, (8, width), 0)
+    vectors = jnp.zeros((8, width), F32)
+    for i, row in enumerate(rows):
+        vectors = jnp.where(at == i, row[None, :], vectors)
     known = lax.axis_size("blk") == 2 and lax.axis_size("wide") == 16
     run = on_chips if known else anywhere
     output, grad_tokens, sums, s_qkv, s_out, s_up, s_down = run(

time: 242 us -> 226 us (0.934)
  local copies, waits for them, and re-layouts: 8.85 us -> 0.79 us
  Pallas kernels: 229 us -> 222 us
    another operation x8 -> x0, local copies, waits for them, and re-layouts: 4.79 us -> none  [shards(): vectors = jnp.stack(rows)]
    pallas_call x1, Pallas kernels: 34.6 us -> 29.9 us  [tail(): pl.pallas_call(tail_kernel, grid=(steps,), in_specs=[pl.BlockSpec(d.shape...]
    pallas_call x1, Pallas kernels: 50.3 us -> 47.5 us  [middle(): pl.pallas_call(functools.partial(middle_kernel, split), grid=(FF_STEPS,),...]
  transfers between devices with their start and end apart: 2 -> 0, of which waited for: 0 -> 0; matrix products, arithmetic and copies ran while one was open for 1% -> 0% of each run, Pallas kernels for 60% -> 0%
where the time goes in v4:
time: 226 us
  Pallas kernels  222 us (98%)
    pallas_call x1, Pallas kernels, backward_all(): pl.pallas_call(backward_all_kernel, grid=(H + 1,), in_specs=specs, out_sp...  80.6 us
    pallas_call x1, Pallas kernels, middle(): pl.pallas_call(functools.partial(middle_kernel, split), grid=(FF_STEPS,),...  47.5 us
    pallas_call x1, Pallas kernels, attend(): pl.pallas_call(functools.partial(forward_kernel, len(parts)), grid=(heads...  30.1 us
    pallas_call x1, Pallas kernels, tail(): pl.pallas_call(tail_kernel, grid=(steps,), in_specs=[pl.BlockSpec(d.shape...  29.9 us
    pallas_call x1, Pallas kernels, front(): pl.pallas_call(front_kernel, grid=(steps,), in_specs=[ANYWHERE, once(vect...  28.7 us
    pallas_call x1, Pallas kernels, finish(): pl.pallas_call(finish_kernel, grid=(steps,), in_specs=[row] * 3 + [once(a...  5.23 us

profile of v4, /device:TPU:0, one launch (start us, length us, event | category | flops | bytes accessed | tf_op | source)
XLA Modules:
  0.0 225.6 jit_solution(1569180839192316291)
XLA Ops:
  0.6 0.7 convert_bitcast_fusion
  1.3 1.5 select_select_fusion.refs_1_.refs_4_
  2.8 28.7 %front.1 = (bf16[768,1024]{1,0:T(8,128)(2,1)}, bf16[12,64,1024]{2,1,0:T(8,128)(2,1)}, bf16[12,64,1024]{2,1,0:T(8,128)(2,1)}, bf16[12,64,1024]{2,1,0:T(8,128)(2,1...) custom-call(bf16[1024,768]{1,0:T(8,128)(2,1)} %refs_2_.2, ...), custom_call_target="tpu_custom_call" | custom-call | flops 3623878656 | bytes 9437184 | tf_op jit(solution)/shard_map/front/pallas_call | solution.py:1072
  31.5 30.1 %attend.1 = (bf16[12,64,1024]{2,1,0:T(8,128)(2,1)}, f32[12,8,1024]{2,1,0:T(8,128)}, bf16[12,1024,1024]{2,1,0:T(8,128)(2,1)}, bf16[12,1024,1024]{2,1,0:T(8,128)(2,1)}, bf16[1024,768]{1,0:T(8,128)(2,1)}) custom-call(bf16[12,64,1024]{2,1,0:T(8,128)(2,1)} %get-tuple-element.62.refs_0_.refs_5_, bf16[16,1024]{1,0:T(8,128)(2,1)} %get-tuple-element.63.refs_1_, ...), custom_call_target="tpu_custom_call" | custom-call | flops 25769803776 | bytes 50331648 | tf_op jit(solution)/shard_map/attend/pallas_call | solution.py:102
  61.7 47.5 %middle.1 = (bf16[1024,768]{1,0:T(8,128)(2,1)}, f32[1024,768]{1,0:T(8,128)}, f32[768,1024]{1,0:T(8,128)}, f32[1,768]{1,0:T(1,128)}, f32[1,768]{1,0:T(1,128)}, /*...) custom-call(bf16[1024,768]{1,0:T(8,128)(2,1)} %get-tuple-element.61., ...), custom_call_target="tpu_custom_call" | custom-call | flops 32614907904 | bytes 31457280 | tf_op jit(solution)/shard_map/middle/pallas_call | solution.py:444
  109.1 80.6 %backward_all.1 = (bf16[3,12,64,1024]{3,2,1,0:T(8,128)(2,1)}, f32[12,64,1]{2,1,0:T(8,128)}, f32[12,64,1]{2,1,0:T(8,128)}, bf16[4,2,2,16,1152]{4,3,2,1,0:T(8,128)...) custom-call(bf16[12,1024,1024]{2,1,0:T(8,128)(2,1)} %get-tuple-eleme, ...), custom_call_target="tpu_custom_call" | custom-call | tf_op jit(solution)/shard_map/backward_all/pallas_call | solution.py:940
  189.8 29.9 %tail.1 = (bf16[1024,768]{1,0:T(8,128)(2,1)}, f32[24,768]{1,0:T(8,128)}, f32[24,768]{1,0:T(8,128)}, f32[24,128]{1,0:T(8,128)}) custom-call(bf16[3,12,64,1024]{3,2,1,0:T(8,128)(2,1)} %get-tuple-element.87.refs_0_, bf16[768,2304]{1,0:T(8,128)(2,1)} %refs_1_.1, bf16[1024,768]{1,0:T(8,128)(2,1)} %get-tuple-element.61.refs_0_.refs_2_, ...), custom_call_target="tpu_custom_call" | custom-call | tf_op jit(solution)/shard_map/tail/pallas_call | solution.py:1227
  219.6 0.0 copy-start
  219.6 5.2 %finish.1 = (bf16[1024,768]{1,0:T(8,128)(2,1)}, bf16[1024,768]{1,0:T(8,128)(2,1)}, f32[24,2304]{1,0:T(8,128)}, f32[24,768]{1,0:T(8,128)}, f32[24,3072]{1,0:T(8,128)}, /*index=5*/f32[96,768]{1,0:T(8,128)}) custom-call(bf16[1024,768]{1,0:T(8,128)(2,1)} %get-tuple-element.72.refs_19_.here_ref, bf16[1024,768]{1,0:T(8,128)(2,1)} %get-tuple-element.86.came_ref, ...), custom_call_target="tpu_custom_call" | custom-call | tf_op jit(solution)/shard_map/finish/pallas_call | solution.py:1302
  224.9 0.0 copy-done
  224.9 0.8 slice_reduce_fusion
  (5 shorter events, 0.0 us)
Async XLA Ops:
  219.6 5.2 %copy-start = (f32[24,128]{1,0:T(8,128)S(1)}, f32[24,128]{1,0:T(8,128)}, u32[]{:S(2)}) copy-start(f32[24,128]{1,0:T(8,128)} %get-tuple-element.105) | copy-start | bytes 36868

commit v5 on v4

--- a/solution.py
+++ b/solution.py
@@ -1296,7 +1296,7 @@
 
 def finish(output, came, grad_tokens, qkvs, out, up, down):
     rows, width = output.shape
-    steps = 4
+    steps = 2
     small = [jax.ShapeDtypeStruct((out.shape[0], 9 * BATCH * HD), F32), out, up, down]
     row = pl.BlockSpec((rows // steps, width), lambda i: (i, 0))
     return pl.pallas_call(

time: 226 us -> 225 us (level)
  no operation moved by 1% of the time
where the time goes in v5:
time: 225 us
  Pallas kernels  221 us (98%)
    pallas_call x1, Pallas kernels, backward_all(): pl.pallas_call(backward_all_kernel, grid=(H + 1,), in_specs=specs, out_sp...  80.6 us
    pallas_call x1, Pallas kernels, middle(): pl.pallas_call(functools.partial(middle_kernel, split), grid=(FF_STEPS,),...  47.5 us
    pallas_call x1, Pallas kernels, attend(): pl.pallas_call(functools.partial(forward_kernel, len(parts)), grid=(heads...  30.1 us
    pallas_call x1, Pallas kernels, tail(): pl.pallas_call(tail_kernel, grid=(steps,), in_specs=[pl.BlockSpec(d.shape...  29.9 us
    pallas_call x1, Pallas kernels, front(): pl.pallas_call(front_kernel, grid=(steps,), in_specs=[ANYWHERE, once(vect...  28.7 us

profile of v5, /device:TPU:0, one launch (start us, length us, event | category | flops | bytes accessed | tf_op | source)
XLA Modules:
  0.0 224.7 jit_solution(3054068815301135279)
XLA Ops:
  0.6 0.7 convert_bitcast_fusion
  1.3 1.5 select_select_fusion.refs_1_.refs_4_
  2.8 28.7 %front.1 = (bf16[768,1024]{1,0:T(8,128)(2,1)}, bf16[12,64,1024]{2,1,0:T(8,128)(2,1)}, bf16[12,64,1024]{2,1,0:T(8,128)(2,1)}, bf16[12,64,1024]{2,1,0:T(8,128)(2,1...) custom-call(bf16[1024,768]{1,0:T(8,128)(2,1)} %refs_2_.2, ...), custom_call_target="tpu_custom_call" | custom-call | flops 3623878656 | bytes 9437184 | tf_op jit(solution)/shard_map/front/pallas_call | solution.py:1072
  31.5 30.1 %attend.1 = (bf16[12,64,1024]{2,1,0:T(8,128)(2,1)}, f32[12,8,1024]{2,1,0:T(8,128)}, bf16[12,1024,1024]{2,1,0:T(8,128)(2,1)}, bf16[12,1024,1024]{2,1,0:T(8,128)(2,1)}, bf16[1024,768]{1,0:T(8,128)(2,1)}) custom-call(bf16[12,64,1024]{2,1,0:T(8,128)(2,1)} %get-tuple-element.62.refs_0_.refs_5_, bf16[16,1024]{1,0:T(8,128)(2,1)} %get-tuple-element.63.refs_1_, ...), custom_call_target="tpu_custom_call" | custom-call | flops 25769803776 | bytes 50331648 | tf_op jit(solution)/shard_map/attend/pallas_call | solution.py:102
  61.7 47.5 %middle.1 = (bf16[1024,768]{1,0:T(8,128)(2,1)}, f32[1024,768]{1,0:T(8,128)}, f32[768,1024]{1,0:T(8,128)}, f32[1,768]{1,0:T(1,128)}, f32[1,768]{1,0:T(1,128)}, /*...) custom-call(bf16[1024,768]{1,0:T(8,128)(2,1)} %get-tuple-element.61., ...), custom_call_target="tpu_custom_call" | custom-call | flops 32614907904 | bytes 31457280 | tf_op jit(solution)/shard_map/middle/pallas_call | solution.py:444
  109.1 80.6 %backward_all.1 = (bf16[3,12,64,1024]{3,2,1,0:T(8,128)(2,1)}, f32[12,64,1]{2,1,0:T(8,128)}, f32[12,64,1]{2,1,0:T(8,128)}, bf16[4,2,2,16,1152]{4,3,2,1,0:T(8,128)...) custom-call(bf16[12,1024,1024]{2,1,0:T(8,128)(2,1)} %get-tuple-eleme, ...), custom_call_target="tpu_custom_call" | custom-call | tf_op jit(solution)/shard_map/backward_all/pallas_call | solution.py:940
  189.8 29.9 %tail.1 = (bf16[1024,768]{1,0:T(8,128)(2,1)}, f32[24,768]{1,0:T(8,128)}, f32[24,768]{1,0:T(8,128)}, f32[24,128]{1,0:T(8,128)}) custom-call(bf16[3,12,64,1024]{3,2,1,0:T(8,128)(2,1)} %get-tuple-element.87.refs_0_, bf16[768,2304]{1,0:T(8,128)(2,1)} %refs_1_.1, bf16[1024,768]{1,0:T(8,128)(2,1)} %get-tuple-element.61.refs_0_.refs_2_, ...), custom_call_target="tpu_custom_call" | custom-call | tf_op jit(solution)/shard_map/tail/pallas_call | solution.py:1227
  219.6 0.0 copy-start
  219.6 4.2 %finish.1 = (bf16[1024,768]{1,0:T(8,128)(2,1)}, bf16[1024,768]{1,0:T(8,128)(2,1)}, f32[24,2304]{1,0:T(8,128)}, f32[24,768]{1,0:T(8,128)}, f32[24,3072]{1,0:T(8,128)}, /*index=5*/f32[96,768]{1,0:T(8,128)}) custom-call(bf16[1024,768]{1,0:T(8,128)(2,1)} %get-tuple-element.72.refs_19_.here_ref, bf16[1024,768]{1,0:T(8,128)(2,1)} %get-tuple-element.86.came_ref, ...), custom_call_target="tpu_custom_call" | custom-call | tf_op jit(solution)/shard_map/finish/pallas_call | solution.py:1302
  223.9 0.0 copy-done
  223.9 0.8 slice_reduce_fusion
  (5 shorter events, 0.0 us)
Async XLA Ops:
  219.6 4.3 %copy-start = (f32[24,128]{1,0:T(8,128)S(1)}, f32[24,128]{1,0:T(8,128)}, u32[]{:S(2)}) copy-start(f32[24,128]{1,0:T(8,128)} %get-tuple-element.105) | copy-start | bytes 36868
